TPU v7x, 32 devices: a whole 2x2x4 slice. The times are simulated.
32 devices in a mesh: groups: 2 (over x), dict: 16 (over z, y, core).
Axes of the slice: x: 2, y: 2, z: 4, core: 2. Of those that a mesh axis runs over, the one named last changes fastest.
Arguments:
- tokens: bfloat16 [128, 4096], P(('groups', 'dict')), parts along dimension 0, may hold values from -25 to 25
- encoder_weight: bfloat16 [2624, 4096], P(('groups', 'dict')), parts along dimension 0, may hold values from -0.09375 to 0.09375
- encoder_bias: float32 [2624], P(('groups', 'dict')), parts along dimension 0, may hold values from -1 to 0.5
- decoder_weight: bfloat16 [2624, 4096], P(('groups', 'dict')), parts along dimension 0, may hold values from -0.15625 to 0.15625
- decoder_bias: float32 [8192], P('groups'), parts along dimension 0, may hold values from -3 to 3
- encoder_first: float32 [2624, 4096], P(('groups', 'dict')), parts along dimension 0, may hold values from -6 to 6
- encoder_second: float32 [2624, 4096], P(('groups', 'dict')), parts along dimension 0, may hold values from 1 to 100
- decoder_first: float32 [2624, 4096], P(('groups', 'dict')), parts along dimension 0, may hold values from -6 to 6
- decoder_second: float32 [2624, 4096], P(('groups', 'dict')), parts along dimension 0, may hold values from 1 to 100
- latent_first: float32 [2624], P(('groups', 'dict')), parts along dimension 0, may hold values from -6 to 6
- latent_second: float32 [2624], P(('groups', 'dict')), parts along dimension 0, may hold values from 1 to 100
- feature_first: float32 [8192], P('groups'), parts along dimension 0, may hold values from -6 to 6
- feature_second: float32 [8192], P('groups'), parts along dimension 0, may hold values from 10 to 1000
Outputs:
- new_encoder_weight: bfloat16 [2624, 4096], P(('groups', 'dict')), parts along dimension 0
- new_encoder_bias: float32 [2624], P(('groups', 'dict')), parts along dimension 0
- new_decoder_weight: bfloat16 [2624, 4096], P(('groups', 'dict')), parts along dimension 0
- new_decoder_bias: float32 [8192], P('groups'), parts along dimension 0
- new_encoder_first: float32 [2624, 4096], P(('groups', 'dict')), parts along dimension 0
- new_encoder_second: float32 [2624, 4096], P(('groups', 'dict')), parts along dimension 0
- new_decoder_first: float32 [2624, 4096], P(('groups', 'dict')), parts along dimension 0
- new_decoder_second: float32 [2624, 4096], P(('groups', 'dict')), parts along dimension 0
- new_latent_first: float32 [2624], P(('groups', 'dict')), parts along dimension 0
- new_latent_second: float32 [2624], P(('groups', 'dict')), parts along dimension 0
- new_feature_first: float32 [8192], P('groups'), parts along dimension 0
- new_feature_second: float32 [8192], P('groups'), parts along dimension 0
There are 2 independent parts, one for each index of `groups`. A program takes and returns all parts, laid end to end along the dimension named above; each array names one. Nothing has to cross between parts.
All inputs are finite; a program needn't handle non-finite values.
Results may differ from a plain program's by a relative error of at most 0.0048.
Values may be sent and summed in bfloat16 or wider, within the bound.
No kernel may reach another device: no remote copies, remote signals or barrier semaphores. Data moves between devices by JAX's collectives and lax.ppermute only.
A program may use at most 128 MiB of HBM per device.

v0:
```python
import jax
import jax.numpy as jnp
from jax import lax
from jax.sharding import PartitionSpec as P

STEP = 100


sharpness = 4.0
sparsity_coef = 0.3
first_decay = 0.9
second_decay = 0.999
learn_rate = 0.001
epsilon = 1e-08


def adam_update(param, grad, first, second):
    first_new = first_decay * first + (1.0 - first_decay) * grad
    second_new = second_decay * second + (1.0 - second_decay) * grad * grad
    first_corr = 1.0 - first_decay**STEP
    second_corr = 1.0 - second_decay**STEP
    change = learn_rate * (first_new / first_corr) / (jnp.sqrt(second_new / second_corr) + epsilon)
    return (param.astype(jnp.float32) - change, first_new, second_new)


def local(
    tokens,
    encoder_weight,
    encoder_bias,
    decoder_weight,
    decoder_bias,
    encoder_first,
    encoder_second,
    decoder_first,
    decoder_second,
    latent_first,
    latent_second,
    feature_first,
    feature_second,
):
    gathered = lax.all_gather(tokens, "dict", axis=0, tiled=True)
    pre = (
        jnp.einsum("td,ld->tl", gathered, encoder_weight, preferred_element_type=jnp.float32)
        + encoder_bias
    )
    act = jax.nn.softplus(sharpness * pre) / sharpness
    act_low = act.astype(jnp.bfloat16)
    recon = lax.psum_scatter(
        jnp.dot(act_low, decoder_weight, preferred_element_type=jnp.float32),
        "dict",
        scatter_dimension=0,
        tiled=True,
    )
    own_errors = (recon + decoder_bias - tokens.astype(jnp.float32)).astype(jnp.bfloat16)
    errors = lax.all_gather(own_errors, "dict", axis=0, tiled=True)
    feature_grad = lax.psum(jnp.sum(own_errors, axis=0, dtype=jnp.float32), "dict")
    decoder_full = decoder_weight.astype(jnp.float32)
    norms = jnp.sqrt(jnp.sum(decoder_full * decoder_full, axis=1) + 1e-06)
    act_total = jnp.sum(act, axis=0)
    decoder_grad = jnp.einsum("tl,td->ld", act_low, errors, preferred_element_type=jnp.float32)
    decoder_grad = decoder_grad + sparsity_coef * act_total[:, None] * decoder_full / norms[:, None]
    act_grad = (
        jnp.einsum("td,ld->tl", errors, decoder_weight, preferred_element_type=jnp.float32)
        + sparsity_coef * norms
    )
    pre_grad = act_grad * jax.nn.sigmoid(sharpness * pre)
    latent_grad = jnp.sum(pre_grad, axis=0)
    pre_low = pre_grad.astype(jnp.bfloat16)
    encoder_grad = jnp.einsum("tl,td->ld", pre_low, gathered, preferred_element_type=jnp.float32)
    enc_new, enc_first, enc_second = adam_update(
        encoder_weight, encoder_grad, encoder_first, encoder_second
    )
    lat_new, lat_first, lat_second = adam_update(
        encoder_bias, latent_grad, latent_first, latent_second
    )
    dec_new, dec_first, dec_second = adam_update(
        decoder_weight, decoder_grad, decoder_first, decoder_second
    )
    feat_new, feat_first, feat_second = adam_update(
        decoder_bias, feature_grad, feature_first, feature_second
    )
    return (
        enc_new.astype(jnp.bfloat16),
        lat_new,
        dec_new.astype(jnp.bfloat16),
        feat_new,
        enc_first,
        enc_second,
        dec_first,
        dec_second,
        lat_first,
        lat_second,
        feat_first,
        feat_second,
    )


def solution(mesh):
    in_specs = (
        P(("groups", "dict"), None),
        P(("groups", "dict"), None),
        P(("groups", "dict")),
        P(("groups", "dict"), None),
        P("groups"),
        P(("groups", "dict"), None),
        P(("groups", "dict"), None),
        P(("groups", "dict"), None),
        P(("groups", "dict"), None),
        P(("groups", "dict")),
        P(("groups", "dict")),
        P("groups"),
        P("groups"),
    )
    out_specs = (
        P(("groups", "dict"), None),
        P(("groups", "dict")),
        P(("groups", "dict"), None),
        P("groups"),
        P(("groups", "dict"), None),
        P(("groups", "dict"), None),
        P(("groups", "dict"), None),
        P(("groups", "dict"), None),
        P(("groups", "dict")),
        P(("groups", "dict")),
        P("groups"),
        P("groups"),
    )
    return jax.shard_map(local, mesh=mesh, in_specs=in_specs, out_specs=out_specs, check_vma=False)
```

profile of v0, /device:TPU:0, one launch (start us, length us, event | category | flops | bytes accessed | tf_op | source)
XLA Modules:
  0.0 221.8 jit_solution(4490684599826476923)
XLA Ops:
  7.2 0.0 copy-start.1
  7.2 0.0 all-reduce.3.cloned.1.call-start
  7.2 0.0 copy-start
  7.3 24.9 %all-gather = bf16[16,4,4096]{2,1,0:T(4,128)(2,1)S(1)} all-gather(bf16[1,4,4096]{2,1,0:T(4,128)(2,1)} %bitcast.11), channel_id=1, replica_groups=mesh['groups'=2,'dict'=16] {'dict'}, dimensions={0}, use_global_device_ids=true | all-gather | bytes 557056 | tf_op jit(solution)/shard_map/all_gather | solution.py:41
  32.2 0.1 reshape.40
  32.3 0.4 fusion.13
  32.7 0.0 copy-start.11
  32.8 0.0 copy-start.2
  32.8 0.0 copy-start.3
  32.8 1.3 fusion.17
  34.1 0.0 all-reduce.3.cloned.1.call-update
  34.1 0.2 fusion
  34.4 0.0 copy-done.11
  34.4 0.6 dynamic-slice
  35.7 89.2 %all-reduce.3.cloned.1.call-done = f32[64,4096]{1,0:T(8,128)} async-done(((f32[64,4096]{1,0:T(8,128)}), f32[64,4096]{1,0:T(8,128)}) %all-reduce.3.cloned.1.call-update) | async-done | bytes 1048592
  124.9 1.0 convert_reduce_fusion
  125.9 21.1 %all-gather.1 = bf16[16,4,4096]{2,1,0:T(4,128)(2,1)S(1)} all-gather(bf16[1,4,4096]{2,1,0:T(4,128)(2,1)S(1)} %bitcast.12), channel_id=1, replica_groups=mesh['groups'=2,'dict'=16] {'dict'}, dimensions={0}, use_global_device_ids=true | all-gather | bytes 557056 | tf_op jit(solution)/shard_map/all_gather | solution.py:55
  147.0 0.1 reshape.42
  147.1 57.8 %psum.7 = f32[4096]{0:T(1024)S(1)} all-reduce(f32[4096]{0:T(1024)S(1)} %get-tuple-element.15), channel_id=1, replica_groups=mesh['groups'=2,'dict'=16] {'dict'}, use_global_device_ids=true, to_apply=%region_5.6 | all-reduce | flops 4096 | bytes 32768 | tf_op jit(solution)/shard_map/psum | solution.py:56
  204.9 0.4 fusion.24
  205.3 0.0 copy-start.7
  205.4 0.0 copy-start.8
  205.4 0.0 copy-start.4
  205.4 0.0 copy-start.5
  205.4 0.0 copy-start.9
  205.4 0.0 copy-start.10
  205.4 5.0 %subtract_convert_fusion = (bf16[82,4096]{1,0:T(8,128)(2,1)}, f32[82,4096]{1,0:T(8,128)}, f32[82,4096]{1,0:T(8,128)}) fusion(bf16[82,4096]{1,0:T(8,128)(2,1)S(1)} %copy-done.1, f32[82,4096]{1,0:T(8,128)} %param.18, f32[82,4096]{1,0:T(8,128)} %param.19, bf16[64,4096]{1,0:T(8,128)(2,1)S(1)} %reshape.40, bf16[64,82]{1,0:T(8,128)(2,1)S(1)} %get-tuple-element.29), kind=kOutput, calls=%fused_computation.12 | convolution fusion | flops 47693824 | bytes 7252224 | tf_op jit(solution)/shard_map/tl,td->ld/dot_general | solution.py:69
  210.4 0.5 divide_subtract_fusion.1
  211.0 0.0 copy-done.5
  211.0 0.6 divide_subtract_fusion
  211.6 0.0 copy-done.9
  211.6 3.3 %fusion.2 = (bf16[82,4096]{1,0:T(8,128)(2,1)}, f32[82,4096]{1,0:T(8,128)}, f32[82,4096]{1,0:T(8,128)}) fusion(bf16[82,4096]{1,0:T(8,128)(2,1)S(1)} %copy-done, f32[82,4096]{1,0:T(8,128)S(1)} %copy-done.9, f32[82,4096]{1,0:T(8,128)S(1)} %copy-done.10, f32[82]{0:T(128)S(1)} %get-tuple-element.26, f32[82]{0:T(128)S(1)} %broadcast_multiply_fusion, ...), kind=kOutput, calls=%fused_computation.8 | convolution fusion | flops 48743424 | bytes 7263376 | tf_op jit(solution)/shard_map/tl,td->ld/dot_general | solution.py:60
  (12 shorter events, 0.0 us)
Async XLA Ops:
  7.2 25.1 %copy-start.1 = (bf16[82,4096]{1,0:T(8,128)(2,1)S(1)}, bf16[82,4096]{1,0:T(8,128)(2,1)}, u32[]{:S(2)}) copy-start(bf16[82,4096]{1,0:T(8,128)(2,1)} %param.14) | copy-start | bytes 2015236
  7.2 25.1 %copy-start.6 = (f32[82]{0:T(128)S(1)}, f32[82]{0:T(128)}, u32[]{:S(2)}) copy-start(f32[82]{0:T(128)} %param.15) | copy-start | bytes 988
  7.2 117.7 %all-reduce.3.cloned.1.call-start = ((), (), s32[]{:S(2)}) async-start(), calls=%async_computation | async-start | bytes 2097152
  7.2 25.5 %copy-start = (bf16[82,4096]{1,0:T(8,128)(2,1)S(1)}, bf16[82,4096]{1,0:T(8,128)(2,1)}, u32[]{:S(2)}) copy-start(bf16[82,4096]{1,0:T(8,128)(2,1)} %param.16) | copy-start | bytes 2015236
  32.7 1.7 copy-start.11
  32.8 92.1 %copy-start.2 = (bf16[4,4096]{1,0:T(4,128)(2,1)S(1)}, bf16[4,4096]{1,0:T(4,128)(2,1)}, u32[]{:S(2)}) copy-start(bf16[4,4096]{1,0:T(4,128)(2,1)} %param.13) | copy-start | bytes 98308
  32.8 92.1 %copy-start.3 = (f32[4096]{0:T(1024)S(1)}, f32[4096]{0:T(1024)}, u32[]{:S(2)}) copy-start(f32[4096]{0:T(1024)} %param.17) | copy-start | bytes 49156
  205.3 5.1 %copy-start.7 = (f32[82]{0:T(128)S(1)}, f32[82]{0:T(128)}, u32[]{:S(2)}) copy-start(f32[82]{0:T(128)} %param.22) | copy-start | bytes 988
  205.4 5.1 %copy-start.8 = (f32[82]{0:T(128)S(1)}, f32[82]{0:T(128)}, u32[]{:S(2)}) copy-start(f32[82]{0:T(128)} %param.23) | copy-start | bytes 988
  205.4 5.6 %copy-start.4 = (f32[4096]{0:T(1024)S(1)}, f32[4096]{0:T(1024)}, u32[]{:S(2)}) copy-start(f32[4096]{0:T(1024)} %param.24) | copy-start | bytes 49156
  205.4 5.6 %copy-start.5 = (f32[4096]{0:T(1024)S(1)}, f32[4096]{0:T(1024)}, u32[]{:S(2)}) copy-start(f32[4096]{0:T(1024)} %param.25) | copy-start | bytes 49156
  205.4 6.2 %copy-start.9 = (f32[82,4096]{1,0:T(8,128)S(1)}, f32[82,4096]{1,0:T(8,128)}, u32[]{:S(2)}) copy-start(f32[82,4096]{1,0:T(8,128)} %param.20) | copy-start | bytes 4030468
  205.4 6.2 %copy-start.10 = (f32[82,4096]{1,0:T(8,128)S(1)}, f32[82,4096]{1,0:T(8,128)}, u32[]{:S(2)}) copy-start(f32[82,4096]{1,0:T(8,128)} %param.21) | copy-start | bytes 4030468
Sparse Core Ops, SparseCore 0:
  34.3 90.5 all-reduce.2
where the time goes:
time: 222 us
  blocking collectives  104 us (47%)
  waiting for transfers between devices  89.2 us (40%)
  between operations  14.9 us (7%)
  matrix products  10.5 us (5%)
  other arithmetic  2.4 us (1%)
    unnamed x2, waiting for transfers between devices  89.2 us
    psum x1, blocking collectives, local(): lax.psum(jnp.sum(own_errors, axis=0, dtype=jnp.float32), 'dict')  57.8 us
    all_gather x1, blocking collectives, local(): gathered = lax.all_gather(tokens, 'dict', axis=0, tiled=True)  24.9 us
    all_gather x1, blocking collectives, local(): errors = lax.all_gather(own_errors, 'dict', axis=0, tiled=True)  21.1 us
    dot_general x1, matrix products, local(): jnp.einsum('tl,td->ld', pre_low, gathered, preferred_element_type=jnp.flo...  5.03 us
  transfers between devices with their start and end apart: 1, of which 1 were waited for; matrix products, arithmetic and copies ran while one was open for 0% of the time, Pallas kernels for 0%

commit v1 on v0

--- a/solution.py
+++ b/solution.py
@@ -23,7 +23,12 @@
     return (param.astype(jnp.float32) - change, first_new, second_new)
 
 
+def swap(x, bit, devices):
+    return lax.ppermute(x, "dict", [(i, i ^ bit) for i in range(devices)])
+
+
 def local(
+    devices,
     tokens,
     encoder_weight,
     encoder_bias,
@@ -38,22 +43,35 @@
     feature_first,
     feature_second,
 ):
-    gathered = lax.all_gather(tokens, "dict", axis=0, tiled=True)
+    bits = [1 << b for b in reversed(range(devices.bit_length() - 1))]
+    own = tokens.shape[0]
+    gathered = tokens
+    for bit in bits:
+        gathered = jnp.concatenate([gathered, swap(gathered, bit, devices)], axis=0)
     pre = (
         jnp.einsum("td,ld->tl", gathered, encoder_weight, preferred_element_type=jnp.float32)
         + encoder_bias
     )
     act = jax.nn.softplus(sharpness * pre) / sharpness
     act_low = act.astype(jnp.bfloat16)
-    recon = lax.psum_scatter(
-        jnp.dot(act_low, decoder_weight, preferred_element_type=jnp.float32),
-        "dict",
-        scatter_dimension=0,
-        tiled=True,
-    )
-    own_errors = (recon + decoder_bias - tokens.astype(jnp.float32)).astype(jnp.bfloat16)
-    errors = lax.all_gather(own_errors, "dict", axis=0, tiled=True)
-    feature_grad = lax.psum(jnp.sum(own_errors, axis=0, dtype=jnp.float32), "dict")
+    part = jnp.dot(act_low, decoder_weight, preferred_element_type=jnp.float32)
+    for bit in reversed(bits[1:]):
+        half = part.shape[0] // 2
+        part = part[:half] + swap(part[half:].astype(jnp.bfloat16), bit, devices).astype(jnp.float32)
+    part = lax.reduce_precision(part, 8, 7)
+    other = swap(part.astype(jnp.bfloat16), bits[0], devices).astype(jnp.float32)
+    recon = part + jnp.concatenate([other[own:], other[:own]], axis=0)
+    errors = (recon + decoder_bias - gathered[: 2 * own].astype(jnp.float32)).astype(jnp.bfloat16)
+    for bit in bits[1:]:
+        errors = jnp.concatenate([errors, swap(errors, bit, devices)], axis=0)
+    rows = errors.astype(jnp.float32).reshape(devices, own, -1)
+    feature_grad = rows[:, 0]
+    for row in range(1, own):
+        feature_grad = feature_grad + rows[:, row]
+    while feature_grad.shape[0] > 1:
+        half = feature_grad.shape[0] // 2
+        feature_grad = feature_grad[:half] + feature_grad[half:]
+    feature_grad = feature_grad[0]
     decoder_full = decoder_weight.astype(jnp.float32)
     norms = jnp.sqrt(jnp.sum(decoder_full * decoder_full, axis=1) + 1e-06)
     act_total = jnp.sum(act, axis=0)
@@ -96,6 +114,7 @@
 
 
 def solution(mesh):
+    devices = mesh.shape["dict"]
     in_specs = (
         P(("groups", "dict"), None),
         P(("groups", "dict"), None),
@@ -125,4 +144,8 @@
         P("groups"),
         P("groups"),
     )
-    return jax.shard_map(local, mesh=mesh, in_specs=in_specs, out_specs=out_specs, check_vma=False)
+
+    def step(*args):
+        return local(devices, *args)
+
+    return jax.shard_map(step, mesh=mesh, in_specs=in_specs, out_specs=out_specs, check_vma=False)

time: 222 us -> 61.6 us (0.28)
  blocking collectives: 104 us -> 0 us
  waiting for transfers between devices: 89.2 us -> 27.7 us
  starting transfers between devices: 0.04 us -> 17.3 us
  between operations: 14.9 us -> 0.96 us
  matrix products: 10.5 us -> 7.55 us
  other arithmetic: 2.4 us -> 5.02 us
    unnamed x2 -> x0, waiting for transfers between devices: 89.2 us -> none
    psum x1 -> x0, blocking collectives: 57.8 us -> none  [local(): lax.psum(jnp.sum(own_errors, axis=0, dtype=jnp.float32), 'dict')]
    all_gather x2 -> x0, blocking collectives: 46 us -> none  [the longest x1 24.9 us: local(): gathered = lax.all_gather(tokens, 'dict', axis=0, tiled=True)]
    ppermute x0 -> x11, waiting for transfers between devices: none -> 27.7 us  [swap(): return lax.ppermute(x, 'dict', [(i, i ^ bit) for i in range(devices)])]
    ppermute x0 -> x11, starting transfers between devices: none -> 17.3 us  [swap(): return lax.ppermute(x, 'dict', [(i, i ^ bit) for i in range(devices)])]
    concatenate x0 -> x5, other arithmetic: none -> 2.45 us  [the longest x3 2.42 us: local(): gathered = jnp.concatenate([gathered, swap(gathered, bit, devices)], axis=0)]
  transfers between devices with their start and end apart: 1 -> 11, of which waited for: 1 -> 11; matrix products, arithmetic and copies ran while one was open for 0% -> 0% of each run, Pallas kernels for 0% -> 0%
where the time goes in v1:
time: 61.6 us; the launch traced here: 61.2 us
  waiting for transfers between devices  27.7 us (45%)
  starting transfers between devices  17.3 us (28%)
  matrix products  7.55 us (12%)
  other arithmetic  5.02 us (8%)
  local copies, waits for them, and re-layouts  2.65 us (4%)
  between operations  0.96 us (2%)
    ppermute x11, waiting for transfers between devices, swap(): return lax.ppermute(x, 'dict', [(i, i ^ bit) for i in range(devices)])  27.7 us
    ppermute x11, starting transfers between devices, swap(): return lax.ppermute(x, 'dict', [(i, i ^ bit) for i in range(devices)])  17.3 us
    dot_general x1, matrix products, local(): jnp.einsum('tl,td->ld', act_low, errors, preferred_element_type=jnp.float32)  3.3 us
    dot_general x1, matrix products, local(): jnp.einsum('tl,td->ld', pre_low, gathered, preferred_element_type=jnp.flo...  3.09 us
    concatenate x3, other arithmetic, local(): gathered = jnp.concatenate([gathered, swap(gathered, bit, devices)], axis=0)  2.42 us
    unnamed x36, local copies, waits for them, and re-layouts  1.36 us
  transfers between devices with their start and end apart: 11, of which 11 were waited for; matrix products, arithmetic and copies ran while one was open for 0% of the time, Pallas kernels for 0%

profile of v1, /device:TPU:0, one launch (start us, length us, event | category | flops | bytes accessed | tf_op | source)
XLA Modules:
  0.0 61.2 jit_solution(5970615698503972827)
XLA Ops:
  0.7 4.1 %collective-permute-start = (bf16[4,4096]{1,0:T(4,128)(2,1)}, bf16[4,4096]{1,0:T(4,128)(2,1)S(1)}, u32[]{:S(2)}, u32[]{:S(2)}) collective-permute-start(bf16[4,4096]{1,0:T(4,128)(2,1)} %param.13), channel_id=1, source_target_pairs={{0,8},{1,9},{2,10},{3,11},{4,12},{5,13},{6,14},{7,15},{8,0},{9,1},... | collective-permute-start | bytes 98312 | tf_op jit(solution)/shard_map/ppermute | solution.py:27
  4.8 2.5 %collective-permute-done = bf16[4,4096]{1,0:T(4,128)(2,1)S(1)} collective-permute-done((bf16[4,4096]{1,0:T(4,128)(2,1)}, bf16[4,4096]{1,0:T(4,128)(2,1)S(1)}, u32[]{:S(2)}, u32[]{:S(2)}) %collective-permute-start) | collective-permute-done | bytes 32800 | tf_op jit(solution)/shard_map/ppermute | solution.py:27
  7.2 0.8 %pad_maximum_fusion.5 = bf16[8,4096]{1,0:T(8,128)(2,1)S(1)} fusion(bf16[4,4096]{1,0:T(4,128)(2,1)S(1)} %collective-permute-done, bf16[4,4096]{1,0:T(4,128)(2,1)} %param.13), kind=kLoop, calls=%fused_computation.41 | loop fusion | flops 131072 | bytes 131072 | tf_op jit(solution)/shard_map/concatenate | solution.py:50
  8.0 1.6 %collective-permute-start.1 = (bf16[8,4096]{1,0:T(8,128)(2,1)S(1)}, bf16[8,4096]{1,0:T(8,128)(2,1)S(1)}, u32[]{:S(2)}, u32[]{:S(2)}) collective-permute-start(bf16[8,4096]{1,0:T(8,128)(2,1)S(1)} %pad_maximum_fusion.5), channel_id=1, source_target_pairs={{0,4},{1,5},{2,6},{3,7},{4,0},{5,1},{6,2},{7,3},{8,12},{9,13},{10,... | collective-permute-start | bytes 196616 | tf_op jit(solution)/shard_map/ppermute | solution.py:27
  9.6 2.7 %collective-permute-done.1 = bf16[8,4096]{1,0:T(8,128)(2,1)S(1)} collective-permute-done((bf16[8,4096]{1,0:T(8,128)(2,1)S(1)}, bf16[8,4096]{1,0:T(8,128)(2,1)S(1)}, u32[]{:S(2)}, u32[]{:S(2)}) %collective-permute-start.1) | collective-permute-done | bytes 65568 | tf_op jit(solution)/shard_map/ppermute | solution.py:27
  12.4 0.8 %pad_maximum_fusion.3 = bf16[16,4096]{1,0:T(8,128)(2,1)S(1)} fusion(bf16[8,4096]{1,0:T(8,128)(2,1)S(1)} %collective-permute-done.1, bf16[4,4096]{1,0:T(4,128)(2,1)S(1)} %collective-permute-done, bf16[4,4096]{1,0:T(4,128)(2,1)} %param.13), kind=kLoop, calls=%fused_computation.32 | loop fusion | flops 393216 | bytes 262144 | tf_op jit(solution)/shard_map/concatenate | solution.py:50
  13.2 1.8 %collective-permute-start.2 = (bf16[16,4096]{1,0:T(8,128)(2,1)S(1)}, bf16[16,4096]{1,0:T(8,128)(2,1)S(1)}, u32[]{:S(2)}, u32[]{:S(2)}) collective-permute-start(bf16[16,4096]{1,0:T(8,128)(2,1)S(1)} %pad_maximum_fusion.3), channel_id=1, source_target_pairs={{0,2},{1,3},{2,0},{3,1},{4,6},{5,7},{6,4},{7,5},{8,10},{9,11},{10,... | collective-permute-start | bytes 393224 | tf_op jit(solution)/shard_map/ppermute | solution.py:27
  15.0 3.2 %collective-permute-done.2 = bf16[16,4096]{1,0:T(8,128)(2,1)S(1)} collective-permute-done((bf16[16,4096]{1,0:T(8,128)(2,1)S(1)}, bf16[16,4096]{1,0:T(8,128)(2,1)S(1)}, u32[]{:S(2)}, u32[]{:S(2)}) %collective-permute-start.2) | collective-permute-done | bytes 131104 | tf_op jit(solution)/shard_map/ppermute | solution.py:27
  18.2 0.8 %pad_maximum_fusion.1 = bf16[32,4096]{1,0:T(8,128)(2,1)S(1)} fusion(bf16[16,4096]{1,0:T(8,128)(2,1)S(1)} %collective-permute-done.2, bf16[8,4096]{1,0:T(8,128)(2,1)S(1)} %collective-permute-done.1, bf16[4,4096]{1,0:T(4,128)(2,1)S(1)} %collective-permute-done, bf16[4,4096]{1,0:T(4,128)(2,1)} %param.13), kind=kLoop, calls=%fused_computation.26 | loop fusion | flops 1048576 | bytes 524288 | tf_op jit(solution)/shard_map/concatenate | solution.py:50
  19.1 1.5 %collective-permute-done.3 = bf16[32,4096]{1,0:T(8,128)(2,1)S(1)} collective-permute-done((bf16[32,4096]{1,0:T(8,128)(2,1)S(1)}, bf16[32,4096]{1,0:T(8,128)(2,1)S(1)}, u32[]{:S(2)}, u32[]{:S(2)}) %collective-permute-start.3) | collective-permute-done | bytes 262176 | tf_op jit(solution)/shard_map/ppermute | solution.py:27
  20.6 0.9 %concatenate.32 = bf16[64,4096]{1,0:T(8,128)(2,1)S(1)} concatenate(bf16[4,4096]{1,0:T(4,128)(2,1)} %param.13, bf16[4,4096]{1,0:T(4,128)(2,1)S(1)} %collective-permute-done, bf16[8,4096]{1,0:T(8,128)(2,1)S(1)} %collective-permute-done.1, bf16[16,4096]{1,0:T(8,128)(2,1)S(1)} %collective-permute-done.2, bf16[32,4096]{1,0:T(8,128)(2,1)S(1)} %collective-permute-done.3), dimensions={0} | concatenate | bytes 1048576 | tf_op jit(solution)/shard_map/concatenate | solution.py:50
  21.6 0.4 fusion.16
  22.6 1.4 %collective-permute-done.4 = bf16[32,4096]{1,0:T(8,128)(2,1)S(1)} collective-permute-done((bf16[32,4096]{1,0:T(8,128)(2,1)S(1)}, bf16[32,4096]{1,0:T(8,128)(2,1)S(1)}, u32[]{:S(2)}, u32[]{:S(2)}) %collective-permute-start.4) | collective-permute-done | bytes 262176 | tf_op jit(solution)/shard_map/ppermute | solution.py:27
  24.1 1.8 %collective-permute-start.5 = (bf16[16,4096]{1,0:T(8,128)(2,1)S(1)}, bf16[16,4096]{1,0:T(8,128)(2,1)S(1)}, u32[]{:S(2)}, u32[]{:S(2)}) collective-permute-start(bf16[16,4096]{1,0:T(8,128)(2,1)S(1)} %slice.146), channel_id=1, source_target_pairs={{0,2},{1,3},{2,0},{3,1},{4,6},{5,7},{6,4},{7,5},{8,10},{9,11},{10,... | collective-permute-start | bytes 393224 | tf_op jit(solution)/shard_map/ppermute | solution.py:27
  25.9 3.8 %collective-permute-done.5 = bf16[16,4096]{1,0:T(8,128)(2,1)S(1)} collective-permute-done((bf16[16,4096]{1,0:T(8,128)(2,1)S(1)}, bf16[16,4096]{1,0:T(8,128)(2,1)S(1)}, u32[]{:S(2)}, u32[]{:S(2)}) %collective-permute-start.5) | collective-permute-done | bytes 131104 | tf_op jit(solution)/shard_map/ppermute | solution.py:27
  29.7 1.6 %collective-permute-start.6 = (bf16[8,4096]{1,0:T(8,128)(2,1)S(1)}, bf16[8,4096]{1,0:T(8,128)(2,1)S(1)}, u32[]{:S(2)}, u32[]{:S(2)}) collective-permute-start(bf16[8,4096]{1,0:T(8,128)(2,1)S(1)} %slice.147), channel_id=1, source_target_pairs={{0,4},{1,5},{2,6},{3,7},{4,0},{5,1},{6,2},{7,3},{8,12},{9,13},{10,... | collective-permute-start | bytes 196616 | tf_op jit(solution)/shard_map/ppermute | solution.py:27
  31.4 2.7 %collective-permute-done.6 = bf16[8,4096]{1,0:T(8,128)(2,1)S(1)} collective-permute-done((bf16[8,4096]{1,0:T(8,128)(2,1)S(1)}, bf16[8,4096]{1,0:T(8,128)(2,1)S(1)}, u32[]{:S(2)}, u32[]{:S(2)}) %collective-permute-start.6) | collective-permute-done | bytes 65568 | tf_op jit(solution)/shard_map/ppermute | solution.py:27
  34.1 2.7 %collective-permute-start.7 = (bf16[8,4096]{1,0:T(8,128)(2,1)S(1)}, bf16[8,4096]{1,0:T(8,128)(2,1)S(1)}, u32[]{:S(2)}, u32[]{:S(2)}) collective-permute-start(bf16[8,4096]{1,0:T(8,128)(2,1)S(1)} %fusion.11), channel_id=1, source_target_pairs={{0,8},{1,9},{2,10},{3,11},{4,12},{5,13},{6,14},{7,15},{8,0},{9,1},... | collective-permute-start | bytes 196616 | tf_op jit(solution)/shard_map/ppermute | solution.py:27
  36.7 2.6 %collective-permute-done.7 = bf16[8,4096]{1,0:T(8,128)(2,1)S(1)} collective-permute-done((bf16[8,4096]{1,0:T(8,128)(2,1)S(1)}, bf16[8,4096]{1,0:T(8,128)(2,1)S(1)}, u32[]{:S(2)}, u32[]{:S(2)}) %collective-permute-start.7) | collective-permute-done | bytes 65568 | tf_op jit(solution)/shard_map/ppermute | solution.py:27
  39.5 1.6 %collective-permute-start.8 = (bf16[8,4096]{1,0:T(8,128)(2,1)S(1)}, bf16[8,4096]{1,0:T(8,128)(2,1)S(1)}, u32[]{:S(2)}, u32[]{:S(2)}) collective-permute-start(bf16[8,4096]{1,0:T(8,128)(2,1)S(1)} %fusion.10), channel_id=1, source_target_pairs={{0,4},{1,5},{2,6},{3,7},{4,0},{5,1},{6,2},{7,3},{8,12},{9,13},{10,... | collective-permute-start | bytes 196616 | tf_op jit(solution)/shard_map/ppermute | solution.py:27
  41.1 2.7 %collective-permute-done.8 = bf16[8,4096]{1,0:T(8,128)(2,1)S(1)} collective-permute-done((bf16[8,4096]{1,0:T(8,128)(2,1)S(1)}, bf16[8,4096]{1,0:T(8,128)(2,1)S(1)}, u32[]{:S(2)}, u32[]{:S(2)}) %collective-permute-start.8) | collective-permute-done | bytes 65568 | tf_op jit(solution)/shard_map/ppermute | solution.py:27
  43.8 1.8 %collective-permute-start.9 = (bf16[16,4096]{1,0:T(8,128)(2,1)S(1)}, bf16[16,4096]{1,0:T(8,128)(2,1)S(1)}, u32[]{:S(2)}, u32[]{:S(2)}) collective-permute-start(bf16[16,4096]{1,0:T(8,128)(2,1)S(1)} %pad_maximum_fusion.4), channel_id=1, source_target_pairs={{0,2},{1,3},{2,0},{3,1},{4,6},{5,7},{6,4},{7,5},{8,10},{9,11},{10,... | collective-permute-start | bytes 393224 | tf_op jit(solution)/shard_map/ppermute | solution.py:27
  45.9 3.0 %collective-permute-done.9 = bf16[16,4096]{1,0:T(8,128)(2,1)S(1)} collective-permute-done((bf16[16,4096]{1,0:T(8,128)(2,1)S(1)}, bf16[16,4096]{1,0:T(8,128)(2,1)S(1)}, u32[]{:S(2)}, u32[]{:S(2)}) %collective-permute-start.9) | collective-permute-done | bytes 131104 | tf_op jit(solution)/shard_map/ppermute | solution.py:27
  49.0 1.5 %collective-permute-done.10 = bf16[32,4096]{1,0:T(8,128)(2,1)S(1)} collective-permute-done((bf16[32,4096]{1,0:T(8,128)(2,1)S(1)}, bf16[32,4096]{1,0:T(8,128)(2,1)S(1)}, u32[]{:S(2)}, u32[]{:S(2)}) %collective-permute-start.10) | collective-permute-done | bytes 262176 | tf_op jit(solution)/shard_map/ppermute | solution.py:27
  50.5 0.7 %copy-done.6 = bf16[32,4096]{1,0:T(8,128)(2,1)} copy-done((bf16[32,4096]{1,0:T(8,128)(2,1)}, bf16[32,4096]{1,0:T(8,128)(2,1)S(1)}, u32[]{:S(2)}) %copy-start.6) | copy-done | bytes 262168
  51.6 0.6 %slice_add_fusion.1 = f32[16,1,4096]{2,1,0:T(1,128)S(1)} fusion(f32[16,4,4096]{2,1,0:T(4,128)S(1)} %reshape.51), kind=kLoop, calls=%fused_computation.21 | loop fusion | flops 196608 | bytes 1310720 | tf_op jit(solution)/shard_map/add | solution.py:70
  52.6 0.6 %divide_subtract_fusion = (f32[4096]{0:T(1024)}, f32[4096]{0:T(1024)}, f32[4096]{0:T(1024)}) fusion(f32[4096]{0:T(1024)S(1)} %copy-done.8, f32[4096]{0:T(1024)S(1)} %bitcast.7, f32[4096]{0:T(1024)S(1)} %copy-done.9, f32[4096]{0:T(1024)S(1)} %copy-done.10), kind=kLoop, calls=%fused_computation.47 | loop fusion | flops 49152 | bytes 114688 | tf_op jit(solution)/shard_map/sub | solution.py:23
  53.2 0.4 fusion.28
  53.7 0.5 copy-done.14
  54.2 3.1 %subtract_convert_fusion = (bf16[82,4096]{1,0:T(8,128)(2,1)}, f32[82,4096]{1,0:T(8,128)}, f32[82,4096]{1,0:T(8,128)}) fusion(bf16[82,4096]{1,0:T(8,128)(2,1)S(1)} %copy-done.3, f32[82,4096]{1,0:T(8,128)S(1)} %copy-done.14, f32[82,4096]{1,0:T(8,128)S(1)} %copy-done.15, bf16[64,4096]{1,0:T(8,128)(2,1)S(1)} %concatenate.32, ...), kind=kOutput, calls=%fused_computation.12 | convolution fusion | flops 47693824 | bytes 7252224 | tf_op jit(solution)/shard_map/tl,td->ld/dot_general | solution.py:87
  57.3 0.5 divide_subtract_fusion.1
  57.9 3.3 %fusion.2 = (bf16[82,4096]{1,0:T(8,128)(2,1)}, f32[82,4096]{1,0:T(8,128)}, f32[82,4096]{1,0:T(8,128)}) fusion(bf16[82,4096]{1,0:T(8,128)(2,1)S(1)} %copy-done, f32[82,4096]{1,0:T(8,128)S(1)} %copy-done.16, f32[82,4096]{1,0:T(8,128)S(1)} %copy-done.17, f32[82]{0:T(128)S(1)} %get-tuple-element.26, f32[82]{0:T(128)S(1)} %broadcast_multiply_fusion, ...), kind=kOutput, calls=%fused_computation.8 | convolution fusion | flops 50840576 | bytes 7263376 | tf_op jit(solution)/shard_map/tl,td->ld/dot_general | solution.py:78
  (57 shorter events, 2.1 us)
Async XLA Ops:
  0.6 20.9 %copy-start.2 = (bf16[82,4096]{1,0:T(8,128)(2,1)S(1)}, bf16[82,4096]{1,0:T(8,128)(2,1)}, u32[]{:S(2)}) copy-start(bf16[82,4096]{1,0:T(8,128)(2,1)} %param.14) | copy-start | bytes 2015236
  0.7 20.9 %copy-start.11 = (f32[82]{0:T(128)S(1)}, f32[82]{0:T(128)}, u32[]{:S(2)}) copy-start(f32[82]{0:T(128)} %param.15) | copy-start | bytes 988
  0.7 6.6 %collective-permute-start = (bf16[4,4096]{1,0:T(4,128)(2,1)}, bf16[4,4096]{1,0:T(4,128)(2,1)S(1)}, u32[]{:S(2)}, u32[]{:S(2)}) collective-permute-start(bf16[4,4096]{1,0:T(4,128)(2,1)} %param.13), channel_id=1, source_target_pairs={{0,8},{1,9},{2,10},{3,11},{4,12},{5,13},{6,14},{7,15},{8,0},{9,1},... | collective-permute-start | bytes 98312 | tf_op jit(solution)/shard_map/ppermute | solution.py:27
  8.0 4.3 %collective-permute-start.1 = (bf16[8,4096]{1,0:T(8,128)(2,1)S(1)}, bf16[8,4096]{1,0:T(8,128)(2,1)S(1)}, u32[]{:S(2)}, u32[]{:S(2)}) collective-permute-start(bf16[8,4096]{1,0:T(8,128)(2,1)S(1)} %pad_maximum_fusion.5), channel_id=1, source_target_pairs={{0,4},{1,5},{2,6},{3,7},{4,0},{5,1},{6,2},{7,3},{8,12},{9,13},{10,... | collective-permute-start | bytes 196616 | tf_op jit(solution)/shard_map/ppermute | solution.py:27
  13.2 8.8 %copy-start = (bf16[82,4096]{1,0:T(8,128)(2,1)S(1)}, bf16[82,4096]{1,0:T(8,128)(2,1)}, u32[]{:S(2)}) copy-start(bf16[82,4096]{1,0:T(8,128)(2,1)} %param.16) | copy-start | bytes 2015236
  13.2 5.0 %collective-permute-start.2 = (bf16[16,4096]{1,0:T(8,128)(2,1)S(1)}, bf16[16,4096]{1,0:T(8,128)(2,1)S(1)}, u32[]{:S(2)}, u32[]{:S(2)}) collective-permute-start(bf16[16,4096]{1,0:T(8,128)(2,1)S(1)} %pad_maximum_fusion.3), channel_id=1, source_target_pairs={{0,2},{1,3},{2,0},{3,1},{4,6},{5,7},{6,4},{7,5},{8,10},{9,11},{10,... | collective-permute-start | bytes 393224 | tf_op jit(solution)/shard_map/ppermute | solution.py:27
  19.0 1.6 %collective-permute-start.3 = (bf16[32,4096]{1,0:T(8,128)(2,1)S(1)}, bf16[32,4096]{1,0:T(8,128)(2,1)S(1)}, u32[]{:S(2)}, u32[]{:S(2)}) collective-permute-start(bf16[32,4096]{1,0:T(8,128)(2,1)S(1)} %pad_maximum_fusion.1), channel_id=1, source_target_pairs={{0,1},{1,0},{2,3},{3,2},{4,5},{5,4},{6,7},{7,6},{8,9},{9,8},{10,11... | collective-permute-start | bytes 786440 | tf_op jit(solution)/shard_map/ppermute | solution.py:27
  22.4 17.0 %copy-start.1 = (bf16[4,4096]{1,0:T(4,128)(2,1)S(1)}, bf16[4,4096]{1,0:T(4,128)(2,1)}, u32[]{:S(2)}) copy-start(bf16[4,4096]{1,0:T(4,128)(2,1)} %param.13) | copy-start | bytes 98308
  22.4 17.0 %copy-start.8 = (f32[4096]{0:T(1024)S(1)}, f32[4096]{0:T(1024)}, u32[]{:S(2)}) copy-start(f32[4096]{0:T(1024)} %param.17) | copy-start | bytes 49156
  22.4 1.6 %collective-permute-start.4 = (bf16[32,4096]{1,0:T(8,128)(2,1)S(1)}, bf16[32,4096]{1,0:T(8,128)(2,1)S(1)}, u32[]{:S(2)}, u32[]{:S(2)}) collective-permute-start(bf16[32,4096]{1,0:T(8,128)(2,1)S(1)} %slice.145), channel_id=1, source_target_pairs={{0,1},{1,0},{2,3},{3,2},{4,5},{5,4},{6,7},{7,6},{8,9},{9,8},{10,11... | collective-permute-start | bytes 786440 | tf_op jit(solution)/shard_map/ppermute | solution.py:27
  24.1 5.6 %collective-permute-start.5 = (bf16[16,4096]{1,0:T(8,128)(2,1)S(1)}, bf16[16,4096]{1,0:T(8,128)(2,1)S(1)}, u32[]{:S(2)}, u32[]{:S(2)}) collective-permute-start(bf16[16,4096]{1,0:T(8,128)(2,1)S(1)} %slice.146), channel_id=1, source_target_pairs={{0,2},{1,3},{2,0},{3,1},{4,6},{5,7},{6,4},{7,5},{8,10},{9,11},{10,... | collective-permute-start | bytes 393224 | tf_op jit(solution)/shard_map/ppermute | solution.py:27
  29.7 4.3 %collective-permute-start.6 = (bf16[8,4096]{1,0:T(8,128)(2,1)S(1)}, bf16[8,4096]{1,0:T(8,128)(2,1)S(1)}, u32[]{:S(2)}, u32[]{:S(2)}) collective-permute-start(bf16[8,4096]{1,0:T(8,128)(2,1)S(1)} %slice.147), channel_id=1, source_target_pairs={{0,4},{1,5},{2,6},{3,7},{4,0},{5,1},{6,2},{7,3},{8,12},{9,13},{10,... | collective-permute-start | bytes 196616 | tf_op jit(solution)/shard_map/ppermute | solution.py:27
  34.1 5.2 %collective-permute-start.7 = (bf16[8,4096]{1,0:T(8,128)(2,1)S(1)}, bf16[8,4096]{1,0:T(8,128)(2,1)S(1)}, u32[]{:S(2)}, u32[]{:S(2)}) collective-permute-start(bf16[8,4096]{1,0:T(8,128)(2,1)S(1)} %fusion.11), channel_id=1, source_target_pairs={{0,8},{1,9},{2,10},{3,11},{4,12},{5,13},{6,14},{7,15},{8,0},{9,1},... | collective-permute-start | bytes 196616 | tf_op jit(solution)/shard_map/ppermute | solution.py:27
  39.5 4.3 %collective-permute-start.8 = (bf16[8,4096]{1,0:T(8,128)(2,1)S(1)}, bf16[8,4096]{1,0:T(8,128)(2,1)S(1)}, u32[]{:S(2)}, u32[]{:S(2)}) collective-permute-start(bf16[8,4096]{1,0:T(8,128)(2,1)S(1)} %fusion.10), channel_id=1, source_target_pairs={{0,4},{1,5},{2,6},{3,7},{4,0},{5,1},{6,2},{7,3},{8,12},{9,13},{10,... | collective-permute-start | bytes 196616 | tf_op jit(solution)/shard_map/ppermute | solution.py:27
  43.8 5.0 %collective-permute-start.9 = (bf16[16,4096]{1,0:T(8,128)(2,1)S(1)}, bf16[16,4096]{1,0:T(8,128)(2,1)S(1)}, u32[]{:S(2)}, u32[]{:S(2)}) collective-permute-start(bf16[16,4096]{1,0:T(8,128)(2,1)S(1)} %pad_maximum_fusion.4), channel_id=1, source_target_pairs={{0,2},{1,3},{2,0},{3,1},{4,6},{5,7},{6,4},{7,5},{8,10},{9,11},{10,... | collective-permute-start | bytes 393224 | tf_op jit(solution)/shard_map/ppermute | solution.py:27
  48.9 1.6 %copy-start.4 = (bf16[16,4096]{1,0:T(8,128)(2,1)}, bf16[16,4096]{1,0:T(8,128)(2,1)S(1)}, u32[]{:S(2)}) copy-start(bf16[16,4096]{1,0:T(8,128)(2,1)S(1)} %collective-permute-done.9) | copy-start | bytes 393220
  48.9 1.6 %collective-permute-start.10 = (bf16[32,4096]{1,0:T(8,128)(2,1)S(1)}, bf16[32,4096]{1,0:T(8,128)(2,1)S(1)}, u32[]{:S(2)}, u32[]{:S(2)}) collective-permute-start(bf16[32,4096]{1,0:T(8,128)(2,1)S(1)} %pad_maximum_fusion.2), channel_id=1, source_target_pairs={{0,1},{1,0},{2,3},{3,2},{4,5},{5,4},{6,7},{7,6},{8,9},{9,8},{10,11... | collective-permute-start | bytes 786440 | tf_op jit(solution)/shard_map/ppermute | solution.py:27
  50.5 0.7 %copy-start.6 = (bf16[32,4096]{1,0:T(8,128)(2,1)}, bf16[32,4096]{1,0:T(8,128)(2,1)S(1)}, u32[]{:S(2)}) copy-start(bf16[32,4096]{1,0:T(8,128)(2,1)S(1)} %collective-permute-done.10) | copy-start | bytes 786436
  51.6 1.0 %copy-start.9 = (f32[4096]{0:T(1024)S(1)}, f32[4096]{0:T(1024)}, u32[]{:S(2)}) copy-start(f32[4096]{0:T(1024)} %param.24) | copy-start | bytes 49156
  51.6 1.0 %copy-start.10 = (f32[4096]{0:T(1024)S(1)}, f32[4096]{0:T(1024)}, u32[]{:S(2)}) copy-start(f32[4096]{0:T(1024)} %param.25) | copy-start | bytes 49156
  51.6 1.6 %copy-start.5 = (bf16[16,4096]{1,0:T(8,128)(2,1)S(1)}, bf16[16,4096]{1,0:T(8,128)(2,1)}, u32[]{:S(2)}) copy-start(bf16[16,4096]{1,0:T(8,128)(2,1)} %copy-done.4) | copy-start | bytes 393220
  51.6 1.6 %copy-start.7 = (bf16[32,4096]{1,0:T(8,128)(2,1)S(1)}, bf16[32,4096]{1,0:T(8,128)(2,1)}, u32[]{:S(2)}) copy-start(bf16[32,4096]{1,0:T(8,128)(2,1)} %copy-done.6) | copy-start | bytes 786436
  51.6 2.0 %copy-start.15 = (f32[82,4096]{1,0:T(8,128)S(1)}, f32[82,4096]{1,0:T(8,128)}, u32[]{:S(2)}) copy-start(f32[82,4096]{1,0:T(8,128)} %param.19) | copy-start | bytes 4030468
  52.5 1.3 %copy-start.3 = (bf16[82,4096]{1,0:T(8,128)(2,1)S(1)}, bf16[82,4096]{1,0:T(8,128)(2,1)}, u32[]{:S(2)}) copy-start(bf16[82,4096]{1,0:T(8,128)(2,1)} %param.14) | copy-start | bytes 2015236
  52.5 1.7 %copy-start.14 = (f32[82,4096]{1,0:T(8,128)S(1)}, f32[82,4096]{1,0:T(8,128)}, u32[]{:S(2)}) copy-start(f32[82,4096]{1,0:T(8,128)} %param.18) | copy-start | bytes 4030468
  54.2 3.1 %copy-start.12 = (f32[82]{0:T(128)S(1)}, f32[82]{0:T(128)}, u32[]{:S(2)}) copy-start(f32[82]{0:T(128)} %param.22) | copy-start | bytes 988
  54.2 3.1 %copy-start.13 = (f32[82]{0:T(128)S(1)}, f32[82]{0:T(128)}, u32[]{:S(2)}) copy-start(f32[82]{0:T(128)} %param.23) | copy-start | bytes 988
  54.2 3.6 %copy-start.16 = (f32[82,4096]{1,0:T(8,128)S(1)}, f32[82,4096]{1,0:T(8,128)}, u32[]{:S(2)}) copy-start(f32[82,4096]{1,0:T(8,128)} %param.20) | copy-start | bytes 4030468
  54.2 3.6 %copy-start.17 = (f32[82,4096]{1,0:T(8,128)S(1)}, f32[82,4096]{1,0:T(8,128)}, u32[]{:S(2)}) copy-start(f32[82,4096]{1,0:T(8,128)} %param.21) | copy-start | bytes 4030468

commit v2 on v1

--- a/solution.py
+++ b/solution.py
@@ -27,6 +27,11 @@
     return lax.ppermute(x, "dict", [(i, i ^ bit) for i in range(devices)])
 
 
+def activation(tokens, weight, bias):
+    pre = jnp.einsum("td,ld->tl", tokens, weight, preferred_element_type=jnp.float32) + bias
+    return pre, jax.nn.softplus(sharpness * pre) / sharpness
+
+
 def local(
     devices,
     tokens,
@@ -43,27 +48,36 @@
     feature_first,
     feature_second,
 ):
-    bits = [1 << b for b in reversed(range(devices.bit_length() - 1))]
+    bits = [1 << b for b in reversed(range(1, devices.bit_length() - 1))]
     own = tokens.shape[0]
-    gathered = tokens
+    mate_encoder = swap(encoder_weight, 1, devices)
+    mate_bias = swap(encoder_bias, 1, devices)
+    mate_decoder = swap(decoder_weight, 1, devices)
+    column = tokens
     for bit in bits:
-        gathered = jnp.concatenate([gathered, swap(gathered, bit, devices)], axis=0)
-    pre = (
-        jnp.einsum("td,ld->tl", gathered, encoder_weight, preferred_element_type=jnp.float32)
-        + encoder_bias
+        column = lax.optimization_barrier(jnp.concatenate([column, swap(column, bit, devices)], axis=0))
+    part = jnp.dot(
+        activation(column, encoder_weight, encoder_bias)[1].astype(jnp.bfloat16),
+        decoder_weight,
+        preferred_element_type=jnp.float32,
+    ) + jnp.dot(
+        activation(column, mate_encoder, mate_bias)[1].astype(jnp.bfloat16),
+        mate_decoder,
+        preferred_element_type=jnp.float32,
     )
-    act = jax.nn.softplus(sharpness * pre) / sharpness
+    half = part.shape[0] // 2
+    part = part[:half] + swap(part[half:].astype(jnp.bfloat16), bits[-1], devices).astype(jnp.float32)
+    for level in reversed(range(len(bits) - 1)):
+        part = lax.reduce_precision(part, 8, 7)
+        other = swap(part.astype(jnp.bfloat16), bits[level], devices).astype(jnp.float32)
+        other = other.reshape(-1, 2, own << level, other.shape[-1])
+        part = part + other[:, ::-1].reshape(part.shape)
+    errors = (part + decoder_bias - column[:half].astype(jnp.float32)).astype(jnp.bfloat16)
+    errors = lax.optimization_barrier(jnp.concatenate([errors, swap(errors, bits[-1], devices)], axis=0))
+    errors = lax.optimization_barrier(jnp.concatenate([errors, swap(errors, 1, devices)], axis=0))
+    gathered = jnp.concatenate([column, swap(column, 1, devices)], axis=0)
+    pre, act = activation(gathered, encoder_weight, encoder_bias)
     act_low = act.astype(jnp.bfloat16)
-    part = jnp.dot(act_low, decoder_weight, preferred_element_type=jnp.float32)
-    for bit in reversed(bits[1:]):
-        half = part.shape[0] // 2
-        part = part[:half] + swap(part[half:].astype(jnp.bfloat16), bit, devices).astype(jnp.float32)
-    part = lax.reduce_precision(part, 8, 7)
-    other = swap(part.astype(jnp.bfloat16), bits[0], devices).astype(jnp.float32)
-    recon = part + jnp.concatenate([other[own:], other[:own]], axis=0)
-    errors = (recon + decoder_bias - gathered[: 2 * own].astype(jnp.float32)).astype(jnp.bfloat16)
-    for bit in bits[1:]:
-        errors = jnp.concatenate([errors, swap(errors, bit, devices)], axis=0)
     rows = errors.astype(jnp.float32).reshape(devices, own, -1)
     feature_grad = rows[:, 0]
     for row in range(1, own):

time: 61.6 us -> 55.3 us (0.90)
  waiting for transfers between devices: 27.7 us -> 22.4 us
  matrix products: 7.55 us -> 9.75 us
  local copies, waits for them, and re-layouts: 2.65 us -> 0.9 us
  other arithmetic: 5.02 us -> 3.35 us
    ppermute x11 -> x12, waiting for transfers between devices: 27.7 us -> 22.4 us  [swap(): return lax.ppermute(x, 'dict', [(i, i ^ bit) for i in range(devices)])]
    dot_general x2 -> x3, matrix products: 0.76 us -> 2.99 us  [the longest x1 1.96 us: local(): jnp.dot(activation(column, encoder_weight, encoder_bias)[1].astype(jnp.bf...]
    concatenate x5, other arithmetic: 2.45 us -> 0.87 us  [the longest x3 0.82 us: local(): jnp.concatenate([column, swap(column, bit, devices)], axis=0)]
    unnamed x36 -> x28, local copies, waits for them, and re-layouts: 1.36 us -> 0.36 us
    concatenate x1 -> x0, local copies, waits for them, and re-layouts: 0.9 us -> none  [local(): gathered = jnp.concatenate([gathered, swap(gathered, bit, devices)], axis=0)]
    ppermute x11 -> x12, starting transfers between devices: 17.3 us -> 17.7 us  [swap(): return lax.ppermute(x, 'dict', [(i, i ^ bit) for i in range(devices)])]
  transfers between devices with their start and end apart: 11 -> 12, of which waited for: 11 -> 8; matrix products, arithmetic and copies ran while one was open for 0% -> 5% of each run, Pallas kernels for 0% -> 0%
where the time goes in v2:
time: 55.3 us; the launch traced here: 55 us
  waiting for transfers between devices  22.4 us (41%)
  starting transfers between devices  17.7 us (32%)
  matrix products  9.75 us (18%)
  other arithmetic  3.35 us (6%)
  between operations  0.96 us (2%)
  local copies, waits for them, and re-layouts  0.9 us (2%)
    ppermute x12, waiting for transfers between devices, swap(): return lax.ppermute(x, 'dict', [(i, i ^ bit) for i in range(devices)])  22.4 us
    ppermute x12, starting transfers between devices, swap(): return lax.ppermute(x, 'dict', [(i, i ^ bit) for i in range(devices)])  17.7 us
    dot_general x1, matrix products, local(): jnp.einsum('tl,td->ld', act_low, errors, preferred_element_type=jnp.float32)  3.28 us
    dot_general x1, matrix products, local(): jnp.einsum('tl,td->ld', pre_low, gathered, preferred_element_type=jnp.flo...  3.08 us
    dot_general x1, matrix products, local(): jnp.dot(activation(column, encoder_weight, encoder_bias)[1].astype(jnp.bf...  1.96 us
    sub x2, other arithmetic, adam_update(): return (param.astype(jnp.float32) - change, first_new, second_new)  1.17 us
  transfers between devices with their start and end apart: 12, of which 8 were waited for; matrix products, arithmetic and copies ran while one was open for 5% of the time, Pallas kernels for 0%

profile of v2, /device:TPU:0, one launch (start us, length us, event | category | flops | bytes accessed | tf_op | source)
XLA Modules:
  0.0 55.0 jit_solution(3320110374487170352)
XLA Ops:
  0.6 4.1 %collective-permute-start = (bf16[4,4096]{1,0:T(4,128)(2,1)}, bf16[4,4096]{1,0:T(4,128)(2,1)S(1)}, u32[]{:S(2)}, u32[]{:S(2)}) collective-permute-start(bf16[4,4096]{1,0:T(4,128)(2,1)} %param.13), channel_id=1, source_target_pairs={{0,8},{1,9},{2,10},{3,11},{4,12},{5,13},{6,14},{7,15},{8,0},{9,1},... | collective-permute-start | bytes 98312 | tf_op jit(solution)/shard_map/ppermute | solution.py:27
  4.7 2.5 %collective-permute-done = bf16[4,4096]{1,0:T(4,128)(2,1)S(1)} collective-permute-done((bf16[4,4096]{1,0:T(4,128)(2,1)}, bf16[4,4096]{1,0:T(4,128)(2,1)S(1)}, u32[]{:S(2)}, u32[]{:S(2)}) %collective-permute-start) | collective-permute-done | bytes 32800 | tf_op jit(solution)/shard_map/ppermute | solution.py:27
  7.2 0.8 %pad_maximum_fusion.7 = bf16[8,4096]{1,0:T(8,128)(2,1)S(1)} fusion(bf16[4,4096]{1,0:T(4,128)(2,1)S(1)} %collective-permute-done, bf16[4,4096]{1,0:T(4,128)(2,1)} %param.13), kind=kLoop, calls=%fused_computation.43 | loop fusion | flops 131072 | bytes 131072 | tf_op jit(solution)/shard_map/concatenate | solution.py:58
  8.0 1.6 %collective-permute-start.1 = (bf16[8,4096]{1,0:T(8,128)(2,1)S(1)}, bf16[8,4096]{1,0:T(8,128)(2,1)S(1)}, u32[]{:S(2)}, u32[]{:S(2)}) collective-permute-start(bf16[8,4096]{1,0:T(8,128)(2,1)S(1)} %pad_maximum_fusion.7), channel_id=1, source_target_pairs={{0,4},{1,5},{2,6},{3,7},{4,0},{5,1},{6,2},{7,3},{8,12},{9,13},{10,... | collective-permute-start | bytes 196616 | tf_op jit(solution)/shard_map/ppermute | solution.py:27
  9.6 2.7 %collective-permute-done.1 = bf16[8,4096]{1,0:T(8,128)(2,1)S(1)} collective-permute-done((bf16[8,4096]{1,0:T(8,128)(2,1)S(1)}, bf16[8,4096]{1,0:T(8,128)(2,1)S(1)}, u32[]{:S(2)}, u32[]{:S(2)}) %collective-permute-start.1) | collective-permute-done | bytes 65568 | tf_op jit(solution)/shard_map/ppermute | solution.py:27
  12.3 1.8 %collective-permute-start.2 = (bf16[16,4096]{1,0:T(8,128)(2,1)S(1)}, bf16[16,4096]{1,0:T(8,128)(2,1)S(1)}, u32[]{:S(2)}, u32[]{:S(2)}) collective-permute-start(bf16[16,4096]{1,0:T(8,128)(2,1)S(1)} %pad_maximum_fusion.6), channel_id=1, source_target_pairs={{0,2},{1,3},{2,0},{3,1},{4,6},{5,7},{6,4},{7,5},{8,10},{9,11},{10,... | collective-permute-start | bytes 393224 | tf_op jit(solution)/shard_map/ppermute | solution.py:27
  14.1 0.5 collective-permute-start.3
  14.6 2.7 %collective-permute-done.2 = bf16[16,4096]{1,0:T(8,128)(2,1)S(1)} collective-permute-done((bf16[16,4096]{1,0:T(8,128)(2,1)S(1)}, bf16[16,4096]{1,0:T(8,128)(2,1)S(1)}, u32[]{:S(2)}, u32[]{:S(2)}) %collective-permute-start.2) | collective-permute-done | bytes 131104 | tf_op jit(solution)/shard_map/ppermute | solution.py:27
  17.4 2.0 %fusion.21 = f32[32,4096]{1,0:T(8,128)S(1)} fusion(bf16[82,4096]{1,0:T(8,128)(2,1)} %param.16, bf16[32,4096]{1,0:T(8,128)(2,1)S(1)} %pad_maximum_fusion.4, bf16[82,4096]{1,0:T(8,128)(2,1)} %param.14, f32[82]{0:T(128)} %param.15), kind=kOutput, calls=%fused_computation.59 | convolution fusion | flops 43017856 | bytes 2130248 | tf_op jit(solution)/shard_map/dot_general | solution.py:59
  19.4 0.6 %convolution_add_fusion.1 = f32[32,4096]{1,0:T(8,128)S(1)} fusion(f32[32,4096]{1,0:T(8,128)S(1)} %fusion.21, bf16[82,4096]{1,0:T(8,128)(2,1)S(1)} %collective-permute-done.5, bf16[32,4096]{1,0:T(8,128)(2,1)S(1)} %pad_maximum_fusion.4, bf16[82,4096]{1,0:T(8,128)(2,1)S(1)} %collective-permute-done.3, f32[82]{0:T(128)S(1)} %collective-permute-done.4), kind=kOutput, calls=%fused_computation.1 | convolution fusion | flops 43148928 | bytes 2654536 | tf_op jit(solution)/shard_map/dot_general | solution.py:63
  20.1 1.8 %collective-permute-start.6 = (bf16[16,4096]{1,0:T(8,128)(2,1)S(1)}, bf16[16,4096]{1,0:T(8,128)(2,1)S(1)}, u32[]{:S(2)}, u32[]{:S(2)}) collective-permute-start(bf16[16,4096]{1,0:T(8,128)(2,1)S(1)} %slice.119), channel_id=1, source_target_pairs={{0,2},{1,3},{2,0},{3,1},{4,6},{5,7},{6,4},{7,5},{8,10},{9,11},{10,... | collective-permute-start | bytes 393224 | tf_op jit(solution)/shard_map/ppermute | solution.py:27
  21.8 3.2 %collective-permute-done.6 = bf16[16,4096]{1,0:T(8,128)(2,1)S(1)} collective-permute-done((bf16[16,4096]{1,0:T(8,128)(2,1)S(1)}, bf16[16,4096]{1,0:T(8,128)(2,1)S(1)}, u32[]{:S(2)}, u32[]{:S(2)}) %collective-permute-start.6) | collective-permute-done | bytes 131104 | tf_op jit(solution)/shard_map/ppermute | solution.py:27
  25.1 1.6 %collective-permute-start.7 = (bf16[16,4096]{1,0:T(8,128)(2,1)S(1)}, bf16[16,4096]{1,0:T(8,128)(2,1)S(1)}, u32[]{:S(2)}, u32[]{:S(2)}) collective-permute-start(bf16[16,4096]{1,0:T(8,128)(2,1)S(1)} %fusion.12), channel_id=1, source_target_pairs={{0,4},{1,5},{2,6},{3,7},{4,0},{5,1},{6,2},{7,3},{8,12},{9,13},{10,... | collective-permute-start | bytes 393224 | tf_op jit(solution)/shard_map/ppermute | solution.py:27
  26.7 3.4 %collective-permute-done.7 = bf16[16,4096]{1,0:T(8,128)(2,1)S(1)} collective-permute-done((bf16[16,4096]{1,0:T(8,128)(2,1)S(1)}, bf16[16,4096]{1,0:T(8,128)(2,1)S(1)}, u32[]{:S(2)}, u32[]{:S(2)}) %collective-permute-start.7) | collective-permute-done | bytes 131104 | tf_op jit(solution)/shard_map/ppermute | solution.py:27
  30.2 3.8 %collective-permute-start.8 = (bf16[16,4096]{1,0:T(8,128)(2,1)S(1)}, bf16[16,4096]{1,0:T(8,128)(2,1)S(1)}, u32[]{:S(2)}, u32[]{:S(2)}) collective-permute-start(bf16[16,4096]{1,0:T(8,128)(2,1)S(1)} %fusion.43), channel_id=1, source_target_pairs={{0,8},{1,9},{2,10},{3,11},{4,12},{5,13},{6,14},{7,15},{8,0},{9,1},... | collective-permute-start | bytes 393224 | tf_op jit(solution)/shard_map/ppermute | solution.py:27
  34.0 0.2 fusion
  34.2 4.1 %collective-permute-done.8 = bf16[16,4096]{1,0:T(8,128)(2,1)S(1)} collective-permute-done((bf16[16,4096]{1,0:T(8,128)(2,1)S(1)}, bf16[16,4096]{1,0:T(8,128)(2,1)S(1)}, u32[]{:S(2)}, u32[]{:S(2)}) %collective-permute-start.8) | collective-permute-done | bytes 131104 | tf_op jit(solution)/shard_map/ppermute | solution.py:27
  38.5 0.1 reshape.77
  38.6 0.1 subtract_convert_fusion.1
  38.7 2.4 %collective-permute-start.9 = (bf16[16,4096]{1,0:T(8,128)(2,1)S(1)}, bf16[16,4096]{1,0:T(8,128)(2,1)S(1)}, u32[]{:S(2)}, u32[]{:S(2)}) collective-permute-start(bf16[16,4096]{1,0:T(8,128)(2,1)S(1)} %subtract_convert_fusion.1), channel_id=1, source_target_pairs={{0,2},{1,3},{2,0},{3,1},{4,6},{5,7},{6,4},{7,5},{8,10},{9,11},{10,... | collective-permute-start | bytes 393224 | tf_op jit(solution)/shard_map/ppermute | solution.py:27
  41.1 2.9 %collective-permute-done.9 = bf16[16,4096]{1,0:T(8,128)(2,1)S(1)} collective-permute-done((bf16[16,4096]{1,0:T(8,128)(2,1)S(1)}, bf16[16,4096]{1,0:T(8,128)(2,1)S(1)}, u32[]{:S(2)}, u32[]{:S(2)}) %collective-permute-start.9) | collective-permute-done | bytes 131104 | tf_op jit(solution)/shard_map/ppermute | solution.py:27
  44.2 0.4 fusion.22
  44.6 0.3 copy-done.12
  44.9 0.8 %collective-permute-done.10 = bf16[32,4096]{1,0:T(8,128)(2,1)S(1)} collective-permute-done((bf16[32,4096]{1,0:T(8,128)(2,1)S(1)}, bf16[32,4096]{1,0:T(8,128)(2,1)S(1)}, u32[]{:S(2)}, u32[]{:S(2)}) %collective-permute-start.10) | collective-permute-done | bytes 262176 | tf_op jit(solution)/shard_map/ppermute | solution.py:27
  45.7 0.3 reshape.85
  46.1 0.6 %slice_add_fusion = f32[16,1,4096]{2,1,0:T(1,128)S(1)} fusion(f32[16,4,4096]{2,1,0:T(4,128)S(1)} %reshape.85), kind=kLoop, calls=%fused_computation.26 | loop fusion | flops 196608 | bytes 1310720 | tf_op jit(solution)/shard_map/add | solution.py:84
  46.8 0.1 slice_add_fusion.4
  47.0 0.4 fusion.48
  47.5 0.5 divide_subtract_fusion.1
  48.0 0.6 %divide_subtract_fusion = (f32[4096]{0:T(1024)}, f32[4096]{0:T(1024)}, f32[4096]{0:T(1024)}) fusion(f32[4096]{0:T(1024)S(1)} %copy-done.2, f32[4096]{0:T(1024)S(1)} %bitcast.23, f32[4096]{0:T(1024)S(1)} %copy-done.3, f32[4096]{0:T(1024)S(1)} %copy-done.4), kind=kLoop, calls=%fused_computation.55 | loop fusion | flops 49152 | bytes 114688 | tf_op jit(solution)/shard_map/sub | solution.py:23
  48.7 3.3 %fusion.2 = (bf16[82,4096]{1,0:T(8,128)(2,1)}, f32[82,4096]{1,0:T(8,128)}, f32[82,4096]{1,0:T(8,128)}) fusion(bf16[82,4096]{1,0:T(8,128)(2,1)S(1)} %copy-done, f32[82,4096]{1,0:T(8,128)S(1)} %copy-done.8, f32[82,4096]{1,0:T(8,128)S(1)} %copy-done.9, f32[82]{0:T(128)S(1)} %get-tuple-element.24, f32[82]{0:T(128)S(1)} %broadcast_multiply_fusion, ...), kind=kOutput, calls=%fused_computation.9 | convolution fusion | flops 48743424 | bytes 7263376 | tf_op jit(solution)/shard_map/tl,td->ld/dot_general | solution.py:92
  52.0 3.1 %subtract_convert_fusion = (bf16[82,4096]{1,0:T(8,128)(2,1)}, f32[82,4096]{1,0:T(8,128)}, f32[82,4096]{1,0:T(8,128)}) fusion(bf16[82,4096]{1,0:T(8,128)(2,1)S(1)} %copy-done.1, f32[82,4096]{1,0:T(8,128)S(1)} %copy-done.10, f32[82,4096]{1,0:T(8,128)S(1)} %copy-done.11, bf16[32,4096]{1,0:T(8,128)(2,1)S(1)} %copy-done.13, ...), kind=kOutput, calls=%fused_computation.13 | convolution fusion | flops 48742400 | bytes 7252224 | tf_op jit(solution)/shard_map/tl,td->ld/dot_general | solution.py:101
  (50 shorter events, 0.6 us)
Async XLA Ops:
  0.6 6.6 %collective-permute-start = (bf16[4,4096]{1,0:T(4,128)(2,1)}, bf16[4,4096]{1,0:T(4,128)(2,1)S(1)}, u32[]{:S(2)}, u32[]{:S(2)}) collective-permute-start(bf16[4,4096]{1,0:T(4,128)(2,1)} %param.13), channel_id=1, source_target_pairs={{0,8},{1,9},{2,10},{3,11},{4,12},{5,13},{6,14},{7,15},{8,0},{9,1},... | collective-permute-start | bytes 98312 | tf_op jit(solution)/shard_map/ppermute | solution.py:27
  8.0 4.3 %collective-permute-start.1 = (bf16[8,4096]{1,0:T(8,128)(2,1)S(1)}, bf16[8,4096]{1,0:T(8,128)(2,1)S(1)}, u32[]{:S(2)}, u32[]{:S(2)}) collective-permute-start(bf16[8,4096]{1,0:T(8,128)(2,1)S(1)} %pad_maximum_fusion.7), channel_id=1, source_target_pairs={{0,4},{1,5},{2,6},{3,7},{4,0},{5,1},{6,2},{7,3},{8,12},{9,13},{10,... | collective-permute-start | bytes 196616 | tf_op jit(solution)/shard_map/ppermute | solution.py:27
  12.3 5.0 %collective-permute-start.2 = (bf16[16,4096]{1,0:T(8,128)(2,1)S(1)}, bf16[16,4096]{1,0:T(8,128)(2,1)S(1)}, u32[]{:S(2)}, u32[]{:S(2)}) collective-permute-start(bf16[16,4096]{1,0:T(8,128)(2,1)S(1)} %pad_maximum_fusion.6), channel_id=1, source_target_pairs={{0,2},{1,3},{2,0},{3,1},{4,6},{5,7},{6,4},{7,5},{8,10},{9,11},{10,... | collective-permute-start | bytes 393224 | tf_op jit(solution)/shard_map/ppermute | solution.py:27
  14.1 5.2 %collective-permute-start.4 = (f32[82]{0:T(128)}, f32[82]{0:T(128)S(1)}, u32[]{:S(2)}, u32[]{:S(2)}) collective-permute-start(f32[82]{0:T(128)} %param.15), channel_id=1, source_target_pairs={{0,1},{1,0},{2,3},{3,2},{4,5},{5,4},{6,7},{7,6},{8,9},{9,8},{10,11... | collective-permute-start | bytes 992 | tf_op jit(solution)/shard_map/ppermute | solution.py:27
  14.1 5.2 %collective-permute-start.3 = (bf16[82,4096]{1,0:T(8,128)(2,1)}, bf16[82,4096]{1,0:T(8,128)(2,1)S(1)}, u32[]{:S(2)}, u32[]{:S(2)}) collective-permute-start(bf16[82,4096]{1,0:T(8,128)(2,1)} %param.14), channel_id=1, source_target_pairs={{0,1},{1,0},{2,3},{3,2},{4,5},{5,4},{6,7},{7,6},{8,9},{9,8},{10,11... | collective-permute-start | bytes 2015240 | tf_op jit(solution)/shard_map/ppermute | solution.py:27
  14.6 4.7 %collective-permute-start.5 = (bf16[82,4096]{1,0:T(8,128)(2,1)}, bf16[82,4096]{1,0:T(8,128)(2,1)S(1)}, u32[]{:S(2)}, u32[]{:S(2)}) collective-permute-start(bf16[82,4096]{1,0:T(8,128)(2,1)} %param.16), channel_id=1, source_target_pairs={{0,1},{1,0},{2,3},{3,2},{4,5},{5,4},{6,7},{7,6},{8,9},{9,8},{10,11... | collective-permute-start | bytes 2015240 | tf_op jit(solution)/shard_map/ppermute | solution.py:27
  20.0 14.0 %copy-start = (bf16[82,4096]{1,0:T(8,128)(2,1)S(1)}, bf16[82,4096]{1,0:T(8,128)(2,1)}, u32[]{:S(2)}) copy-start(bf16[82,4096]{1,0:T(8,128)(2,1)} %param.16) | copy-start | bytes 2015236
  20.1 5.0 %collective-permute-start.6 = (bf16[16,4096]{1,0:T(8,128)(2,1)S(1)}, bf16[16,4096]{1,0:T(8,128)(2,1)S(1)}, u32[]{:S(2)}, u32[]{:S(2)}) collective-permute-start(bf16[16,4096]{1,0:T(8,128)(2,1)S(1)} %slice.119), channel_id=1, source_target_pairs={{0,2},{1,3},{2,0},{3,1},{4,6},{5,7},{6,4},{7,5},{8,10},{9,11},{10,... | collective-permute-start | bytes 393224 | tf_op jit(solution)/shard_map/ppermute | solution.py:27
  25.1 5.0 %collective-permute-start.7 = (bf16[16,4096]{1,0:T(8,128)(2,1)S(1)}, bf16[16,4096]{1,0:T(8,128)(2,1)S(1)}, u32[]{:S(2)}, u32[]{:S(2)}) collective-permute-start(bf16[16,4096]{1,0:T(8,128)(2,1)S(1)} %fusion.12), channel_id=1, source_target_pairs={{0,4},{1,5},{2,6},{3,7},{4,0},{5,1},{6,2},{7,3},{8,12},{9,13},{10,... | collective-permute-start | bytes 393224 | tf_op jit(solution)/shard_map/ppermute | solution.py:27
  30.2 8.4 %copy-start.2 = (f32[4096]{0:T(1024)S(1)}, f32[4096]{0:T(1024)}, u32[]{:S(2)}) copy-start(f32[4096]{0:T(1024)} %param.17) | copy-start | bytes 49156
  30.2 8.1 %collective-permute-start.8 = (bf16[16,4096]{1,0:T(8,128)(2,1)S(1)}, bf16[16,4096]{1,0:T(8,128)(2,1)S(1)}, u32[]{:S(2)}, u32[]{:S(2)}) collective-permute-start(bf16[16,4096]{1,0:T(8,128)(2,1)S(1)} %fusion.43), channel_id=1, source_target_pairs={{0,8},{1,9},{2,10},{3,11},{4,12},{5,13},{6,14},{7,15},{8,0},{9,1},... | collective-permute-start | bytes 393224 | tf_op jit(solution)/shard_map/ppermute | solution.py:27
  38.4 5.7 %copy-start.1 = (bf16[82,4096]{1,0:T(8,128)(2,1)S(1)}, bf16[82,4096]{1,0:T(8,128)(2,1)}, u32[]{:S(2)}) copy-start(bf16[82,4096]{1,0:T(8,128)(2,1)} %param.14) | copy-start | bytes 2015236
  38.5 5.7 %copy-start.5 = (f32[82]{0:T(128)S(1)}, f32[82]{0:T(128)}, u32[]{:S(2)}) copy-start(f32[82]{0:T(128)} %param.15) | copy-start | bytes 988
  38.7 5.4 %collective-permute-start.9 = (bf16[16,4096]{1,0:T(8,128)(2,1)S(1)}, bf16[16,4096]{1,0:T(8,128)(2,1)S(1)}, u32[]{:S(2)}, u32[]{:S(2)}) collective-permute-start(bf16[16,4096]{1,0:T(8,128)(2,1)S(1)} %subtract_convert_fusion.1), channel_id=1, source_target_pairs={{0,2},{1,3},{2,0},{3,1},{4,6},{5,7},{6,4},{7,5},{8,10},{9,11},{10,... | collective-permute-start | bytes 393224 | tf_op jit(solution)/shard_map/ppermute | solution.py:27
  41.1 3.0 %collective-permute-start.11 = (bf16[32,4096]{1,0:T(8,128)(2,1)S(1)}, bf16[32,4096]{1,0:T(8,128)(2,1)S(1)}, u32[]{:S(2)}, u32[]{:S(2)}) collective-permute-start(bf16[32,4096]{1,0:T(8,128)(2,1)S(1)} %pad_maximum_fusion.4), channel_id=1, source_target_pairs={{0,1},{1,0},{2,3},{3,2},{4,5},{5,4},{6,7},{7,6},{8,9},{9,8},{10,11... | collective-permute-start | bytes 786440 | tf_op jit(solution)/shard_map/ppermute | solution.py:27
  44.1 1.6 %collective-permute-start.10 = (bf16[32,4096]{1,0:T(8,128)(2,1)S(1)}, bf16[32,4096]{1,0:T(8,128)(2,1)S(1)}, u32[]{:S(2)}, u32[]{:S(2)}) collective-permute-start(bf16[32,4096]{1,0:T(8,128)(2,1)S(1)} %pad_maximum_fusion.5), channel_id=1, source_target_pairs={{0,1},{1,0},{2,3},{3,2},{4,5},{5,4},{6,7},{7,6},{8,9},{9,8},{10,11... | collective-permute-start | bytes 786440 | tf_op jit(solution)/shard_map/ppermute | solution.py:27
  44.2 0.7 %copy-start.12 = (bf16[32,4096]{1,0:T(8,128)(2,1)}, bf16[32,4096]{1,0:T(8,128)(2,1)S(1)}, u32[]{:S(2)}) copy-start(bf16[32,4096]{1,0:T(8,128)(2,1)S(1)} %collective-permute-done.11) | copy-start | bytes 786436
  46.1 1.4 %copy-start.6 = (f32[82]{0:T(128)S(1)}, f32[82]{0:T(128)}, u32[]{:S(2)}) copy-start(f32[82]{0:T(128)} %param.22) | copy-start | bytes 988
  46.1 1.4 %copy-start.7 = (f32[82]{0:T(128)S(1)}, f32[82]{0:T(128)}, u32[]{:S(2)}) copy-start(f32[82]{0:T(128)} %param.23) | copy-start | bytes 988
  46.1 1.9 %copy-start.3 = (f32[4096]{0:T(1024)S(1)}, f32[4096]{0:T(1024)}, u32[]{:S(2)}) copy-start(f32[4096]{0:T(1024)} %param.24) | copy-start | bytes 49156
  46.1 1.9 %copy-start.4 = (f32[4096]{0:T(1024)S(1)}, f32[4096]{0:T(1024)}, u32[]{:S(2)}) copy-start(f32[4096]{0:T(1024)} %param.25) | copy-start | bytes 49156
  46.1 2.5 %copy-start.8 = (f32[82,4096]{1,0:T(8,128)S(1)}, f32[82,4096]{1,0:T(8,128)}, u32[]{:S(2)}) copy-start(f32[82,4096]{1,0:T(8,128)} %param.20) | copy-start | bytes 4030468
  46.1 2.5 %copy-start.9 = (f32[82,4096]{1,0:T(8,128)S(1)}, f32[82,4096]{1,0:T(8,128)}, u32[]{:S(2)}) copy-start(f32[82,4096]{1,0:T(8,128)} %param.21) | copy-start | bytes 4030468
  48.6 3.3 %copy-start.10 = (f32[82,4096]{1,0:T(8,128)S(1)}, f32[82,4096]{1,0:T(8,128)}, u32[]{:S(2)}) copy-start(f32[82,4096]{1,0:T(8,128)} %param.18) | copy-start | bytes 4030468
  48.6 3.3 %copy-start.11 = (f32[82,4096]{1,0:T(8,128)S(1)}, f32[82,4096]{1,0:T(8,128)}, u32[]{:S(2)}) copy-start(f32[82,4096]{1,0:T(8,128)} %param.19) | copy-start | bytes 4030468
  48.7 3.3 %copy-start.13 = (bf16[32,4096]{1,0:T(8,128)(2,1)S(1)}, bf16[32,4096]{1,0:T(8,128)(2,1)}, u32[]{:S(2)}) copy-start(bf16[32,4096]{1,0:T(8,128)(2,1)} %copy-done.12) | copy-start | bytes 786436

commit v3 on v0

v3 whole, which is shorter than its diff:
```python
import functools

import jax
import jax.numpy as jnp
from jax import lax
from jax.experimental import pallas as pl
from jax.experimental.pallas import tpu as pltpu
from jax.sharding import PartitionSpec as P

STEP = 100


sharpness = 4.0
sparsity_coef = 0.3
first_decay = 0.9
second_decay = 0.999
learn_rate = 0.001
epsilon = 1e-08

f32 = jnp.float32
bf16 = jnp.bfloat16


def adam_update(param, grad, first, second):
    first_new = first_decay * first + (1.0 - first_decay) * grad
    second_new = second_decay * second + (1.0 - second_decay) * grad * grad
    first_corr = 1.0 - first_decay**STEP
    second_corr = 1.0 - second_decay**STEP
    square = second_new * (1.0 / second_corr)
    root = square * lax.rsqrt(square)
    change = (learn_rate / first_corr) * first_new / (root + epsilon)
    return (param.astype(f32) - change, first_new, second_new)


def softplus(x):
    return jnp.maximum(x, 0.0) + jnp.log1p(jnp.exp(-jnp.abs(x)))


def nt_dot(a, b):
    return lax.dot_general(a, b, (((1,), (1,)), ((), ())), preferred_element_type=f32)


def turn(vector):
    side = max(vector.shape)
    square = (side, side)
    diagonal = lax.broadcasted_iota(jnp.int32, square, 0) == lax.broadcasted_iota(jnp.int32, square, 1)
    axis = 1 if vector.shape[0] == 1 else 0
    return jnp.sum(jnp.where(diagonal, jnp.broadcast_to(vector, square), 0.0), axis=axis, keepdims=True)


def swap(x, bit, devices):
    return lax.ppermute(x, "dict", [(i, i ^ bit) for i in range(devices)])


def in_vmem(array):
    return pltpu.with_memory_space_constraint(array, pltpu.VMEM)


def in_hbm(array):
    return pltpu.with_memory_space_constraint(array, pltpu.HBM)


VMEM_SPEC = pl.BlockSpec(memory_space=pltpu.VMEM)
ANY_SPEC = pl.BlockSpec(memory_space=pl.ANY)


def load_kernel(*refs):
    count = len(refs) // 2
    copies = [pltpu.make_async_copy(refs[i], refs[count + i], refs[-1].at[i]) for i in range(count)]
    for copy in copies:
        copy.start()
    for copy in copies:
        copy.wait()


def load(*arrays):
    return pl.pallas_call(
        load_kernel,
        in_specs=[ANY_SPEC] * len(arrays),
        out_specs=[VMEM_SPEC] * len(arrays),
        out_shape=[pltpu.VMEM(array.shape, array.dtype) for array in arrays],
        scratch_shapes=[pltpu.SemaphoreType.DMA((len(arrays),))],
        compiler_params=pltpu.CompilerParams(vmem_limit_bytes=2**20),
        cost_estimate=pl.CostEstimate(
            flops=0, bytes_accessed=2 * sum(array.size * array.dtype.itemsize for array in arrays), transcendentals=0
        ),
    )(*map(in_hbm, arrays))


def forward_kernel(
    tokens_ref, encoder_ref, mate_encoder_ref, bias_ref, mate_bias_ref, decoder_ref, mate_decoder_ref, keep_ref, send_ref
):
    tokens = tokens_ref[...]

    def act(weight_ref, row_ref):
        pre = nt_dot(tokens, weight_ref[...]) + row_ref[...]
        return (softplus(sharpness * pre) / sharpness).astype(bf16)

    own = act(encoder_ref, bias_ref)
    mate = act(mate_encoder_ref, mate_bias_ref)
    half = keep_ref.shape[0]
    width = 1024
    for start in range(0, keep_ref.shape[1], width):
        columns = pl.ds(start, width)
        part = jnp.dot(own, decoder_ref[:, columns], preferred_element_type=f32) + jnp.dot(
            mate, mate_decoder_ref[:, columns], preferred_element_type=f32
        )
        keep_ref[:, columns] = part[:half]
        send_ref[:, columns] = part[half:].astype(bf16)


def forward(tokens, encoder, mate_encoder, bias, mate_bias, decoder, mate_decoder):
    half, features = tokens.shape[0] // 2, tokens.shape[1]
    latents = encoder.shape[0]
    return pl.pallas_call(
        forward_kernel,
        in_specs=[VMEM_SPEC] * 7,
        out_specs=[VMEM_SPEC] * 2,
        out_shape=[pltpu.VMEM((half, features), f32), pltpu.VMEM((half, features), bf16)],
        compiler_params=pltpu.CompilerParams(vmem_limit_bytes=16 * 2**20),
        cost_estimate=pl.CostEstimate(
            flops=16 * half * latents * features, bytes_accessed=8 * latents * features, transcendentals=8 * half * latents
        ),
    )(*map(in_vmem, (tokens, encoder, mate_encoder, bias, mate_bias, decoder, mate_decoder)))


def prepare_kernel(
    tokens_ref,
    mate_tokens_ref,
    encoder_ref,
    bias_ref,
    decoder_ref,
    encoder_first_ref,
    encoder_second_ref,
    decoder_first_ref,
    decoder_second_ref,
    gathered_ref,
    slope_ref,
    act_ref,
    floor_ref,
    pull_ref,
    encoder_first_out,
    encoder_second_out,
    decoder_first_out,
    decoder_second_out,
    sems,
):
    moves = [
        (encoder_first_ref, encoder_first_out),
        (encoder_second_ref, encoder_second_out),
        (decoder_first_ref, decoder_first_out),
        (decoder_second_ref, decoder_second_out),
    ]
    pieces = sems.shape[1]
    width = encoder_first_ref.shape[1] // pieces
    copies = [
        pltpu.make_async_copy(
            source.at[:, pl.ds(piece * width, width)], target.at[:, pl.ds(piece * width, width)], sems.at[which, piece]
        )
        for which, (source, target) in enumerate(moves)
        for piece in range(pieces)
    ]
    for copy in copies:
        copy.start()
    tokens = jnp.concatenate([tokens_ref[...], mate_tokens_ref[...]], axis=0)
    gathered_ref[...] = tokens
    pre = nt_dot(encoder_ref[...], tokens) + turn(bias_ref[...])
    act = softplus(sharpness * pre) / sharpness
    slope_ref[...] = jax.nn.sigmoid(sharpness * pre)
    act_ref[...] = act.astype(bf16)
    decoder = decoder_ref[...].astype(f32)
    norms = jnp.sqrt(jnp.sum(decoder * decoder, axis=1, keepdims=True) + 1e-06)
    floor_ref[...] = sparsity_coef * norms
    pull_ref[...] = sparsity_coef * jnp.sum(act, axis=1, keepdims=True) / norms
    for copy in copies:
        copy.wait()


def prepare(tokens, mate_tokens, encoder, bias, decoder, *moments):
    latents, features = encoder.shape
    count = 2 * tokens.shape[0]
    return pl.pallas_call(
        prepare_kernel,
        in_specs=[VMEM_SPEC] * 5 + [ANY_SPEC] * 4,
        out_specs=[VMEM_SPEC] * 9,
        out_shape=[
            pltpu.VMEM((count, features), bf16),
            pltpu.VMEM((latents, count), f32),
            pltpu.VMEM((latents, count), bf16),
            pltpu.VMEM((latents, 1), f32),
            pltpu.VMEM((latents, 1), f32),
        ]
        + [pltpu.VMEM((latents, features), f32)] * 4,
        scratch_shapes=[pltpu.SemaphoreType.DMA((4, 2))],
        compiler_params=pltpu.CompilerParams(vmem_limit_bytes=16 * 2**20),
        cost_estimate=pl.CostEstimate(
            flops=2 * count * latents * features, bytes_accessed=20 * latents * features, transcendentals=3 * count * latents
        ),
    )(*map(in_vmem, (tokens, mate_tokens, encoder, bias, decoder)), *map(in_hbm, moments))


def update_kernel(
    own,
    errors_ref,
    tokens_ref,
    slope_ref,
    act_ref,
    floor_ref,
    pull_ref,
    encoder_first_ref,
    encoder_second_ref,
    decoder_first_ref,
    decoder_second_ref,
    encoder_ref,
    decoder_ref,
    encoder_bias_ref,
    latent_first_ref,
    latent_second_ref,
    decoder_bias_ref,
    feature_first_ref,
    feature_second_ref,
    *refs,
):
    outs, slots, (pre_ref, sems) = refs[:12], refs[12:24], refs[24:]
    features = encoder_ref.shape[1]
    blocks = sems.shape[1]
    width = features // blocks

    def block_copy(which, block):
        columns = pl.ds(pl.multiple_of(block * width, width), width)
        return pltpu.make_async_copy(slots[which].at[:, columns], outs[which].at[:, columns], sems.at[which, block])

    def whole_copy(which):
        return pltpu.make_async_copy(slots[which], outs[which], sems.at[which, 0])

    def decoder_block(block, carry):
        columns = pl.ds(pl.multiple_of(block * width, width), width)
        weight = decoder_ref[:, columns].astype(f32)
        grad = jnp.dot(act_ref[...], errors_ref[:, columns], preferred_element_type=f32) + pull_ref[...] * weight
        new, slots[4][:, columns], slots[5][:, columns] = adam_update(
            weight, grad, decoder_first_ref[:, columns], decoder_second_ref[:, columns]
        )
        slots[1][:, columns] = new.astype(bf16)
        for which in (1, 4, 5):
            block_copy(which, block).start()
        return carry

    lax.fori_loop(0, blocks, decoder_block, 0)

    grad = (nt_dot(decoder_ref[...], errors_ref[...]) + floor_ref[...]) * slope_ref[...]
    pre_ref[...] = grad.astype(bf16)
    total = turn(jnp.sum(grad, axis=1, keepdims=True))
    slots[6][...], slots[7][...], slots[8][...] = adam_update(
        encoder_bias_ref[...], total, latent_first_ref[...], latent_second_ref[...]
    )
    rows = errors_ref[...].astype(f32)
    while rows.shape[0] > own:
        half = rows.shape[0] // 2
        rows = rows[:half] + rows[half:]
    total = rows[0:1]
    for row in range(1, own):
        total = total + rows[row : row + 1]
    slots[9][...], slots[10][...], slots[11][...] = adam_update(
        decoder_bias_ref[...], total, feature_first_ref[...], feature_second_ref[...]
    )
    for which in range(6, 12):
        whole_copy(which).start()

    def encoder_block(block, carry):
        columns = pl.ds(pl.multiple_of(block * width, width), width)
        grad = jnp.dot(pre_ref[...], tokens_ref[:, columns], preferred_element_type=f32)
        new, slots[2][:, columns], slots[3][:, columns] = adam_update(
            encoder_ref[:, columns], grad, encoder_first_ref[:, columns], encoder_second_ref[:, columns]
        )
        slots[0][:, columns] = new.astype(bf16)
        for which in (0, 2, 3):
            block_copy(which, block).start()
        return carry

    lax.fori_loop(0, blocks, encoder_block, 0)
    for block in range(blocks):
        for which in range(6):
            block_copy(which, block).wait()
    for which in range(6, 12):
        whole_copy(which).wait()


def update(own, errors, prepared, encoder, decoder, *short):
    latents, features = encoder.shape
    count = errors.shape[0]
    shapes = [((latents, features), bf16)] * 2 + [((latents, features), f32)] * 4
    shapes += [((1, latents), f32)] * 3 + [((1, features), f32)] * 3
    return pl.pallas_call(
        functools.partial(update_kernel, own),
        in_specs=[VMEM_SPEC] * 18,
        out_specs=[ANY_SPEC] * 12,
        out_shape=[jax.ShapeDtypeStruct(*shape) for shape in shapes],
        scratch_shapes=[pltpu.VMEM(*shape) for shape in shapes]
        + [pltpu.VMEM((latents, count), bf16), pltpu.SemaphoreType.DMA((12, 8))],
        compiler_params=pltpu.CompilerParams(vmem_limit_bytes=24 * 2**20),
        cost_estimate=pl.CostEstimate(
            flops=6 * count * latents * features,
            bytes_accessed=40 * latents * features,
            transcendentals=4 * latents * features,
        ),
    )(*map(in_vmem, (errors, *prepared, encoder, decoder, *short)))


def local(
    devices,
    tokens,
    encoder_weight,
    encoder_bias,
    decoder_weight,
    decoder_bias,
    encoder_first,
    encoder_second,
    decoder_first,
    decoder_second,
    latent_first,
    latent_second,
    feature_first,
    feature_second,
):
    bits = [1 << b for b in reversed(range(1, devices.bit_length() - 1))]
    own = tokens.shape[0]
    row = lambda array: array.reshape(1, -1)
    encoder_bias, latent_first, latent_second, decoder_bias, feature_first, feature_second = map(
        row, (encoder_bias, latent_first, latent_second, decoder_bias, feature_first, feature_second)
    )
    far = swap(tokens, bits[0], devices)
    column, encoder, decoder, bias = load(tokens, encoder_weight, decoder_weight, encoder_bias)
    column = lax.optimization_barrier(jnp.concatenate([column, far], axis=0))
    mate_encoder = swap(encoder, 1, devices)
    mate_bias = swap(bias, 1, devices)
    mate_decoder = swap(decoder, 1, devices)
    for bit in bits[1:]:
        column = lax.optimization_barrier(jnp.concatenate([column, swap(column, bit, devices)], axis=0))
    part, send = forward(column, encoder, mate_encoder, bias, mate_bias, decoder, mate_decoder)
    part = part + swap(send, bits[-1], devices).astype(f32)
    mate_column = swap(column, 1, devices)
    half = part.shape[0]
    for level in reversed(range(len(bits) - 1)):
        part = lax.reduce_precision(part, 8, 7)
        sent = part.astype(bf16)
        if level == 0:
            sent, mate_column = lax.optimization_barrier((sent, mate_column))
        other = swap(sent, bits[level], devices)
        if level == 0:
            prepared = prepare(
                column, mate_column, encoder, bias, decoder, encoder_first, encoder_second, decoder_first, decoder_second
            )
            other, prepared = lax.optimization_barrier((other, prepared))
        size = own << level
        pieces = [other[start ^ size : (start ^ size) + size] for start in range(0, half, size)]
        part = part + jnp.concatenate(pieces, axis=0).astype(f32)
    errors = (part + decoder_bias - column[:half].astype(f32)).astype(bf16)
    errors = lax.optimization_barrier(jnp.concatenate([errors, swap(errors, bits[-1], devices)], axis=0))
    errors = jnp.concatenate([errors, swap(errors, 1, devices)], axis=0)
    out = update(
        own,
        errors,
        prepared,
        encoder,
        decoder,
        bias,
        latent_first,
        latent_second,
        decoder_bias,
        feature_first,
        feature_second,
    )
    new_encoder, new_decoder, enc_first, enc_second, dec_first, dec_second = out[:6]
    lat_new, lat_first, lat_second, feat_new, feat_first, feat_second = (array.reshape(-1) for array in out[6:])
    return (
        new_encoder,
        lat_new,
        new_decoder,
        feat_new,
        enc_first,
        enc_second,
        dec_first,
        dec_second,
        lat_first,
        lat_second,
        feat_first,
        feat_second,
    )


def solution(mesh):
    devices = mesh.shape["dict"]
    in_specs = (
        P(("groups", "dict"), None),
        P(("groups", "dict"), None),
        P(("groups", "dict")),
        P(("groups", "dict"), None),
        P("groups"),
        P(("groups", "dict"), None),
        P(("groups", "dict"), None),
        P(("groups", "dict"), None),
        P(("groups", "dict"), None),
        P(("groups", "dict")),
        P(("groups", "dict")),
        P("groups"),
        P("groups"),
    )
    out_specs = (
        P(("groups", "dict"), None),
        P(("groups", "dict")),
        P(("groups", "dict"), None),
        P("groups"),
        P(("groups", "dict"), None),
        P(("groups", "dict"), None),
        P(("groups", "dict"), None),
        P(("groups", "dict"), None),
        P(("groups", "dict")),
        P(("groups", "dict")),
        P("groups"),
        P("groups"),
    )

    def step(*args):
        return local(devices, *args)

    return jax.shard_map(step, mesh=mesh, in_specs=in_specs, out_specs=out_specs, check_vma=False)
```

time: 222 us -> 48.7 us (0.22)
  blocking collectives: 104 us -> 0 us
  waiting for transfers between devices: 89.2 us -> 19.3 us
  starting transfers between devices: 0.04 us -> 16.3 us
  between operations: 14.9 us -> 0.83 us
  Pallas kernels: 0 us -> 11.6 us
  matrix products: 10.5 us -> 0 us
    unnamed x2 -> x0, waiting for transfers between devices: 89.2 us -> none
    psum x1 -> x0, blocking collectives: 57.8 us -> none  [local(): lax.psum(jnp.sum(own_errors, axis=0, dtype=jnp.float32), 'dict')]
    all_gather x2 -> x0, blocking collectives: 46 us -> none  [the longest x1 24.9 us: local(): gathered = lax.all_gather(tokens, 'dict', axis=0, tiled=True)]
    ppermute x0 -> x12, waiting for transfers between devices: none -> 19.3 us  [swap(): return lax.ppermute(x, 'dict', [(i, i ^ bit) for i in range(devices)])]
    ppermute x0 -> x12, starting transfers between devices: none -> 16.3 us  [swap(): return lax.ppermute(x, 'dict', [(i, i ^ bit) for i in range(devices)])]
    pallas_call x0 -> x4, Pallas kernels: none -> 11.6 us  [the longest x1 6.29 us: update(): pl.pallas_call(functools.partial(update_kernel, own), in_specs=[VMEM_SPEC...]
    dot_general x5 -> x0, matrix products: 10.5 us -> none  [the longest x1 5.03 us: local(): jnp.einsum('tl,td->ld', pre_low, gathered, preferred_element_type=jnp.flo...]
  transfers between devices with their start and end apart: 1 -> 12, of which waited for: 1 -> 8; matrix products, arithmetic and copies ran while one was open for 0% -> 0% of each run, Pallas kernels for 0% -> 9%
where the time goes in v3:
time: 48.7 us; the launch traced here: 48.5 us
  waiting for transfers between devices  19.3 us (40%)
  starting transfers between devices  16.3 us (33%)
  Pallas kernels  11.6 us (24%)
  between operations  0.83 us (2%)
    ppermute x12, waiting for transfers between devices, swap(): return lax.ppermute(x, 'dict', [(i, i ^ bit) for i in range(devices)])  19.3 us
    ppermute x12, starting transfers between devices, swap(): return lax.ppermute(x, 'dict', [(i, i ^ bit) for i in range(devices)])  16.3 us
    pallas_call x1, Pallas kernels, update(): pl.pallas_call(functools.partial(update_kernel, own), in_specs=[VMEM_SPEC...  6.29 us
    pallas_call x1, Pallas kernels, prepare(): pl.pallas_call(prepare_kernel, in_specs=[VMEM_SPEC] * 5 + [ANY_SPEC] * 4,...  2.94 us
    pallas_call x1, Pallas kernels, load(): pl.pallas_call(load_kernel, in_specs=[ANY_SPEC] * len(arrays), out_specs=...  1.38 us
    pallas_call x1, Pallas kernels, forward(): pl.pallas_call(forward_kernel, in_specs=[VMEM_SPEC] * 7, out_specs=[VMEM_...  1 us
  transfers between devices with their start and end apart: 12, of which 8 were waited for; matrix products, arithmetic and copies ran while one was open for 0% of the time, Pallas kernels for 9%

profile of v3, /device:TPU:0, one launch (start us, length us, event | category | flops | bytes accessed | tf_op | source)
XLA Modules:
  0.0 48.5 jit_solution(4335569444938401324)
XLA Ops:
  0.6 4.1 %collective-permute-start = (bf16[4,4096]{1,0:T(4,128)(2,1)}, bf16[4,4096]{1,0:T(4,128)(2,1)S(1)}, u32[]{:S(2)}, u32[]{:S(2)}) collective-permute-start(bf16[4,4096]{1,0:T(4,128)(2,1)} %refs_0_.1), channel_id=1, source_target_pairs={{0,8},{1,9},{2,10},{3,11},{4,12},{5,13},{6,14},{7,15},{8,0},{9,1},... | collective-permute-start | bytes 98312 | tf_op jit(solution)/shard_map/ppermute | solution.py:52
  4.7 1.4 %shard_map.220 = (bf16[4,4096]{1,0:T(4,128)(2,1)S(1)}, bf16[82,4096]{1,0:T(8,128)(2,1)S(1)}, bf16[82,4096]{1,0:T(8,128)(2,1)S(1)}, f32[1,82]{1,0:T(1,128)S(1)}) custom-call(bf16[4,4096]{1,0:T(4,128)(2,1)} %refs_0_.1, bf16[82,4096]{1,0:T(8,128)(2,1)} %refs_1_.1, bf16[82,4096]{1,0:T(8,128)(2,1)} %refs_2_.1, f32[1,82]{1,0:T(1,128)} %bitcast.17), custom_call_target="tpu_custom_call" | custom-call | bytes 2753168 | tf_op jit(solution)/shard_map/pallas_call | solution.py:77
  6.1 1.1 %collective-permute-done = bf16[4,4096]{1,0:T(4,128)(2,1)S(1)} collective-permute-done((bf16[4,4096]{1,0:T(4,128)(2,1)}, bf16[4,4096]{1,0:T(4,128)(2,1)S(1)}, u32[]{:S(2)}, u32[]{:S(2)}) %collective-permute-start) | collective-permute-done | bytes 32800 | tf_op jit(solution)/shard_map/ppermute | solution.py:52
  7.2 1.6 %collective-permute-start.1 = (bf16[8,4096]{1,0:T(8,128)(2,1)S(1)}, bf16[8,4096]{1,0:T(8,128)(2,1)S(1)}, u32[]{:S(2)}, u32[]{:S(2)}) collective-permute-start(bf16[8,4096]{1,0:T(8,128)(2,1)S(1)} %pad_maximum_fusion.4), channel_id=1, source_target_pairs={{0,4},{1,5},{2,6},{3,7},{4,0},{5,1},{6,2},{7,3},{8,12},{9,13},{10,... | collective-permute-start | bytes 196616 | tf_op jit(solution)/shard_map/ppermute | solution.py:52
  8.9 0.0 collective-permute-start.3
  8.9 0.5 %collective-permute-start.5 = (bf16[82,4096]{1,0:T(8,128)(2,1)S(1)}, bf16[82,4096]{1,0:T(8,128)(2,1)S(1)}, u32[]{:S(2)}, u32[]{:S(2)}) collective-permute-start(bf16[82,4096]{1,0:T(8,128)(2,1)S(1)} %get-tuple-element.54.decoder_ref), channel_id=1, source_target_pairs={{0,1},{1,0},{2,3},{3,2},{4,5},{5,4},{6,7},{7,6},{8,9},{9,8},{10,11... | collective-permute-start | bytes 2015240 | tf_op jit(solution)/shard_map/ppermute | solution.py:52
  9.4 2.2 %collective-permute-done.1 = bf16[8,4096]{1,0:T(8,128)(2,1)S(1)} collective-permute-done((bf16[8,4096]{1,0:T(8,128)(2,1)S(1)}, bf16[8,4096]{1,0:T(8,128)(2,1)S(1)}, u32[]{:S(2)}, u32[]{:S(2)}) %collective-permute-start.1) | collective-permute-done | bytes 65568 | tf_op jit(solution)/shard_map/ppermute | solution.py:52
  11.6 1.8 %collective-permute-start.2 = (bf16[16,4096]{1,0:T(8,128)(2,1)S(1)}, bf16[16,4096]{1,0:T(8,128)(2,1)S(1)}, u32[]{:S(2)}, u32[]{:S(2)}) collective-permute-start(bf16[16,4096]{1,0:T(8,128)(2,1)S(1)} %pad_maximum_fusion.3), channel_id=1, source_target_pairs={{0,2},{1,3},{2,0},{3,1},{4,6},{5,7},{6,4},{7,5},{8,10},{9,11},{10,... | collective-permute-start | bytes 393224 | tf_op jit(solution)/shard_map/ppermute | solution.py:52
  13.4 0.0 collective-permute-start.4
  13.4 3.2 %collective-permute-done.2 = bf16[16,4096]{1,0:T(8,128)(2,1)S(1)} collective-permute-done((bf16[16,4096]{1,0:T(8,128)(2,1)S(1)}, bf16[16,4096]{1,0:T(8,128)(2,1)S(1)}, u32[]{:S(2)}, u32[]{:S(2)}) %collective-permute-start.2) | collective-permute-done | bytes 131104 | tf_op jit(solution)/shard_map/ppermute | solution.py:52
  16.6 0.0 collective-permute-done.4.mate_bias_ref
  16.7 0.0 collective-permute-done.5.mate_decoder_ref
  16.7 1.0 %shard_map.221 = (f32[16,4096]{1,0:T(8,128)S(1)}, bf16[16,4096]{1,0:T(8,128)(2,1)S(1)}) custom-call(bf16[32,4096]{1,0:T(8,128)(2,1)S(1)} %pad_maximum_fusion.1.tokens_ref, bf16[82,4096]{1,0:T(8,128)(2,1)S(1)} %get-tuple-element.52.encoder_ref, bf16[82,4096]{1,0:T(8,128)(2,1)S(1)} %collective-permute-done.3.mate_encoder_ref, ...), custom_call_target="tpu_custom_call" | custom-call | flops 85983232 | bytes 2686976 | tf_op jit(solution)/shard_map/pallas_call | solution.py:115
  17.7 1.8 %collective-permute-start.6 = (bf16[16,4096]{1,0:T(8,128)(2,1)S(1)}, bf16[16,4096]{1,0:T(8,128)(2,1)S(1)}, u32[]{:S(2)}, u32[]{:S(2)}) collective-permute-start(bf16[16,4096]{1,0:T(8,128)(2,1)S(1)} %get-tuple-element.56), channel_id=1, source_target_pairs={{0,2},{1,3},{2,0},{3,1},{4,6},{5,7},{6,4},{7,5},{8,10},{9,11},{10,... | collective-permute-start | bytes 393224 | tf_op jit(solution)/shard_map/ppermute | solution.py:52
  19.5 3.2 %collective-permute-done.6 = bf16[16,4096]{1,0:T(8,128)(2,1)S(1)} collective-permute-done((bf16[16,4096]{1,0:T(8,128)(2,1)S(1)}, bf16[16,4096]{1,0:T(8,128)(2,1)S(1)}, u32[]{:S(2)}, u32[]{:S(2)}) %collective-permute-start.6) | collective-permute-done | bytes 131104 | tf_op jit(solution)/shard_map/ppermute | solution.py:52
  22.7 1.6 %collective-permute-start.7 = (bf16[16,4096]{1,0:T(8,128)(2,1)S(1)}, bf16[16,4096]{1,0:T(8,128)(2,1)S(1)}, u32[]{:S(2)}, u32[]{:S(2)}) collective-permute-start(bf16[16,4096]{1,0:T(8,128)(2,1)S(1)} %fusion), channel_id=1, source_target_pairs={{0,4},{1,5},{2,6},{3,7},{4,0},{5,1},{6,2},{7,3},{8,12},{9,13},{10,... | collective-permute-start | bytes 393224 | tf_op jit(solution)/shard_map/ppermute | solution.py:52
  24.4 3.4 %collective-permute-done.7 = bf16[16,4096]{1,0:T(8,128)(2,1)S(1)} collective-permute-done((bf16[16,4096]{1,0:T(8,128)(2,1)S(1)}, bf16[16,4096]{1,0:T(8,128)(2,1)S(1)}, u32[]{:S(2)}, u32[]{:S(2)}) %collective-permute-start.7) | collective-permute-done | bytes 131104 | tf_op jit(solution)/shard_map/ppermute | solution.py:52
  27.8 0.1 fusion.1
  27.9 0.0 copy-start
  27.9 3.0 %collective-permute-start.9 = (bf16[16,4096]{1,0:T(8,128)(2,1)S(1)}, bf16[16,4096]{1,0:T(8,128)(2,1)S(1)}, u32[]{:S(2)}, u32[]{:S(2)}) collective-permute-start(bf16[16,4096]{1,0:T(8,128)(2,1)S(1)} %fusion.1), channel_id=1, source_target_pairs={{0,8},{1,9},{2,10},{3,11},{4,12},{5,13},{6,14},{7,15},{8,0},{9,1},... | collective-permute-start | bytes 393224 | tf_op jit(solution)/shard_map/ppermute | solution.py:52
  30.9 2.9 %shard_map.222 = (bf16[64,4096]{1,0:T(8,128)(2,1)S(1)}, f32[82,64]{1,0:T(8,128)S(1)}, bf16[82,64]{1,0:T(8,128)(2,1)S(1)}, f32[82,1]{1,0:T(8,128)S(1)}, f32[82,1]...) custom-call(bf16[32,4096]{1,0:T(8,128)(2,1)S(1)} %pad_maximum_fusion, ...), custom_call_target="tpu_custom_call" | custom-call | flops 42991616 | bytes 6717440 | tf_op jit(solution)/shard_map/pallas_call | solution.py:182
  33.8 0.0 copy-start.1
  33.8 0.0 copy-start.2
  33.9 0.0 copy-start.3
  33.9 0.0 copy-start.4
  33.9 1.4 %collective-permute-done.9 = bf16[16,4096]{1,0:T(8,128)(2,1)S(1)} collective-permute-done((bf16[16,4096]{1,0:T(8,128)(2,1)S(1)}, bf16[16,4096]{1,0:T(8,128)(2,1)S(1)}, u32[]{:S(2)}, u32[]{:S(2)}) %collective-permute-start.9) | collective-permute-done | bytes 131104 | tf_op jit(solution)/shard_map/ppermute | solution.py:52
  35.3 0.2 subtract_convert_fusion
  35.5 1.8 %collective-permute-start.10 = (bf16[16,4096]{1,0:T(8,128)(2,1)S(1)}, bf16[16,4096]{1,0:T(8,128)(2,1)S(1)}, u32[]{:S(2)}, u32[]{:S(2)}) collective-permute-start(bf16[16,4096]{1,0:T(8,128)(2,1)S(1)} %subtract_convert_fusion), channel_id=1, source_target_pairs={{0,2},{1,3},{2,0},{3,1},{4,6},{5,7},{6,4},{7,5},{8,10},{9,11},{10,... | collective-permute-start | bytes 393224 | tf_op jit(solution)/shard_map/ppermute | solution.py:52
  37.2 3.3 %collective-permute-done.10 = bf16[16,4096]{1,0:T(8,128)(2,1)S(1)} collective-permute-done((bf16[16,4096]{1,0:T(8,128)(2,1)S(1)}, bf16[16,4096]{1,0:T(8,128)(2,1)S(1)}, u32[]{:S(2)}, u32[]{:S(2)}) %collective-permute-start.10) | collective-permute-done | bytes 131104 | tf_op jit(solution)/shard_map/ppermute | solution.py:52
  40.5 0.1 collective-permute-start.11
  40.6 1.5 %collective-permute-done.11 = bf16[32,4096]{1,0:T(8,128)(2,1)S(1)} collective-permute-done((bf16[32,4096]{1,0:T(8,128)(2,1)S(1)}, bf16[32,4096]{1,0:T(8,128)(2,1)S(1)}, u32[]{:S(2)}, u32[]{:S(2)}) %collective-permute-start.11) | collective-permute-done | bytes 262176 | tf_op jit(solution)/shard_map/ppermute | solution.py:52
  42.2 6.3 %shard_map.223 = (bf16[82,4096]{1,0:T(8,128)(2,1)}, bf16[82,4096]{1,0:T(8,128)(2,1)}, f32[82,4096]{1,0:T(8,128)}, f32[82,4096]{1,0:T(8,128)}, f32[82,4096]{1,0:T...) custom-call(bf16[64,4096]{1,0:T(8,128)(2,1)S(1)} %pad_maximum_fusion, ...), custom_call_target="tpu_custom_call" | custom-call | flops 128974848 | bytes 13434880 | tf_op jit(solution)/shard_map/pallas_call | solution.py:293
  (16 shorter events, 0.2 us)
Async XLA Ops:
  0.6 6.6 %collective-permute-start = (bf16[4,4096]{1,0:T(4,128)(2,1)}, bf16[4,4096]{1,0:T(4,128)(2,1)S(1)}, u32[]{:S(2)}, u32[]{:S(2)}) collective-permute-start(bf16[4,4096]{1,0:T(4,128)(2,1)} %refs_0_.1), channel_id=1, source_target_pairs={{0,8},{1,9},{2,10},{3,11},{4,12},{5,13},{6,14},{7,15},{8,0},{9,1},... | collective-permute-start | bytes 98312 | tf_op jit(solution)/shard_map/ppermute | solution.py:52
  7.2 4.3 %collective-permute-start.1 = (bf16[8,4096]{1,0:T(8,128)(2,1)S(1)}, bf16[8,4096]{1,0:T(8,128)(2,1)S(1)}, u32[]{:S(2)}, u32[]{:S(2)}) collective-permute-start(bf16[8,4096]{1,0:T(8,128)(2,1)S(1)} %pad_maximum_fusion.4), channel_id=1, source_target_pairs={{0,4},{1,5},{2,6},{3,7},{4,0},{5,1},{6,2},{7,3},{8,12},{9,13},{10,... | collective-permute-start | bytes 196616 | tf_op jit(solution)/shard_map/ppermute | solution.py:52
  8.9 7.8 %collective-permute-start.3 = (bf16[82,4096]{1,0:T(8,128)(2,1)S(1)}, bf16[82,4096]{1,0:T(8,128)(2,1)S(1)}, u32[]{:S(2)}, u32[]{:S(2)}) collective-permute-start(bf16[82,4096]{1,0:T(8,128)(2,1)S(1)} %get-tuple-element.52.encoder_ref), channel_id=1, source_target_pairs={{0,1},{1,0},{2,3},{3,2},{4,5},{5,4},{6,7},{7,6},{8,9},{9,8},{10,11... | collective-permute-start | bytes 2015240 | tf_op jit(solution)/shard_map/ppermute | solution.py:52
  8.9 7.8 %collective-permute-start.5 = (bf16[82,4096]{1,0:T(8,128)(2,1)S(1)}, bf16[82,4096]{1,0:T(8,128)(2,1)S(1)}, u32[]{:S(2)}, u32[]{:S(2)}) collective-permute-start(bf16[82,4096]{1,0:T(8,128)(2,1)S(1)} %get-tuple-element.54.decoder_ref), channel_id=1, source_target_pairs={{0,1},{1,0},{2,3},{3,2},{4,5},{5,4},{6,7},{7,6},{8,9},{9,8},{10,11... | collective-permute-start | bytes 2015240 | tf_op jit(solution)/shard_map/ppermute | solution.py:52
  11.6 5.0 %collective-permute-start.2 = (bf16[16,4096]{1,0:T(8,128)(2,1)S(1)}, bf16[16,4096]{1,0:T(8,128)(2,1)S(1)}, u32[]{:S(2)}, u32[]{:S(2)}) collective-permute-start(bf16[16,4096]{1,0:T(8,128)(2,1)S(1)} %pad_maximum_fusion.3), channel_id=1, source_target_pairs={{0,2},{1,3},{2,0},{3,1},{4,6},{5,7},{6,4},{7,5},{8,10},{9,11},{10,... | collective-permute-start | bytes 393224 | tf_op jit(solution)/shard_map/ppermute | solution.py:52
  13.4 3.3 %collective-permute-start.4 = (f32[1,82]{1,0:T(1,128)S(1)}, f32[1,82]{1,0:T(1,128)S(1)}, u32[]{:S(2)}, u32[]{:S(2)}) collective-permute-start(f32[1,82]{1,0:T(1,128)S(1)} %get-tuple-element.53.bias_ref.encoder_bias_ref), channel_id=1, source_target_pairs={{0,1},{1,0},{2,3},{3,2},{4,5},{5,4},{6,7},{7,6},{8,9},{9,8},{10,11... | collective-permute-start | bytes 992 | tf_op jit(solution)/shard_map/ppermute | solution.py:52
  17.7 5.0 %collective-permute-start.6 = (bf16[16,4096]{1,0:T(8,128)(2,1)S(1)}, bf16[16,4096]{1,0:T(8,128)(2,1)S(1)}, u32[]{:S(2)}, u32[]{:S(2)}) collective-permute-start(bf16[16,4096]{1,0:T(8,128)(2,1)S(1)} %get-tuple-element.56), channel_id=1, source_target_pairs={{0,2},{1,3},{2,0},{3,1},{4,6},{5,7},{6,4},{7,5},{8,10},{9,11},{10,... | collective-permute-start | bytes 393224 | tf_op jit(solution)/shard_map/ppermute | solution.py:52
  22.7 5.0 %collective-permute-start.7 = (bf16[16,4096]{1,0:T(8,128)(2,1)S(1)}, bf16[16,4096]{1,0:T(8,128)(2,1)S(1)}, u32[]{:S(2)}, u32[]{:S(2)}) collective-permute-start(bf16[16,4096]{1,0:T(8,128)(2,1)S(1)} %fusion), channel_id=1, source_target_pairs={{0,4},{1,5},{2,6},{3,7},{4,0},{5,1},{6,2},{7,3},{8,12},{9,13},{10,... | collective-permute-start | bytes 393224 | tf_op jit(solution)/shard_map/ppermute | solution.py:52
  24.4 3.5 %collective-permute-start.8 = (bf16[32,4096]{1,0:T(8,128)(2,1)S(1)}, bf16[32,4096]{1,0:T(8,128)(2,1)S(1)}, u32[]{:S(2)}, u32[]{:S(2)}) collective-permute-start(bf16[32,4096]{1,0:T(8,128)(2,1)S(1)} %pad_maximum_fusion.1.tokens_ref), channel_id=1, source_target_pairs={{0,1},{1,0},{2,3},{3,2},{4,5},{5,4},{6,7},{7,6},{8,9},{9,8},{10,11... | collective-permute-start | bytes 786440 | tf_op jit(solution)/shard_map/ppermute | solution.py:52
  27.9 7.4 %copy-start = (f32[4096]{0:T(1024)S(1)}, f32[4096]{0:T(1024)}, u32[]{:S(2)}) copy-start(f32[4096]{0:T(1024)} %param.17) | copy-start | bytes 49156
  27.9 7.4 %collective-permute-start.9 = (bf16[16,4096]{1,0:T(8,128)(2,1)S(1)}, bf16[16,4096]{1,0:T(8,128)(2,1)S(1)}, u32[]{:S(2)}, u32[]{:S(2)}) collective-permute-start(bf16[16,4096]{1,0:T(8,128)(2,1)S(1)} %fusion.1), channel_id=1, source_target_pairs={{0,8},{1,9},{2,10},{3,11},{4,12},{5,13},{6,14},{7,15},{8,0},{9,1},... | collective-permute-start | bytes 393224 | tf_op jit(solution)/shard_map/ppermute | solution.py:52
  33.8 8.3 %copy-start.1 = (f32[4096]{0:T(1024)S(1)}, f32[4096]{0:T(1024)}, u32[]{:S(2)}) copy-start(f32[4096]{0:T(1024)} %param.24) | copy-start | bytes 49156
  33.8 8.3 %copy-start.2 = (f32[4096]{0:T(1024)S(1)}, f32[4096]{0:T(1024)}, u32[]{:S(2)}) copy-start(f32[4096]{0:T(1024)} %param.25) | copy-start | bytes 49156
  33.9 8.3 %copy-start.3 = (f32[82]{0:T(128)S(1)}, f32[82]{0:T(128)}, u32[]{:S(2)}) copy-start(f32[82]{0:T(128)} %param.22) | copy-start | bytes 988
  33.9 8.3 %copy-start.4 = (f32[82]{0:T(128)S(1)}, f32[82]{0:T(128)}, u32[]{:S(2)}) copy-start(f32[82]{0:T(128)} %param.23) | copy-start | bytes 988
  35.5 5.0 %collective-permute-start.10 = (bf16[16,4096]{1,0:T(8,128)(2,1)S(1)}, bf16[16,4096]{1,0:T(8,128)(2,1)S(1)}, u32[]{:S(2)}, u32[]{:S(2)}) collective-permute-start(bf16[16,4096]{1,0:T(8,128)(2,1)S(1)} %subtract_convert_fusion), channel_id=1, source_target_pairs={{0,2},{1,3},{2,0},{3,1},{4,6},{5,7},{6,4},{7,5},{8,10},{9,11},{10,... | collective-permute-start | bytes 393224 | tf_op jit(solution)/shard_map/ppermute | solution.py:52
  40.5 1.6 %collective-permute-start.11 = (bf16[32,4096]{1,0:T(8,128)(2,1)S(1)}, bf16[32,4096]{1,0:T(8,128)(2,1)S(1)}, u32[]{:S(2)}, u32[]{:S(2)}) collective-permute-start(bf16[32,4096]{1,0:T(8,128)(2,1)S(1)} %pad_maximum_fusion.2), channel_id=1, source_target_pairs={{0,1},{1,0},{2,3},{3,2},{4,5},{5,4},{6,7},{7,6},{8,9},{9,8},{10,11... | collective-permute-start | bytes 786440 | tf_op jit(solution)/shard_map/ppermute | solution.py:52

commit v4 on v3

--- a/solution.py
+++ b/solution.py
@@ -199,6 +199,10 @@
     )(*map(in_vmem, (tokens, mate_tokens, encoder, bias, decoder)), *map(in_hbm, moments))
 
 
+DECODER_BLOCKS = (1,) * 8
+ENCODER_BLOCKS = (1,) * 8
+
+
 def update_kernel(
     own,
     errors_ref,
@@ -223,18 +227,18 @@
 ):
     outs, slots, (pre_ref, sems) = refs[:12], refs[12:24], refs[24:]
     features = encoder_ref.shape[1]
-    blocks = sems.shape[1]
-    width = features // blocks
-
-    def block_copy(which, block):
-        columns = pl.ds(pl.multiple_of(block * width, width), width)
-        return pltpu.make_async_copy(slots[which].at[:, columns], outs[which].at[:, columns], sems.at[which, block])
-
-    def whole_copy(which):
-        return pltpu.make_async_copy(slots[which], outs[which], sems.at[which, 0])
-
-    def decoder_block(block, carry):
-        columns = pl.ds(pl.multiple_of(block * width, width), width)
+
+    def send(which, columns=slice(None)):
+        pltpu.make_async_copy(slots[which].at[:, columns], outs[which].at[:, columns], sems.at[which]).start()
+
+    def blocks(eighths):
+        start = 0
+        for count in eighths:
+            width = features // 8 * count
+            yield pl.ds(start, width)
+            start += width
+
+    for columns in blocks(DECODER_BLOCKS):
         weight = decoder_ref[:, columns].astype(f32)
         grad = jnp.dot(act_ref[...], errors_ref[:, columns], preferred_element_type=f32) + pull_ref[...] * weight
         new, slots[4][:, columns], slots[5][:, columns] = adam_update(
@@ -242,10 +246,7 @@
         )
         slots[1][:, columns] = new.astype(bf16)
         for which in (1, 4, 5):
-            block_copy(which, block).start()
-        return carry
-
-    lax.fori_loop(0, blocks, decoder_block, 0)
+            send(which, columns)
 
     grad = (nt_dot(decoder_ref[...], errors_ref[...]) + floor_ref[...]) * slope_ref[...]
     pre_ref[...] = grad.astype(bf16)
@@ -253,6 +254,17 @@
     slots[6][...], slots[7][...], slots[8][...] = adam_update(
         encoder_bias_ref[...], total, latent_first_ref[...], latent_second_ref[...]
     )
+    for which in range(6, 9):
+        send(which)
+
+    for columns in blocks(ENCODER_BLOCKS):
+        grad = jnp.dot(pre_ref[...], tokens_ref[:, columns], preferred_element_type=f32)
+        new, slots[2][:, columns], slots[3][:, columns] = adam_update(
+            encoder_ref[:, columns], grad, encoder_first_ref[:, columns], encoder_second_ref[:, columns]
+        )
+        slots[0][:, columns] = new.astype(bf16)
+        for which in (0, 2, 3):
+            send(which, columns)
     rows = errors_ref[...].astype(f32)
     while rows.shape[0] > own:
         half = rows.shape[0] // 2
@@ -263,26 +275,10 @@
     slots[9][...], slots[10][...], slots[11][...] = adam_update(
         decoder_bias_ref[...], total, feature_first_ref[...], feature_second_ref[...]
     )
-    for which in range(6, 12):
-        whole_copy(which).start()
-
-    def encoder_block(block, carry):
-        columns = pl.ds(pl.multiple_of(block * width, width), width)
-        grad = jnp.dot(pre_ref[...], tokens_ref[:, columns], preferred_element_type=f32)
-        new, slots[2][:, columns], slots[3][:, columns] = adam_update(
-            encoder_ref[:, columns], grad, encoder_first_ref[:, columns], encoder_second_ref[:, columns]
-        )
-        slots[0][:, columns] = new.astype(bf16)
-        for which in (0, 2, 3):
-            block_copy(which, block).start()
-        return carry
-
-    lax.fori_loop(0, blocks, encoder_block, 0)
-    for block in range(blocks):
-        for which in range(6):
-            block_copy(which, block).wait()
-    for which in range(6, 12):
-        whole_copy(which).wait()
+    for which in range(9, 12):
+        send(which)
+    for which in range(12):
+        pltpu.make_async_copy(slots[which], outs[which], sems.at[which]).wait()
 
 
 def update(own, errors, prepared, encoder, decoder, *short):
@@ -296,7 +292,7 @@
         out_specs=[ANY_SPEC] * 12,
         out_shape=[jax.ShapeDtypeStruct(*shape) for shape in shapes],
         scratch_shapes=[pltpu.VMEM(*shape) for shape in shapes]
-        + [pltpu.VMEM((latents, count), bf16), pltpu.SemaphoreType.DMA((12, 8))],
+        + [pltpu.VMEM((latents, count), bf16), pltpu.SemaphoreType.DMA((12,))],
         compiler_params=pltpu.CompilerParams(vmem_limit_bytes=24 * 2**20),
         cost_estimate=pl.CostEstimate(
             flops=6 * count * latents * features,

time: 48.7 us -> 46 us (0.945)
  Pallas kernels: 11.6 us -> 8.94 us
    pallas_call x1, Pallas kernels: 6.29 us -> 3.61 us  [update(): pl.pallas_call(functools.partial(update_kernel, own), in_specs=[VMEM_SPEC...]
where the time goes in v4:
time: 46 us; the launch traced here: 45.8 us
  waiting for transfers between devices  19.3 us (42%)
  starting transfers between devices  16.3 us (35%)
  Pallas kernels  8.94 us (19%)
  between operations  0.83 us (2%)
    ppermute x12, waiting for transfers between devices, swap(): return lax.ppermute(x, 'dict', [(i, i ^ bit) for i in range(devices)])  19.3 us
    ppermute x12, starting transfers between devices, swap(): return lax.ppermute(x, 'dict', [(i, i ^ bit) for i in range(devices)])  16.3 us
    pallas_call x1, Pallas kernels, update(): pl.pallas_call(functools.partial(update_kernel, own), in_specs=[VMEM_SPEC...  3.61 us
    pallas_call x1, Pallas kernels, prepare(): pl.pallas_call(prepare_kernel, in_specs=[VMEM_SPEC] * 5 + [ANY_SPEC] * 4,...  2.94 us
    pallas_call x1, Pallas kernels, load(): pl.pallas_call(load_kernel, in_specs=[ANY_SPEC] * len(arrays), out_specs=...  1.38 us
    pallas_call x1, Pallas kernels, forward(): pl.pallas_call(forward_kernel, in_specs=[VMEM_SPEC] * 7, out_specs=[VMEM_...  1 us
  transfers between devices with their start and end apart: 12, of which 8 were waited for; matrix products, arithmetic and copies ran while one was open for 0% of the time, Pallas kernels for 9%

profile of v4, /device:TPU:0, one launch (start us, length us, event | category | flops | bytes accessed | tf_op | source)
XLA Modules:
  0.0 45.8 jit_solution(8690134434685066581)
XLA Ops:
  0.6 4.1 %collective-permute-start = (bf16[4,4096]{1,0:T(4,128)(2,1)}, bf16[4,4096]{1,0:T(4,128)(2,1)S(1)}, u32[]{:S(2)}, u32[]{:S(2)}) collective-permute-start(bf16[4,4096]{1,0:T(4,128)(2,1)} %refs_0_.1), channel_id=1, source_target_pairs={{0,8},{1,9},{2,10},{3,11},{4,12},{5,13},{6,14},{7,15},{8,0},{9,1},... | collective-permute-start | bytes 98312 | tf_op jit(solution)/shard_map/ppermute | solution.py:52
  4.7 1.4 %shard_map.220 = (bf16[4,4096]{1,0:T(4,128)(2,1)S(1)}, bf16[82,4096]{1,0:T(8,128)(2,1)S(1)}, bf16[82,4096]{1,0:T(8,128)(2,1)S(1)}, f32[1,82]{1,0:T(1,128)S(1)}) custom-call(bf16[4,4096]{1,0:T(4,128)(2,1)} %refs_0_.1, bf16[82,4096]{1,0:T(8,128)(2,1)} %refs_1_.1, bf16[82,4096]{1,0:T(8,128)(2,1)} %refs_2_.1, f32[1,82]{1,0:T(1,128)} %bitcast.17), custom_call_target="tpu_custom_call" | custom-call | bytes 2753168 | tf_op jit(solution)/shard_map/pallas_call | solution.py:77
  6.1 1.1 %collective-permute-done = bf16[4,4096]{1,0:T(4,128)(2,1)S(1)} collective-permute-done((bf16[4,4096]{1,0:T(4,128)(2,1)}, bf16[4,4096]{1,0:T(4,128)(2,1)S(1)}, u32[]{:S(2)}, u32[]{:S(2)}) %collective-permute-start) | collective-permute-done | bytes 32800 | tf_op jit(solution)/shard_map/ppermute | solution.py:52
  7.2 1.6 %collective-permute-start.1 = (bf16[8,4096]{1,0:T(8,128)(2,1)S(1)}, bf16[8,4096]{1,0:T(8,128)(2,1)S(1)}, u32[]{:S(2)}, u32[]{:S(2)}) collective-permute-start(bf16[8,4096]{1,0:T(8,128)(2,1)S(1)} %pad_maximum_fusion.4), channel_id=1, source_target_pairs={{0,4},{1,5},{2,6},{3,7},{4,0},{5,1},{6,2},{7,3},{8,12},{9,13},{10,... | collective-permute-start | bytes 196616 | tf_op jit(solution)/shard_map/ppermute | solution.py:52
  8.9 0.0 collective-permute-start.3
  8.9 0.5 %collective-permute-start.5 = (bf16[82,4096]{1,0:T(8,128)(2,1)S(1)}, bf16[82,4096]{1,0:T(8,128)(2,1)S(1)}, u32[]{:S(2)}, u32[]{:S(2)}) collective-permute-start(bf16[82,4096]{1,0:T(8,128)(2,1)S(1)} %get-tuple-element.54.decoder_ref), channel_id=1, source_target_pairs={{0,1},{1,0},{2,3},{3,2},{4,5},{5,4},{6,7},{7,6},{8,9},{9,8},{10,11... | collective-permute-start | bytes 2015240 | tf_op jit(solution)/shard_map/ppermute | solution.py:52
  9.4 2.2 %collective-permute-done.1 = bf16[8,4096]{1,0:T(8,128)(2,1)S(1)} collective-permute-done((bf16[8,4096]{1,0:T(8,128)(2,1)S(1)}, bf16[8,4096]{1,0:T(8,128)(2,1)S(1)}, u32[]{:S(2)}, u32[]{:S(2)}) %collective-permute-start.1) | collective-permute-done | bytes 65568 | tf_op jit(solution)/shard_map/ppermute | solution.py:52
  11.6 1.8 %collective-permute-start.2 = (bf16[16,4096]{1,0:T(8,128)(2,1)S(1)}, bf16[16,4096]{1,0:T(8,128)(2,1)S(1)}, u32[]{:S(2)}, u32[]{:S(2)}) collective-permute-start(bf16[16,4096]{1,0:T(8,128)(2,1)S(1)} %pad_maximum_fusion.3), channel_id=1, source_target_pairs={{0,2},{1,3},{2,0},{3,1},{4,6},{5,7},{6,4},{7,5},{8,10},{9,11},{10,... | collective-permute-start | bytes 393224 | tf_op jit(solution)/shard_map/ppermute | solution.py:52
  13.4 0.0 collective-permute-start.4
  13.4 3.2 %collective-permute-done.2 = bf16[16,4096]{1,0:T(8,128)(2,1)S(1)} collective-permute-done((bf16[16,4096]{1,0:T(8,128)(2,1)S(1)}, bf16[16,4096]{1,0:T(8,128)(2,1)S(1)}, u32[]{:S(2)}, u32[]{:S(2)}) %collective-permute-start.2) | collective-permute-done | bytes 131104 | tf_op jit(solution)/shard_map/ppermute | solution.py:52
  16.6 0.0 collective-permute-done.4.mate_bias_ref
  16.7 0.0 collective-permute-done.5.mate_decoder_ref
  16.7 1.0 %shard_map.221 = (f32[16,4096]{1,0:T(8,128)S(1)}, bf16[16,4096]{1,0:T(8,128)(2,1)S(1)}) custom-call(bf16[32,4096]{1,0:T(8,128)(2,1)S(1)} %pad_maximum_fusion.1.tokens_ref, bf16[82,4096]{1,0:T(8,128)(2,1)S(1)} %get-tuple-element.52.encoder_ref, bf16[82,4096]{1,0:T(8,128)(2,1)S(1)} %collective-permute-done.3.mate_encoder_ref, ...), custom_call_target="tpu_custom_call" | custom-call | flops 85983232 | bytes 2686976 | tf_op jit(solution)/shard_map/pallas_call | solution.py:115
  17.7 1.8 %collective-permute-start.6 = (bf16[16,4096]{1,0:T(8,128)(2,1)S(1)}, bf16[16,4096]{1,0:T(8,128)(2,1)S(1)}, u32[]{:S(2)}, u32[]{:S(2)}) collective-permute-start(bf16[16,4096]{1,0:T(8,128)(2,1)S(1)} %get-tuple-element.56), channel_id=1, source_target_pairs={{0,2},{1,3},{2,0},{3,1},{4,6},{5,7},{6,4},{7,5},{8,10},{9,11},{10,... | collective-permute-start | bytes 393224 | tf_op jit(solution)/shard_map/ppermute | solution.py:52
  19.5 3.2 %collective-permute-done.6 = bf16[16,4096]{1,0:T(8,128)(2,1)S(1)} collective-permute-done((bf16[16,4096]{1,0:T(8,128)(2,1)S(1)}, bf16[16,4096]{1,0:T(8,128)(2,1)S(1)}, u32[]{:S(2)}, u32[]{:S(2)}) %collective-permute-start.6) | collective-permute-done | bytes 131104 | tf_op jit(solution)/shard_map/ppermute | solution.py:52
  22.7 1.6 %collective-permute-start.7 = (bf16[16,4096]{1,0:T(8,128)(2,1)S(1)}, bf16[16,4096]{1,0:T(8,128)(2,1)S(1)}, u32[]{:S(2)}, u32[]{:S(2)}) collective-permute-start(bf16[16,4096]{1,0:T(8,128)(2,1)S(1)} %fusion), channel_id=1, source_target_pairs={{0,4},{1,5},{2,6},{3,7},{4,0},{5,1},{6,2},{7,3},{8,12},{9,13},{10,... | collective-permute-start | bytes 393224 | tf_op jit(solution)/shard_map/ppermute | solution.py:52
  24.4 3.4 %collective-permute-done.7 = bf16[16,4096]{1,0:T(8,128)(2,1)S(1)} collective-permute-done((bf16[16,4096]{1,0:T(8,128)(2,1)S(1)}, bf16[16,4096]{1,0:T(8,128)(2,1)S(1)}, u32[]{:S(2)}, u32[]{:S(2)}) %collective-permute-start.7) | collective-permute-done | bytes 131104 | tf_op jit(solution)/shard_map/ppermute | solution.py:52
  27.8 0.1 fusion.1
  27.9 0.0 copy-start
  27.9 3.0 %collective-permute-start.9 = (bf16[16,4096]{1,0:T(8,128)(2,1)S(1)}, bf16[16,4096]{1,0:T(8,128)(2,1)S(1)}, u32[]{:S(2)}, u32[]{:S(2)}) collective-permute-start(bf16[16,4096]{1,0:T(8,128)(2,1)S(1)} %fusion.1), channel_id=1, source_target_pairs={{0,8},{1,9},{2,10},{3,11},{4,12},{5,13},{6,14},{7,15},{8,0},{9,1},... | collective-permute-start | bytes 393224 | tf_op jit(solution)/shard_map/ppermute | solution.py:52
  30.9 2.9 %shard_map.222 = (bf16[64,4096]{1,0:T(8,128)(2,1)S(1)}, f32[82,64]{1,0:T(8,128)S(1)}, bf16[82,64]{1,0:T(8,128)(2,1)S(1)}, f32[82,1]{1,0:T(8,128)S(1)}, f32[82,1]...) custom-call(bf16[32,4096]{1,0:T(8,128)(2,1)S(1)} %pad_maximum_fusion, ...), custom_call_target="tpu_custom_call" | custom-call | flops 42991616 | bytes 6717440 | tf_op jit(solution)/shard_map/pallas_call | solution.py:182
  33.8 0.0 copy-start.1
  33.8 0.0 copy-start.2
  33.9 0.0 copy-start.3
  33.9 0.0 copy-start.4
  33.9 1.4 %collective-permute-done.9 = bf16[16,4096]{1,0:T(8,128)(2,1)S(1)} collective-permute-done((bf16[16,4096]{1,0:T(8,128)(2,1)S(1)}, bf16[16,4096]{1,0:T(8,128)(2,1)S(1)}, u32[]{:S(2)}, u32[]{:S(2)}) %collective-permute-start.9) | collective-permute-done | bytes 131104 | tf_op jit(solution)/shard_map/ppermute | solution.py:52
  35.3 0.2 subtract_convert_fusion
  35.5 1.8 %collective-permute-start.10 = (bf16[16,4096]{1,0:T(8,128)(2,1)S(1)}, bf16[16,4096]{1,0:T(8,128)(2,1)S(1)}, u32[]{:S(2)}, u32[]{:S(2)}) collective-permute-start(bf16[16,4096]{1,0:T(8,128)(2,1)S(1)} %subtract_convert_fusion), channel_id=1, source_target_pairs={{0,2},{1,3},{2,0},{3,1},{4,6},{5,7},{6,4},{7,5},{8,10},{9,11},{10,... | collective-permute-start | bytes 393224 | tf_op jit(solution)/shard_map/ppermute | solution.py:52
  37.2 3.3 %collective-permute-done.10 = bf16[16,4096]{1,0:T(8,128)(2,1)S(1)} collective-permute-done((bf16[16,4096]{1,0:T(8,128)(2,1)S(1)}, bf16[16,4096]{1,0:T(8,128)(2,1)S(1)}, u32[]{:S(2)}, u32[]{:S(2)}) %collective-permute-start.10) | collective-permute-done | bytes 131104 | tf_op jit(solution)/shard_map/ppermute | solution.py:52
  40.5 0.1 collective-permute-start.11
  40.6 1.5 %collective-permute-done.11 = bf16[32,4096]{1,0:T(8,128)(2,1)S(1)} collective-permute-done((bf16[32,4096]{1,0:T(8,128)(2,1)S(1)}, bf16[32,4096]{1,0:T(8,128)(2,1)S(1)}, u32[]{:S(2)}, u32[]{:S(2)}) %collective-permute-start.11) | collective-permute-done | bytes 262176 | tf_op jit(solution)/shard_map/ppermute | solution.py:52
  42.2 3.6 %shard_map.223 = (bf16[82,4096]{1,0:T(8,128)(2,1)}, bf16[82,4096]{1,0:T(8,128)(2,1)}, f32[82,4096]{1,0:T(8,128)}, f32[82,4096]{1,0:T(8,128)}, f32[82,4096]{1,0:T...) custom-call(bf16[64,4096]{1,0:T(8,128)(2,1)S(1)} %pad_maximum_fusion, ...), custom_call_target="tpu_custom_call" | custom-call | flops 128974848 | bytes 13434880 | tf_op jit(solution)/shard_map/pallas_call | solution.py:289
  (16 shorter events, 0.2 us)
Async XLA Ops:
  0.6 6.6 %collective-permute-start = (bf16[4,4096]{1,0:T(4,128)(2,1)}, bf16[4,4096]{1,0:T(4,128)(2,1)S(1)}, u32[]{:S(2)}, u32[]{:S(2)}) collective-permute-start(bf16[4,4096]{1,0:T(4,128)(2,1)} %refs_0_.1), channel_id=1, source_target_pairs={{0,8},{1,9},{2,10},{3,11},{4,12},{5,13},{6,14},{7,15},{8,0},{9,1},... | collective-permute-start | bytes 98312 | tf_op jit(solution)/shard_map/ppermute | solution.py:52
  7.2 4.3 %collective-permute-start.1 = (bf16[8,4096]{1,0:T(8,128)(2,1)S(1)}, bf16[8,4096]{1,0:T(8,128)(2,1)S(1)}, u32[]{:S(2)}, u32[]{:S(2)}) collective-permute-start(bf16[8,4096]{1,0:T(8,128)(2,1)S(1)} %pad_maximum_fusion.4), channel_id=1, source_target_pairs={{0,4},{1,5},{2,6},{3,7},{4,0},{5,1},{6,2},{7,3},{8,12},{9,13},{10,... | collective-permute-start | bytes 196616 | tf_op jit(solution)/shard_map/ppermute | solution.py:52
  8.9 7.8 %collective-permute-start.3 = (bf16[82,4096]{1,0:T(8,128)(2,1)S(1)}, bf16[82,4096]{1,0:T(8,128)(2,1)S(1)}, u32[]{:S(2)}, u32[]{:S(2)}) collective-permute-start(bf16[82,4096]{1,0:T(8,128)(2,1)S(1)} %get-tuple-element.52.encoder_ref), channel_id=1, source_target_pairs={{0,1},{1,0},{2,3},{3,2},{4,5},{5,4},{6,7},{7,6},{8,9},{9,8},{10,11... | collective-permute-start | bytes 2015240 | tf_op jit(solution)/shard_map/ppermute | solution.py:52
  8.9 7.8 %collective-permute-start.5 = (bf16[82,4096]{1,0:T(8,128)(2,1)S(1)}, bf16[82,4096]{1,0:T(8,128)(2,1)S(1)}, u32[]{:S(2)}, u32[]{:S(2)}) collective-permute-start(bf16[82,4096]{1,0:T(8,128)(2,1)S(1)} %get-tuple-element.54.decoder_ref), channel_id=1, source_target_pairs={{0,1},{1,0},{2,3},{3,2},{4,5},{5,4},{6,7},{7,6},{8,9},{9,8},{10,11... | collective-permute-start | bytes 2015240 | tf_op jit(solution)/shard_map/ppermute | solution.py:52
  11.6 5.0 %collective-permute-start.2 = (bf16[16,4096]{1,0:T(8,128)(2,1)S(1)}, bf16[16,4096]{1,0:T(8,128)(2,1)S(1)}, u32[]{:S(2)}, u32[]{:S(2)}) collective-permute-start(bf16[16,4096]{1,0:T(8,128)(2,1)S(1)} %pad_maximum_fusion.3), channel_id=1, source_target_pairs={{0,2},{1,3},{2,0},{3,1},{4,6},{5,7},{6,4},{7,5},{8,10},{9,11},{10,... | collective-permute-start | bytes 393224 | tf_op jit(solution)/shard_map/ppermute | solution.py:52
  13.4 3.3 %collective-permute-start.4 = (f32[1,82]{1,0:T(1,128)S(1)}, f32[1,82]{1,0:T(1,128)S(1)}, u32[]{:S(2)}, u32[]{:S(2)}) collective-permute-start(f32[1,82]{1,0:T(1,128)S(1)} %get-tuple-element.53.bias_ref.encoder_bias_ref), channel_id=1, source_target_pairs={{0,1},{1,0},{2,3},{3,2},{4,5},{5,4},{6,7},{7,6},{8,9},{9,8},{10,11... | collective-permute-start | bytes 992 | tf_op jit(solution)/shard_map/ppermute | solution.py:52
  17.7 5.0 %collective-permute-start.6 = (bf16[16,4096]{1,0:T(8,128)(2,1)S(1)}, bf16[16,4096]{1,0:T(8,128)(2,1)S(1)}, u32[]{:S(2)}, u32[]{:S(2)}) collective-permute-start(bf16[16,4096]{1,0:T(8,128)(2,1)S(1)} %get-tuple-element.56), channel_id=1, source_target_pairs={{0,2},{1,3},{2,0},{3,1},{4,6},{5,7},{6,4},{7,5},{8,10},{9,11},{10,... | collective-permute-start | bytes 393224 | tf_op jit(solution)/shard_map/ppermute | solution.py:52
  22.7 5.0 %collective-permute-start.7 = (bf16[16,4096]{1,0:T(8,128)(2,1)S(1)}, bf16[16,4096]{1,0:T(8,128)(2,1)S(1)}, u32[]{:S(2)}, u32[]{:S(2)}) collective-permute-start(bf16[16,4096]{1,0:T(8,128)(2,1)S(1)} %fusion), channel_id=1, source_target_pairs={{0,4},{1,5},{2,6},{3,7},{4,0},{5,1},{6,2},{7,3},{8,12},{9,13},{10,... | collective-permute-start | bytes 393224 | tf_op jit(solution)/shard_map/ppermute | solution.py:52
  24.4 3.5 %collective-permute-start.8 = (bf16[32,4096]{1,0:T(8,128)(2,1)S(1)}, bf16[32,4096]{1,0:T(8,128)(2,1)S(1)}, u32[]{:S(2)}, u32[]{:S(2)}) collective-permute-start(bf16[32,4096]{1,0:T(8,128)(2,1)S(1)} %pad_maximum_fusion.1.tokens_ref), channel_id=1, source_target_pairs={{0,1},{1,0},{2,3},{3,2},{4,5},{5,4},{6,7},{7,6},{8,9},{9,8},{10,11... | collective-permute-start | bytes 786440 | tf_op jit(solution)/shard_map/ppermute | solution.py:52
  27.9 7.4 %copy-start = (f32[4096]{0:T(1024)S(1)}, f32[4096]{0:T(1024)}, u32[]{:S(2)}) copy-start(f32[4096]{0:T(1024)} %param.17) | copy-start | bytes 49156
  27.9 7.4 %collective-permute-start.9 = (bf16[16,4096]{1,0:T(8,128)(2,1)S(1)}, bf16[16,4096]{1,0:T(8,128)(2,1)S(1)}, u32[]{:S(2)}, u32[]{:S(2)}) collective-permute-start(bf16[16,4096]{1,0:T(8,128)(2,1)S(1)} %fusion.1), channel_id=1, source_target_pairs={{0,8},{1,9},{2,10},{3,11},{4,12},{5,13},{6,14},{7,15},{8,0},{9,1},... | collective-permute-start | bytes 393224 | tf_op jit(solution)/shard_map/ppermute | solution.py:52
  33.8 8.3 %copy-start.1 = (f32[4096]{0:T(1024)S(1)}, f32[4096]{0:T(1024)}, u32[]{:S(2)}) copy-start(f32[4096]{0:T(1024)} %param.24) | copy-start | bytes 49156
  33.8 8.3 %copy-start.2 = (f32[4096]{0:T(1024)S(1)}, f32[4096]{0:T(1024)}, u32[]{:S(2)}) copy-start(f32[4096]{0:T(1024)} %param.25) | copy-start | bytes 49156
  33.9 8.3 %copy-start.3 = (f32[82]{0:T(128)S(1)}, f32[82]{0:T(128)}, u32[]{:S(2)}) copy-start(f32[82]{0:T(128)} %param.22) | copy-start | bytes 988
  33.9 8.3 %copy-start.4 = (f32[82]{0:T(128)S(1)}, f32[82]{0:T(128)}, u32[]{:S(2)}) copy-start(f32[82]{0:T(128)} %param.23) | copy-start | bytes 988
  35.5 5.0 %collective-permute-start.10 = (bf16[16,4096]{1,0:T(8,128)(2,1)S(1)}, bf16[16,4096]{1,0:T(8,128)(2,1)S(1)}, u32[]{:S(2)}, u32[]{:S(2)}) collective-permute-start(bf16[16,4096]{1,0:T(8,128)(2,1)S(1)} %subtract_convert_fusion), channel_id=1, source_target_pairs={{0,2},{1,3},{2,0},{3,1},{4,6},{5,7},{6,4},{7,5},{8,10},{9,11},{10,... | collective-permute-start | bytes 393224 | tf_op jit(solution)/shard_map/ppermute | solution.py:52
  40.5 1.6 %collective-permute-start.11 = (bf16[32,4096]{1,0:T(8,128)(2,1)S(1)}, bf16[32,4096]{1,0:T(8,128)(2,1)S(1)}, u32[]{:S(2)}, u32[]{:S(2)}) collective-permute-start(bf16[32,4096]{1,0:T(8,128)(2,1)S(1)} %pad_maximum_fusion.2), channel_id=1, source_target_pairs={{0,1},{1,0},{2,3},{3,2},{4,5},{5,4},{6,7},{7,6},{8,9},{9,8},{10,11... | collective-permute-start | bytes 786440 | tf_op jit(solution)/shard_map/ppermute | solution.py:52

commit v5 on v4

--- a/solution.py
+++ b/solution.py
@@ -88,7 +88,15 @@
 
 
 def forward_kernel(
-    tokens_ref, encoder_ref, mate_encoder_ref, bias_ref, mate_bias_ref, decoder_ref, mate_decoder_ref, keep_ref, send_ref
+    tokens_ref,
+    encoder_ref,
+    mate_encoder_ref,
+    bias_ref,
+    mate_bias_ref,
+    decoder_ref,
+    mate_decoder_ref,
+    keep_ref,
+    *send_refs,
 ):
     tokens = tokens_ref[...]
 
@@ -98,70 +106,36 @@
 
     own = act(encoder_ref, bias_ref)
     mate = act(mate_encoder_ref, mate_bias_ref)
-    half = keep_ref.shape[0]
+    rows = keep_ref.shape[0]
     width = 1024
     for start in range(0, keep_ref.shape[1], width):
         columns = pl.ds(start, width)
         part = jnp.dot(own, decoder_ref[:, columns], preferred_element_type=f32) + jnp.dot(
             mate, mate_decoder_ref[:, columns], preferred_element_type=f32
         )
-        keep_ref[:, columns] = part[:half]
-        send_ref[:, columns] = part[half:].astype(bf16)
+        keep_ref[:, columns] = part[:rows]
+        for quarter, send_ref in enumerate(send_refs, 1):
+            send_ref[:, columns] = part[quarter * rows : (quarter + 1) * rows].astype(bf16)
 
 
 def forward(tokens, encoder, mate_encoder, bias, mate_bias, decoder, mate_decoder):
-    half, features = tokens.shape[0] // 2, tokens.shape[1]
+    rows, features = tokens.shape[0] // 4, tokens.shape[1]
     latents = encoder.shape[0]
     return pl.pallas_call(
         forward_kernel,
         in_specs=[VMEM_SPEC] * 7,
-        out_specs=[VMEM_SPEC] * 2,
-        out_shape=[pltpu.VMEM((half, features), f32), pltpu.VMEM((half, features), bf16)],
+        out_specs=[VMEM_SPEC] * 4,
+        out_shape=[pltpu.VMEM((rows, features), f32)] + [pltpu.VMEM((rows, features), bf16)] * 3,
         compiler_params=pltpu.CompilerParams(vmem_limit_bytes=16 * 2**20),
         cost_estimate=pl.CostEstimate(
-            flops=16 * half * latents * features, bytes_accessed=8 * latents * features, transcendentals=8 * half * latents
+            flops=32 * rows * latents * features, bytes_accessed=8 * latents * features, transcendentals=16 * rows * latents
         ),
     )(*map(in_vmem, (tokens, encoder, mate_encoder, bias, mate_bias, decoder, mate_decoder)))
 
 
 def prepare_kernel(
-    tokens_ref,
-    mate_tokens_ref,
-    encoder_ref,
-    bias_ref,
-    decoder_ref,
-    encoder_first_ref,
-    encoder_second_ref,
-    decoder_first_ref,
-    decoder_second_ref,
-    gathered_ref,
-    slope_ref,
-    act_ref,
-    floor_ref,
-    pull_ref,
-    encoder_first_out,
-    encoder_second_out,
-    decoder_first_out,
-    decoder_second_out,
-    sems,
+    tokens_ref, mate_tokens_ref, encoder_ref, bias_ref, decoder_ref, gathered_ref, slope_ref, act_ref, floor_ref, pull_ref
 ):
-    moves = [
-        (encoder_first_ref, encoder_first_out),
-        (encoder_second_ref, encoder_second_out),
-        (decoder_first_ref, decoder_first_out),
-        (decoder_second_ref, decoder_second_out),
-    ]
-    pieces = sems.shape[1]
-    width = encoder_first_ref.shape[1] // pieces
-    copies = [
-        pltpu.make_async_copy(
-            source.at[:, pl.ds(piece * width, width)], target.at[:, pl.ds(piece * width, width)], sems.at[which, piece]
-        )
-        for which, (source, target) in enumerate(moves)
-        for piece in range(pieces)
-    ]
-    for copy in copies:
-        copy.start()
     tokens = jnp.concatenate([tokens_ref[...], mate_tokens_ref[...]], axis=0)
     gathered_ref[...] = tokens
     pre = nt_dot(encoder_ref[...], tokens) + turn(bias_ref[...])
@@ -172,31 +146,27 @@
     norms = jnp.sqrt(jnp.sum(decoder * decoder, axis=1, keepdims=True) + 1e-06)
     floor_ref[...] = sparsity_coef * norms
     pull_ref[...] = sparsity_coef * jnp.sum(act, axis=1, keepdims=True) / norms
-    for copy in copies:
-        copy.wait()
-
-
-def prepare(tokens, mate_tokens, encoder, bias, decoder, *moments):
+
+
+def prepare(tokens, mate_tokens, encoder, bias, decoder):
     latents, features = encoder.shape
     count = 2 * tokens.shape[0]
     return pl.pallas_call(
         prepare_kernel,
-        in_specs=[VMEM_SPEC] * 5 + [ANY_SPEC] * 4,
-        out_specs=[VMEM_SPEC] * 9,
+        in_specs=[VMEM_SPEC] * 5,
+        out_specs=[VMEM_SPEC] * 5,
         out_shape=[
             pltpu.VMEM((count, features), bf16),
             pltpu.VMEM((latents, count), f32),
             pltpu.VMEM((latents, count), bf16),
             pltpu.VMEM((latents, 1), f32),
             pltpu.VMEM((latents, 1), f32),
-        ]
-        + [pltpu.VMEM((latents, features), f32)] * 4,
-        scratch_shapes=[pltpu.SemaphoreType.DMA((4, 2))],
+        ],
         compiler_params=pltpu.CompilerParams(vmem_limit_bytes=16 * 2**20),
         cost_estimate=pl.CostEstimate(
-            flops=2 * count * latents * features, bytes_accessed=20 * latents * features, transcendentals=3 * count * latents
+            flops=2 * count * latents * features, bytes_accessed=10 * latents * features, transcendentals=3 * count * latents
         ),
-    )(*map(in_vmem, (tokens, mate_tokens, encoder, bias, decoder)), *map(in_hbm, moments))
+    )(*map(in_vmem, (tokens, mate_tokens, encoder, bias, decoder)))
 
 
 DECODER_BLOCKS = (1,) * 8
@@ -318,45 +288,47 @@
     feature_first,
     feature_second,
 ):
-    bits = [1 << b for b in reversed(range(1, devices.bit_length() - 1))]
+    far = [1 << b for b in reversed(range(3, devices.bit_length() - 1))]
+    near = (4, 2, 6)
     own = tokens.shape[0]
     row = lambda array: array.reshape(1, -1)
     encoder_bias, latent_first, latent_second, decoder_bias, feature_first, feature_second = map(
         row, (encoder_bias, latent_first, latent_second, decoder_bias, feature_first, feature_second)
     )
-    far = swap(tokens, bits[0], devices)
-    column, encoder, decoder, bias = load(tokens, encoder_weight, decoder_weight, encoder_bias)
-    column = lax.optimization_barrier(jnp.concatenate([column, far], axis=0))
-    mate_encoder = swap(encoder, 1, devices)
-    mate_bias = swap(bias, 1, devices)
-    mate_decoder = swap(decoder, 1, devices)
-    for bit in bits[1:]:
+    other = swap(tokens, far[0], devices)
+    (column,) = load(tokens)
+    mate_encoder = swap(encoder_weight, 1, devices)
+    mate_decoder = swap(decoder_weight, 1, devices)
+    mate_bias = swap(encoder_bias, 1, devices)
+    encoder, decoder, bias = load(encoder_weight, decoder_weight, encoder_bias)
+    column = lax.optimization_barrier(jnp.concatenate([column, other], axis=0))
+    for bit in far[1:]:
         column = lax.optimization_barrier(jnp.concatenate([column, swap(column, bit, devices)], axis=0))
-    part, send = forward(column, encoder, mate_encoder, bias, mate_bias, decoder, mate_decoder)
-    part = part + swap(send, bits[-1], devices).astype(f32)
-    mate_column = swap(column, 1, devices)
-    half = part.shape[0]
-    for level in reversed(range(len(bits) - 1)):
+    rows = column.shape[0]
+    column = lax.optimization_barrier(jnp.concatenate([column] + [swap(column, bits, devices) for bits in near], axis=0))
+    part, *sent = forward(column, encoder, mate_encoder, bias, mate_bias, decoder, mate_decoder)
+    received = {bits: swap(piece, bits, devices) for bits, piece in reversed(list(zip(near, sent)))}
+    moments = load(encoder_first, encoder_second, decoder_first, decoder_second)
+    received, moments = lax.optimization_barrier((received, moments))
+    for bits in (6, 4, 2):
+        part = part + received[bits].astype(f32)
+    for level in reversed(range(len(far))):
         part = lax.reduce_precision(part, 8, 7)
-        sent = part.astype(bf16)
-        if level == 0:
-            sent, mate_column = lax.optimization_barrier((sent, mate_column))
-        other = swap(sent, bits[level], devices)
-        if level == 0:
-            prepared = prepare(
-                column, mate_column, encoder, bias, decoder, encoder_first, encoder_second, decoder_first, decoder_second
-            )
-            other, prepared = lax.optimization_barrier((other, prepared))
+        piece = part.astype(bf16)
+        other = swap(piece, far[level], devices)
         size = own << level
-        pieces = [other[start ^ size : (start ^ size) + size] for start in range(0, half, size)]
+        pieces = [other[start ^ size : (start ^ size) + size] for start in range(0, rows, size)]
         part = part + jnp.concatenate(pieces, axis=0).astype(f32)
-    errors = (part + decoder_bias - column[:half].astype(f32)).astype(bf16)
-    errors = lax.optimization_barrier(jnp.concatenate([errors, swap(errors, bits[-1], devices)], axis=0))
+    errors = (part + decoder_bias - column[:rows].astype(f32)).astype(bf16)
+    errors, column = lax.optimization_barrier((errors, column))
+    received = [swap(errors, bits, devices) for bits in near]
+    prepared = prepare(column, swap(column, 1, devices), encoder, bias, decoder)
+    errors = lax.optimization_barrier(jnp.concatenate([errors] + received, axis=0))
     errors = jnp.concatenate([errors, swap(errors, 1, devices)], axis=0)
     out = update(
         own,
         errors,
-        prepared,
+        (*prepared, *moments),
         encoder,
         decoder,
         bias,

time: 46 us -> 41.3 us (0.90)
  waiting for transfers between devices: 19.3 us -> 11.9 us
  starting transfers between devices: 16.3 us -> 18.1 us
  Pallas kernels: 8.94 us -> 9.93 us
    ppermute x12 -> x16, waiting for transfers between devices: 19.3 us -> 11.9 us  [swap(): return lax.ppermute(x, 'dict', [(i, i ^ bit) for i in range(devices)])]
    pallas_call x1 -> x3, Pallas kernels: 1.38 us -> 4.82 us  [load(): pl.pallas_call(load_kernel, in_specs=[ANY_SPEC] * len(arrays), out_specs=...]
    pallas_call x1, Pallas kernels: 2.94 us -> 0.53 us  [prepare(): pl.pallas_call(prepare_kernel, in_specs=[VMEM_SPEC] * 5, out_specs=[VMEM_...]
    ppermute x12 -> x16, starting transfers between devices: 16.3 us -> 18.1 us  [swap(): return lax.ppermute(x, 'dict', [(i, i ^ bit) for i in range(devices)])]
  transfers between devices with their start and end apart: 12 -> 16, of which waited for: 8 -> 10; matrix products, arithmetic and copies ran while one was open for 0% -> 0% of each run, Pallas kernels for 9% -> 13%
where the time goes in v5:
time: 41.3 us; the launch traced here: 41.1 us
  starting transfers between devices  18.1 us (44%)
  waiting for transfers between devices  11.9 us (29%)
  Pallas kernels  9.93 us (24%)
  between operations  0.85 us (2%)
    ppermute x16, starting transfers between devices, swap(): return lax.ppermute(x, 'dict', [(i, i ^ bit) for i in range(devices)])  18.1 us
    ppermute x16, waiting for transfers between devices, swap(): return lax.ppermute(x, 'dict', [(i, i ^ bit) for i in range(devices)])  11.9 us
    pallas_call x3, Pallas kernels, load(): pl.pallas_call(load_kernel, in_specs=[ANY_SPEC] * len(arrays), out_specs=...  4.82 us
    pallas_call x1, Pallas kernels, update(): pl.pallas_call(functools.partial(update_kernel, own), in_specs=[VMEM_SPEC...  3.58 us
    pallas_call x1, Pallas kernels, forward(): pl.pallas_call(forward_kernel, in_specs=[VMEM_SPEC] * 7, out_specs=[VMEM_...  1 us
  transfers between devices with their start and end apart: 16, of which 10 were waited for; matrix products, arithmetic and copies ran while one was open for 0% of the time, Pallas kernels for 13%

profile of v5, /device:TPU:0, one launch (start us, length us, event | category | flops | bytes accessed | tf_op | source)
XLA Modules:
  0.0 41.1 jit_solution(10490562883121240432)
XLA Ops:
  0.7 4.1 %collective-permute-start = (bf16[4,4096]{1,0:T(4,128)(2,1)}, bf16[4,4096]{1,0:T(4,128)(2,1)S(1)}, u32[]{:S(2)}, u32[]{:S(2)}) collective-permute-start(bf16[4,4096]{1,0:T(4,128)(2,1)} %refs_0_.3), channel_id=1, source_target_pairs={{0,8},{1,9},{2,10},{3,11},{4,12},{5,13},{6,14},{7,15},{8,0},{9,1},... | collective-permute-start | bytes 98312 | tf_op jit(solution)/shard_map/ppermute | solution.py:52
  4.8 0.5 %collective-permute-start.6 = (bf16[82,4096]{1,0:T(8,128)(2,1)}, bf16[82,4096]{1,0:T(8,128)(2,1)S(1)}, u32[]{:S(2)}, u32[]{:S(2)}) collective-permute-start(bf16[82,4096]{1,0:T(8,128)(2,1)} %refs_1_.2), channel_id=1, source_target_pairs={{0,1},{1,0},{2,3},{3,2},{4,5},{5,4},{6,7},{7,6},{8,9},{9,8},{10,11... | collective-permute-start | bytes 2015240 | tf_op jit(solution)/shard_map/ppermute | solution.py:52
  5.3 0.8 %shard_map.220 = bf16[4,4096]{1,0:T(4,128)(2,1)S(1)} custom-call(bf16[4,4096]{1,0:T(4,128)(2,1)} %refs_0_.3), custom_call_target="tpu_custom_call" | custom-call | bytes 65536 | tf_op jit(solution)/shard_map/pallas_call | solution.py:77
  6.0 1.2 %collective-permute-done = bf16[4,4096]{1,0:T(4,128)(2,1)S(1)} collective-permute-done((bf16[4,4096]{1,0:T(4,128)(2,1)}, bf16[4,4096]{1,0:T(4,128)(2,1)S(1)}, u32[]{:S(2)}, u32[]{:S(2)}) %collective-permute-start) | collective-permute-done | bytes 32800 | tf_op jit(solution)/shard_map/ppermute | solution.py:52
  7.3 2.6 %collective-permute-start.3 = (bf16[8,4096]{1,0:T(8,128)(2,1)S(1)}, bf16[8,4096]{1,0:T(8,128)(2,1)S(1)}, u32[]{:S(2)}, u32[]{:S(2)}) collective-permute-start(bf16[8,4096]{1,0:T(8,128)(2,1)S(1)} %pad_maximum_fusion.3), channel_id=1, source_target_pairs={{0,6},{1,7},{2,4},{3,5},{4,2},{5,3},{6,0},{7,1},{8,14},{9,15},{10,... | collective-permute-start | bytes 196616 | tf_op jit(solution)/shard_map/ppermute | solution.py:52
  9.8 0.5 %collective-permute-start.2 = (bf16[8,4096]{1,0:T(8,128)(2,1)S(1)}, bf16[8,4096]{1,0:T(8,128)(2,1)S(1)}, u32[]{:S(2)}, u32[]{:S(2)}) collective-permute-start(bf16[8,4096]{1,0:T(8,128)(2,1)S(1)} %pad_maximum_fusion.3), channel_id=1, source_target_pairs={{0,2},{1,3},{2,0},{3,1},{4,6},{5,7},{6,4},{7,5},{8,10},{9,11},{10,... | collective-permute-start | bytes 196616 | tf_op jit(solution)/shard_map/ppermute | solution.py:52
  10.3 0.5 %collective-permute-start.1 = (bf16[8,4096]{1,0:T(8,128)(2,1)S(1)}, bf16[8,4096]{1,0:T(8,128)(2,1)S(1)}, u32[]{:S(2)}, u32[]{:S(2)}) collective-permute-start(bf16[8,4096]{1,0:T(8,128)(2,1)S(1)} %pad_maximum_fusion.3), channel_id=1, source_target_pairs={{0,4},{1,5},{2,6},{3,7},{4,0},{5,1},{6,2},{7,3},{8,12},{9,13},{10,... | collective-permute-start | bytes 196616 | tf_op jit(solution)/shard_map/ppermute | solution.py:52
  10.8 1.4 %shard_map.221 = (bf16[82,4096]{1,0:T(8,128)(2,1)S(1)}, bf16[82,4096]{1,0:T(8,128)(2,1)S(1)}, f32[1,82]{1,0:T(1,128)S(1)}) custom-call(bf16[82,4096]{1,0:T(8,128)(2,1)} %refs_0_.4, bf16[82,4096]{1,0:T(8,128)(2,1)} %refs_1_.2, f32[1,82]{1,0:T(1,128)} %bitcast.17), custom_call_target="tpu_custom_call" | custom-call | bytes 2687632 | tf_op jit(solution)/shard_map/pallas_call | solution.py:77
  12.2 0.7 %collective-permute-done.3 = bf16[8,4096]{1,0:T(8,128)(2,1)S(1)} collective-permute-done((bf16[8,4096]{1,0:T(8,128)(2,1)S(1)}, bf16[8,4096]{1,0:T(8,128)(2,1)S(1)}, u32[]{:S(2)}, u32[]{:S(2)}) %collective-permute-start.3) | collective-permute-done | bytes 65568 | tf_op jit(solution)/shard_map/ppermute | solution.py:52
  12.9 1.2 %collective-permute-done.2 = bf16[8,4096]{1,0:T(8,128)(2,1)S(1)} collective-permute-done((bf16[8,4096]{1,0:T(8,128)(2,1)S(1)}, bf16[8,4096]{1,0:T(8,128)(2,1)S(1)}, u32[]{:S(2)}, u32[]{:S(2)}) %collective-permute-start.2) | collective-permute-done | bytes 65568 | tf_op jit(solution)/shard_map/ppermute | solution.py:52
  14.1 0.5 %collective-permute-done.1 = bf16[8,4096]{1,0:T(8,128)(2,1)S(1)} collective-permute-done((bf16[8,4096]{1,0:T(8,128)(2,1)S(1)}, bf16[8,4096]{1,0:T(8,128)(2,1)S(1)}, u32[]{:S(2)}, u32[]{:S(2)}) %collective-permute-start.1) | collective-permute-done | bytes 65568 | tf_op jit(solution)/shard_map/ppermute | solution.py:52
  14.7 1.0 %shard_map.222 = (f32[8,4096]{1,0:T(8,128)S(1)}, bf16[8,4096]{1,0:T(8,128)(2,1)S(1)}, bf16[8,4096]{1,0:T(8,128)(2,1)S(1)}, bf16[8,4096]{1,0:T(8,128)(2,1)S(1)}) custom-call(bf16[32,4096]{1,0:T(8,128)(2,1)S(1)} %pad_maximum_fusion.1.tokens_ref, bf16[82,4096]{1,0:T(8,128)(2,1)S(1)} %get-tuple-element.49.encoder_ref, ...), custom_call_target="tpu_custom_call" | custom-call | flops 85983232 | bytes 2686976 | tf_op jit(solution)/shard_map/pallas_call | solution.py:124
  15.7 1.6 %collective-permute-start.7 = (bf16[8,4096]{1,0:T(8,128)(2,1)S(1)}, bf16[8,4096]{1,0:T(8,128)(2,1)S(1)}, u32[]{:S(2)}, u32[]{:S(2)}) collective-permute-start(bf16[8,4096]{1,0:T(8,128)(2,1)S(1)} %get-tuple-element.53), channel_id=1, source_target_pairs={{0,2},{1,3},{2,0},{3,1},{4,6},{5,7},{6,4},{7,5},{8,10},{9,11},{10,... | collective-permute-start | bytes 196616 | tf_op jit(solution)/shard_map/ppermute | solution.py:52
  17.2 0.7 %collective-permute-start.8 = (bf16[8,4096]{1,0:T(8,128)(2,1)S(1)}, bf16[8,4096]{1,0:T(8,128)(2,1)S(1)}, u32[]{:S(2)}, u32[]{:S(2)}) collective-permute-start(bf16[8,4096]{1,0:T(8,128)(2,1)S(1)} %get-tuple-element.54), channel_id=1, source_target_pairs={{0,4},{1,5},{2,6},{3,7},{4,0},{5,1},{6,2},{7,3},{8,12},{9,13},{10,... | collective-permute-start | bytes 196616 | tf_op jit(solution)/shard_map/ppermute | solution.py:52
  17.9 1.3 %collective-permute-start.9 = (bf16[8,4096]{1,0:T(8,128)(2,1)S(1)}, bf16[8,4096]{1,0:T(8,128)(2,1)S(1)}, u32[]{:S(2)}, u32[]{:S(2)}) collective-permute-start(bf16[8,4096]{1,0:T(8,128)(2,1)S(1)} %get-tuple-element.55), channel_id=1, source_target_pairs={{0,6},{1,7},{2,4},{3,5},{4,2},{5,3},{6,0},{7,1},{8,14},{9,15},{10,... | collective-permute-start | bytes 196616 | tf_op jit(solution)/shard_map/ppermute | solution.py:52
  19.2 2.7 %shard_map.223 = (f32[82,4096]{1,0:T(8,128)S(1)}, f32[82,4096]{1,0:T(8,128)S(1)}, f32[82,4096]{1,0:T(8,128)S(1)}, f32[82,4096]{1,0:T(8,128)S(1)}) custom-call(f32[82,4096]{1,0:T(8,128)} %refs_0_.5, f32[82,4096]{1,0:T(8,128)} %refs_1_.3, f32[82,4096]{1,0:T(8,128)} %refs_2_.1, f32[82,4096]{1,0:T(8,128)} %refs_3_.1), custom_call_target="tpu_custom_call" | custom-call | bytes 10747904 | tf_op jit(solution)/shard_map/pallas_call | solution.py:77
  22.0 1.1 %collective-permute-done.9 = bf16[8,4096]{1,0:T(8,128)(2,1)S(1)} collective-permute-done((bf16[8,4096]{1,0:T(8,128)(2,1)S(1)}, bf16[8,4096]{1,0:T(8,128)(2,1)S(1)}, u32[]{:S(2)}, u32[]{:S(2)}) %collective-permute-start.9) | collective-permute-done | bytes 65568 | tf_op jit(solution)/shard_map/ppermute | solution.py:52
  23.1 2.7 %collective-permute-start.10 = (bf16[8,4096]{1,0:T(8,128)(2,1)S(1)}, bf16[8,4096]{1,0:T(8,128)(2,1)S(1)}, u32[]{:S(2)}, u32[]{:S(2)}) collective-permute-start(bf16[8,4096]{1,0:T(8,128)(2,1)S(1)} %fusion), channel_id=1, source_target_pairs={{0,8},{1,9},{2,10},{3,11},{4,12},{5,13},{6,14},{7,15},{8,0},{9,1},... | collective-permute-start | bytes 196616 | tf_op jit(solution)/shard_map/ppermute | solution.py:52
  25.9 2.5 %collective-permute-done.10 = bf16[8,4096]{1,0:T(8,128)(2,1)S(1)} collective-permute-done((bf16[8,4096]{1,0:T(8,128)(2,1)S(1)}, bf16[8,4096]{1,0:T(8,128)(2,1)S(1)}, u32[]{:S(2)}, u32[]{:S(2)}) %collective-permute-start.10) | collective-permute-done | bytes 65568 | tf_op jit(solution)/shard_map/ppermute | solution.py:52
  28.4 0.1 subtract_convert_fusion
  28.5 1.5 %collective-permute-start.13 = (bf16[8,4096]{1,0:T(8,128)(2,1)S(1)}, bf16[8,4096]{1,0:T(8,128)(2,1)S(1)}, u32[]{:S(2)}, u32[]{:S(2)}) collective-permute-start(bf16[8,4096]{1,0:T(8,128)(2,1)S(1)} %subtract_convert_fusion), channel_id=1, source_target_pairs={{0,6},{1,7},{2,4},{3,5},{4,2},{5,3},{6,0},{7,1},{8,14},{9,15},{10,... | collective-permute-start | bytes 196616 | tf_op jit(solution)/shard_map/ppermute | solution.py:52
  30.0 1.4 %collective-permute-start.12 = (bf16[8,4096]{1,0:T(8,128)(2,1)S(1)}, bf16[8,4096]{1,0:T(8,128)(2,1)S(1)}, u32[]{:S(2)}, u32[]{:S(2)}) collective-permute-start(bf16[8,4096]{1,0:T(8,128)(2,1)S(1)} %subtract_convert_fusion), channel_id=1, source_target_pairs={{0,2},{1,3},{2,0},{3,1},{4,6},{5,7},{6,4},{7,5},{8,10},{9,11},{10,... | collective-permute-start | bytes 196616 | tf_op jit(solution)/shard_map/ppermute | solution.py:52
  31.5 0.6 %collective-permute-start.11 = (bf16[8,4096]{1,0:T(8,128)(2,1)S(1)}, bf16[8,4096]{1,0:T(8,128)(2,1)S(1)}, u32[]{:S(2)}, u32[]{:S(2)}) collective-permute-start(bf16[8,4096]{1,0:T(8,128)(2,1)S(1)} %subtract_convert_fusion), channel_id=1, source_target_pairs={{0,4},{1,5},{2,6},{3,7},{4,0},{5,1},{6,2},{7,3},{8,12},{9,13},{10,... | collective-permute-start | bytes 196616 | tf_op jit(solution)/shard_map/ppermute | solution.py:52
  32.1 1.7 %collective-permute-done.13 = bf16[8,4096]{1,0:T(8,128)(2,1)S(1)} collective-permute-done((bf16[8,4096]{1,0:T(8,128)(2,1)S(1)}, bf16[8,4096]{1,0:T(8,128)(2,1)S(1)}, u32[]{:S(2)}, u32[]{:S(2)}) %collective-permute-start.13) | collective-permute-done | bytes 65568 | tf_op jit(solution)/shard_map/ppermute | solution.py:52
  33.7 0.7 %collective-permute-done.12 = bf16[8,4096]{1,0:T(8,128)(2,1)S(1)} collective-permute-done((bf16[8,4096]{1,0:T(8,128)(2,1)S(1)}, bf16[8,4096]{1,0:T(8,128)(2,1)S(1)}, u32[]{:S(2)}, u32[]{:S(2)}) %collective-permute-start.12) | collective-permute-done | bytes 65568 | tf_op jit(solution)/shard_map/ppermute | solution.py:52
  34.4 1.3 %collective-permute-done.11 = bf16[8,4096]{1,0:T(8,128)(2,1)S(1)} collective-permute-done((bf16[8,4096]{1,0:T(8,128)(2,1)S(1)}, bf16[8,4096]{1,0:T(8,128)(2,1)S(1)}, u32[]{:S(2)}, u32[]{:S(2)}) %collective-permute-start.11) | collective-permute-done | bytes 65568 | tf_op jit(solution)/shard_map/ppermute | solution.py:52
  35.8 0.0 copy-start.3
  35.8 0.0 copy-start.4
  35.8 0.1 collective-permute-start.14
  35.9 0.5 %shard_map.224 = (bf16[64,4096]{1,0:T(8,128)(2,1)S(1)}, f32[82,64]{1,0:T(8,128)S(1)}, bf16[82,64]{1,0:T(8,128)(2,1)S(1)}, f32[82,1]{1,0:T(8,128)S(1)}, f32[82,1]{1,0:T(8,128)S(1)}) custom-call(bf16[32,4096]{1,0:T(8,128)(2,1)S(1)} %pad_maximum_fusion.1.tokens_ref, bf16[32,4096]{1,0:T(8,128)(2,1)S(1)} %collective-permute-done.15.mate_tokens_ref, ...), custom_call_target="tpu_custom_call" | custom-call | flops 42991616 | bytes 3358720 | tf_op jit(solution)/shard_map/pallas_call | solution.py:154
  36.4 1.0 %collective-permute-done.14 = bf16[32,4096]{1,0:T(8,128)(2,1)S(1)} collective-permute-done((bf16[32,4096]{1,0:T(8,128)(2,1)S(1)}, bf16[32,4096]{1,0:T(8,128)(2,1)S(1)}, u32[]{:S(2)}, u32[]{:S(2)}) %collective-permute-start.14) | collective-permute-done | bytes 262176 | tf_op jit(solution)/shard_map/ppermute | solution.py:52
  37.5 3.6 %shard_map.225 = (bf16[82,4096]{1,0:T(8,128)(2,1)}, bf16[82,4096]{1,0:T(8,128)(2,1)}, f32[82,4096]{1,0:T(8,128)}, f32[82,4096]{1,0:T(8,128)}, f32[82,4096]{1,0:T...) custom-call(bf16[64,4096]{1,0:T(8,128)(2,1)S(1)} %pad_maximum_fusion, ...), custom_call_target="tpu_custom_call" | custom-call | flops 128974848 | bytes 13434880 | tf_op jit(solution)/shard_map/pallas_call | solution.py:259
  (25 shorter events, 0.2 us)
Async XLA Ops:
  0.6 12.2 %copy-start.5 = (f32[82]{0:T(128)S(1)}, f32[82]{0:T(128)}, u32[]{:S(2)}) copy-start(f32[82]{0:T(128)} %param.15) | copy-start | bytes 988
  0.7 6.6 %collective-permute-start = (bf16[4,4096]{1,0:T(4,128)(2,1)}, bf16[4,4096]{1,0:T(4,128)(2,1)S(1)}, u32[]{:S(2)}, u32[]{:S(2)}) collective-permute-start(bf16[4,4096]{1,0:T(4,128)(2,1)} %refs_0_.3), channel_id=1, source_target_pairs={{0,8},{1,9},{2,10},{3,11},{4,12},{5,13},{6,14},{7,15},{8,0},{9,1},... | collective-permute-start | bytes 98312 | tf_op jit(solution)/shard_map/ppermute | solution.py:52
  4.8 9.9 %collective-permute-start.4 = (bf16[82,4096]{1,0:T(8,128)(2,1)}, bf16[82,4096]{1,0:T(8,128)(2,1)S(1)}, u32[]{:S(2)}, u32[]{:S(2)}) collective-permute-start(bf16[82,4096]{1,0:T(8,128)(2,1)} %refs_0_.4), channel_id=1, source_target_pairs={{0,1},{1,0},{2,3},{3,2},{4,5},{5,4},{6,7},{7,6},{8,9},{9,8},{10,11... | collective-permute-start | bytes 2015240 | tf_op jit(solution)/shard_map/ppermute | solution.py:52
  4.8 9.9 %collective-permute-start.6 = (bf16[82,4096]{1,0:T(8,128)(2,1)}, bf16[82,4096]{1,0:T(8,128)(2,1)S(1)}, u32[]{:S(2)}, u32[]{:S(2)}) collective-permute-start(bf16[82,4096]{1,0:T(8,128)(2,1)} %refs_1_.2), channel_id=1, source_target_pairs={{0,1},{1,0},{2,3},{3,2},{4,5},{5,4},{6,7},{7,6},{8,9},{9,8},{10,11... | collective-permute-start | bytes 2015240 | tf_op jit(solution)/shard_map/ppermute | solution.py:52
  7.3 5.6 %collective-permute-start.3 = (bf16[8,4096]{1,0:T(8,128)(2,1)S(1)}, bf16[8,4096]{1,0:T(8,128)(2,1)S(1)}, u32[]{:S(2)}, u32[]{:S(2)}) collective-permute-start(bf16[8,4096]{1,0:T(8,128)(2,1)S(1)} %pad_maximum_fusion.3), channel_id=1, source_target_pairs={{0,6},{1,7},{2,4},{3,5},{4,2},{5,3},{6,0},{7,1},{8,14},{9,15},{10,... | collective-permute-start | bytes 196616 | tf_op jit(solution)/shard_map/ppermute | solution.py:52
  9.8 4.3 %collective-permute-start.2 = (bf16[8,4096]{1,0:T(8,128)(2,1)S(1)}, bf16[8,4096]{1,0:T(8,128)(2,1)S(1)}, u32[]{:S(2)}, u32[]{:S(2)}) collective-permute-start(bf16[8,4096]{1,0:T(8,128)(2,1)S(1)} %pad_maximum_fusion.3), channel_id=1, source_target_pairs={{0,2},{1,3},{2,0},{3,1},{4,6},{5,7},{6,4},{7,5},{8,10},{9,11},{10,... | collective-permute-start | bytes 196616 | tf_op jit(solution)/shard_map/ppermute | solution.py:52
  10.3 4.3 %collective-permute-start.1 = (bf16[8,4096]{1,0:T(8,128)(2,1)S(1)}, bf16[8,4096]{1,0:T(8,128)(2,1)S(1)}, u32[]{:S(2)}, u32[]{:S(2)}) collective-permute-start(bf16[8,4096]{1,0:T(8,128)(2,1)S(1)} %pad_maximum_fusion.3), channel_id=1, source_target_pairs={{0,4},{1,5},{2,6},{3,7},{4,0},{5,1},{6,2},{7,3},{8,12},{9,13},{10,... | collective-permute-start | bytes 196616 | tf_op jit(solution)/shard_map/ppermute | solution.py:52
  12.9 1.8 %collective-permute-start.5 = (f32[1,82]{1,0:T(1,128)S(1)}, f32[1,82]{1,0:T(1,128)S(1)}, u32[]{:S(2)}, u32[]{:S(2)}) collective-permute-start(f32[1,82]{1,0:T(1,128)S(1)} %bitcast.18), channel_id=1, source_target_pairs={{0,1},{1,0},{2,3},{3,2},{4,5},{5,4},{6,7},{7,6},{8,9},{9,8},{10,11... | collective-permute-start | bytes 992 | tf_op jit(solution)/shard_map/ppermute | solution.py:52
  15.7 6.3 %collective-permute-start.7 = (bf16[8,4096]{1,0:T(8,128)(2,1)S(1)}, bf16[8,4096]{1,0:T(8,128)(2,1)S(1)}, u32[]{:S(2)}, u32[]{:S(2)}) collective-permute-start(bf16[8,4096]{1,0:T(8,128)(2,1)S(1)} %get-tuple-element.53), channel_id=1, source_target_pairs={{0,2},{1,3},{2,0},{3,1},{4,6},{5,7},{6,4},{7,5},{8,10},{9,11},{10,... | collective-permute-start | bytes 196616 | tf_op jit(solution)/shard_map/ppermute | solution.py:52
  17.2 4.7 %collective-permute-start.8 = (bf16[8,4096]{1,0:T(8,128)(2,1)S(1)}, bf16[8,4096]{1,0:T(8,128)(2,1)S(1)}, u32[]{:S(2)}, u32[]{:S(2)}) collective-permute-start(bf16[8,4096]{1,0:T(8,128)(2,1)S(1)} %get-tuple-element.54), channel_id=1, source_target_pairs={{0,4},{1,5},{2,6},{3,7},{4,0},{5,1},{6,2},{7,3},{8,12},{9,13},{10,... | collective-permute-start | bytes 196616 | tf_op jit(solution)/shard_map/ppermute | solution.py:52
  17.9 10.5 %copy-start = (f32[4096]{0:T(1024)S(1)}, f32[4096]{0:T(1024)}, u32[]{:S(2)}) copy-start(f32[4096]{0:T(1024)} %param.17) | copy-start | bytes 49156
  17.9 5.2 %collective-permute-start.9 = (bf16[8,4096]{1,0:T(8,128)(2,1)S(1)}, bf16[8,4096]{1,0:T(8,128)(2,1)S(1)}, u32[]{:S(2)}, u32[]{:S(2)}) collective-permute-start(bf16[8,4096]{1,0:T(8,128)(2,1)S(1)} %get-tuple-element.55), channel_id=1, source_target_pairs={{0,6},{1,7},{2,4},{3,5},{4,2},{5,3},{6,0},{7,1},{8,14},{9,15},{10,... | collective-permute-start | bytes 196616 | tf_op jit(solution)/shard_map/ppermute | solution.py:52
  23.1 5.2 %collective-permute-start.10 = (bf16[8,4096]{1,0:T(8,128)(2,1)S(1)}, bf16[8,4096]{1,0:T(8,128)(2,1)S(1)}, u32[]{:S(2)}, u32[]{:S(2)}) collective-permute-start(bf16[8,4096]{1,0:T(8,128)(2,1)S(1)} %fusion), channel_id=1, source_target_pairs={{0,8},{1,9},{2,10},{3,11},{4,12},{5,13},{6,14},{7,15},{8,0},{9,1},... | collective-permute-start | bytes 196616 | tf_op jit(solution)/shard_map/ppermute | solution.py:52
  28.5 5.2 %collective-permute-start.13 = (bf16[8,4096]{1,0:T(8,128)(2,1)S(1)}, bf16[8,4096]{1,0:T(8,128)(2,1)S(1)}, u32[]{:S(2)}, u32[]{:S(2)}) collective-permute-start(bf16[8,4096]{1,0:T(8,128)(2,1)S(1)} %subtract_convert_fusion), channel_id=1, source_target_pairs={{0,6},{1,7},{2,4},{3,5},{4,2},{5,3},{6,0},{7,1},{8,14},{9,15},{10,... | collective-permute-start | bytes 196616 | tf_op jit(solution)/shard_map/ppermute | solution.py:52
  30.0 4.4 %collective-permute-start.12 = (bf16[8,4096]{1,0:T(8,128)(2,1)S(1)}, bf16[8,4096]{1,0:T(8,128)(2,1)S(1)}, u32[]{:S(2)}, u32[]{:S(2)}) collective-permute-start(bf16[8,4096]{1,0:T(8,128)(2,1)S(1)} %subtract_convert_fusion), channel_id=1, source_target_pairs={{0,2},{1,3},{2,0},{3,1},{4,6},{5,7},{6,4},{7,5},{8,10},{9,11},{10,... | collective-permute-start | bytes 196616 | tf_op jit(solution)/shard_map/ppermute | solution.py:52
  31.5 4.3 %collective-permute-start.11 = (bf16[8,4096]{1,0:T(8,128)(2,1)S(1)}, bf16[8,4096]{1,0:T(8,128)(2,1)S(1)}, u32[]{:S(2)}, u32[]{:S(2)}) collective-permute-start(bf16[8,4096]{1,0:T(8,128)(2,1)S(1)} %subtract_convert_fusion), channel_id=1, source_target_pairs={{0,4},{1,5},{2,6},{3,7},{4,0},{5,1},{6,2},{7,3},{8,12},{9,13},{10,... | collective-permute-start | bytes 196616 | tf_op jit(solution)/shard_map/ppermute | solution.py:52
  32.1 3.8 %collective-permute-start.15 = (bf16[32,4096]{1,0:T(8,128)(2,1)S(1)}, bf16[32,4096]{1,0:T(8,128)(2,1)S(1)}, u32[]{:S(2)}, u32[]{:S(2)}) collective-permute-start(bf16[32,4096]{1,0:T(8,128)(2,1)S(1)} %pad_maximum_fusion.1.tokens_ref), channel_id=1, source_target_pairs={{0,1},{1,0},{2,3},{3,2},{4,5},{5,4},{6,7},{7,6},{8,9},{9,8},{10,11... | collective-permute-start | bytes 786440 | tf_op jit(solution)/shard_map/ppermute | solution.py:52
  35.8 1.7 %copy-start.1 = (f32[4096]{0:T(1024)S(1)}, f32[4096]{0:T(1024)}, u32[]{:S(2)}) copy-start(f32[4096]{0:T(1024)} %param.24) | copy-start | bytes 49156
  35.8 1.7 %copy-start.2 = (f32[4096]{0:T(1024)S(1)}, f32[4096]{0:T(1024)}, u32[]{:S(2)}) copy-start(f32[4096]{0:T(1024)} %param.25) | copy-start | bytes 49156
  35.8 1.7 %copy-start.3 = (f32[82]{0:T(128)S(1)}, f32[82]{0:T(128)}, u32[]{:S(2)}) copy-start(f32[82]{0:T(128)} %param.22) | copy-start | bytes 988
  35.8 1.7 %copy-start.4 = (f32[82]{0:T(128)S(1)}, f32[82]{0:T(128)}, u32[]{:S(2)}) copy-start(f32[82]{0:T(128)} %param.23) | copy-start | bytes 988
  35.8 1.6 %collective-permute-start.14 = (bf16[32,4096]{1,0:T(8,128)(2,1)S(1)}, bf16[32,4096]{1,0:T(8,128)(2,1)S(1)}, u32[]{:S(2)}, u32[]{:S(2)}) collective-permute-start(bf16[32,4096]{1,0:T(8,128)(2,1)S(1)} %pad_maximum_fusion.2), channel_id=1, source_target_pairs={{0,1},{1,0},{2,3},{3,2},{4,5},{5,4},{6,7},{7,6},{8,9},{9,8},{10,11... | collective-permute-start | bytes 786440 | tf_op jit(solution)/shard_map/ppermute | solution.py:52

commit v6 on v5

--- a/solution.py
+++ b/solution.py
@@ -290,6 +290,8 @@
 ):
     far = [1 << b for b in reversed(range(3, devices.bit_length() - 1))]
     near = (4, 2, 6)
+    near_last = (2, 4, 6)
+    near_sums = (2, 4, 6)
     own = tokens.shape[0]
     row = lambda array: array.reshape(1, -1)
     encoder_bias, latent_first, latent_second, decoder_bias, feature_first, feature_second = map(
@@ -305,13 +307,16 @@
     for bit in far[1:]:
         column = lax.optimization_barrier(jnp.concatenate([column, swap(column, bit, devices)], axis=0))
     rows = column.shape[0]
-    column = lax.optimization_barrier(jnp.concatenate([column] + [swap(column, bits, devices) for bits in near], axis=0))
+    blocks = {bits: swap(column, bits, devices) for bits in near}
+    last_column = lax.optimization_barrier(jnp.concatenate([column] + [blocks[bits] for bits in near_last], axis=0))
+    column = lax.optimization_barrier(jnp.concatenate([column] + [blocks[bits] for bits in near], axis=0))
     part, *sent = forward(column, encoder, mate_encoder, bias, mate_bias, decoder, mate_decoder)
-    received = {bits: swap(piece, bits, devices) for bits, piece in reversed(list(zip(near, sent)))}
+    sent = dict(zip(near, sent))
+    received = [swap(sent[bits], bits, devices) for bits in near_sums]
     moments = load(encoder_first, encoder_second, decoder_first, decoder_second)
     received, moments = lax.optimization_barrier((received, moments))
-    for bits in (6, 4, 2):
-        part = part + received[bits].astype(f32)
+    for piece in received:
+        part = part + piece.astype(f32)
     for level in reversed(range(len(far))):
         part = lax.reduce_precision(part, 8, 7)
         piece = part.astype(bf16)
@@ -320,8 +325,9 @@
         pieces = [other[start ^ size : (start ^ size) + size] for start in range(0, rows, size)]
         part = part + jnp.concatenate(pieces, axis=0).astype(f32)
     errors = (part + decoder_bias - column[:rows].astype(f32)).astype(bf16)
+    column = last_column
     errors, column = lax.optimization_barrier((errors, column))
-    received = [swap(errors, bits, devices) for bits in near]
+    received = [swap(errors, bits, devices) for bits in near_last]
     prepared = prepare(column, swap(column, 1, devices), encoder, bias, decoder)
     errors = lax.optimization_barrier(jnp.concatenate([errors] + received, axis=0))
     errors = jnp.concatenate([errors, swap(errors, 1, devices)], axis=0)

time: 41.3 us -> 40.4 us (0.978)
  waiting for transfers between devices: 11.9 us -> 11.1 us
    ppermute x16, waiting for transfers between devices: 11.9 us -> 11.1 us  [swap(): return lax.ppermute(x, 'dict', [(i, i ^ bit) for i in range(devices)])]
where the time goes in v6:
time: 40.4 us; the launch traced here: 40.2 us
  starting transfers between devices  18.1 us (45%)
  waiting for transfers between devices  11.1 us (27%)
  Pallas kernels  9.93 us (25%)
  between operations  0.85 us (2%)
    ppermute x16, starting transfers between devices, swap(): return lax.ppermute(x, 'dict', [(i, i ^ bit) for i in range(devices)])  18.1 us
    ppermute x16, waiting for transfers between devices, swap(): return lax.ppermute(x, 'dict', [(i, i ^ bit) for i in range(devices)])  11.1 us
    pallas_call x3, Pallas kernels, load(): pl.pallas_call(load_kernel, in_specs=[ANY_SPEC] * len(arrays), out_specs=...  4.82 us
    pallas_call x1, Pallas kernels, update(): pl.pallas_call(functools.partial(update_kernel, own), in_specs=[VMEM_SPEC...  3.59 us
    pallas_call x1, Pallas kernels, forward(): pl.pallas_call(forward_kernel, in_specs=[VMEM_SPEC] * 7, out_specs=[VMEM_...  1 us
  transfers between devices with their start and end apart: 16, of which 10 were waited for; matrix products, arithmetic and copies ran while one was open for 0% of the time, Pallas kernels for 13%

profile of v6, /device:TPU:0, one launch (start us, length us, event | category | flops | bytes accessed | tf_op | source)
XLA Modules:
  0.0 40.2 jit_solution(10529960364583288572)
XLA Ops:
  0.7 4.1 %collective-permute-start = (bf16[4,4096]{1,0:T(4,128)(2,1)}, bf16[4,4096]{1,0:T(4,128)(2,1)S(1)}, u32[]{:S(2)}, u32[]{:S(2)}) collective-permute-start(bf16[4,4096]{1,0:T(4,128)(2,1)} %refs_0_.3), channel_id=1, source_target_pairs={{0,8},{1,9},{2,10},{3,11},{4,12},{5,13},{6,14},{7,15},{8,0},{9,1},... | collective-permute-start | bytes 98312 | tf_op jit(solution)/shard_map/ppermute | solution.py:52
  4.8 0.5 %collective-permute-start.6 = (bf16[82,4096]{1,0:T(8,128)(2,1)}, bf16[82,4096]{1,0:T(8,128)(2,1)S(1)}, u32[]{:S(2)}, u32[]{:S(2)}) collective-permute-start(bf16[82,4096]{1,0:T(8,128)(2,1)} %refs_1_.2), channel_id=1, source_target_pairs={{0,1},{1,0},{2,3},{3,2},{4,5},{5,4},{6,7},{7,6},{8,9},{9,8},{10,11... | collective-permute-start | bytes 2015240 | tf_op jit(solution)/shard_map/ppermute | solution.py:52
  5.3 0.8 %shard_map.220 = bf16[4,4096]{1,0:T(4,128)(2,1)S(1)} custom-call(bf16[4,4096]{1,0:T(4,128)(2,1)} %refs_0_.3), custom_call_target="tpu_custom_call" | custom-call | bytes 65536 | tf_op jit(solution)/shard_map/pallas_call | solution.py:77
  6.0 1.2 %collective-permute-done = bf16[4,4096]{1,0:T(4,128)(2,1)S(1)} collective-permute-done((bf16[4,4096]{1,0:T(4,128)(2,1)}, bf16[4,4096]{1,0:T(4,128)(2,1)S(1)}, u32[]{:S(2)}, u32[]{:S(2)}) %collective-permute-start) | collective-permute-done | bytes 32800 | tf_op jit(solution)/shard_map/ppermute | solution.py:52
  7.3 2.6 %collective-permute-start.3 = (bf16[8,4096]{1,0:T(8,128)(2,1)S(1)}, bf16[8,4096]{1,0:T(8,128)(2,1)S(1)}, u32[]{:S(2)}, u32[]{:S(2)}) collective-permute-start(bf16[8,4096]{1,0:T(8,128)(2,1)S(1)} %pad_maximum_fusion.6), channel_id=1, source_target_pairs={{0,6},{1,7},{2,4},{3,5},{4,2},{5,3},{6,0},{7,1},{8,14},{9,15},{10,... | collective-permute-start | bytes 196616 | tf_op jit(solution)/shard_map/ppermute | solution.py:52
  9.8 0.5 %collective-permute-start.2 = (bf16[8,4096]{1,0:T(8,128)(2,1)S(1)}, bf16[8,4096]{1,0:T(8,128)(2,1)S(1)}, u32[]{:S(2)}, u32[]{:S(2)}) collective-permute-start(bf16[8,4096]{1,0:T(8,128)(2,1)S(1)} %pad_maximum_fusion.6), channel_id=1, source_target_pairs={{0,2},{1,3},{2,0},{3,1},{4,6},{5,7},{6,4},{7,5},{8,10},{9,11},{10,... | collective-permute-start | bytes 196616 | tf_op jit(solution)/shard_map/ppermute | solution.py:52
  10.3 0.5 %collective-permute-start.1 = (bf16[8,4096]{1,0:T(8,128)(2,1)S(1)}, bf16[8,4096]{1,0:T(8,128)(2,1)S(1)}, u32[]{:S(2)}, u32[]{:S(2)}) collective-permute-start(bf16[8,4096]{1,0:T(8,128)(2,1)S(1)} %pad_maximum_fusion.6), channel_id=1, source_target_pairs={{0,4},{1,5},{2,6},{3,7},{4,0},{5,1},{6,2},{7,3},{8,12},{9,13},{10,... | collective-permute-start | bytes 196616 | tf_op jit(solution)/shard_map/ppermute | solution.py:52
  10.8 1.4 %shard_map.221 = (bf16[82,4096]{1,0:T(8,128)(2,1)S(1)}, bf16[82,4096]{1,0:T(8,128)(2,1)S(1)}, f32[1,82]{1,0:T(1,128)S(1)}) custom-call(bf16[82,4096]{1,0:T(8,128)(2,1)} %refs_0_.4, bf16[82,4096]{1,0:T(8,128)(2,1)} %refs_1_.2, f32[1,82]{1,0:T(1,128)} %bitcast.17), custom_call_target="tpu_custom_call" | custom-call | bytes 2687632 | tf_op jit(solution)/shard_map/pallas_call | solution.py:77
  12.2 0.7 %collective-permute-done.3 = bf16[8,4096]{1,0:T(8,128)(2,1)S(1)} collective-permute-done((bf16[8,4096]{1,0:T(8,128)(2,1)S(1)}, bf16[8,4096]{1,0:T(8,128)(2,1)S(1)}, u32[]{:S(2)}, u32[]{:S(2)}) %collective-permute-start.3) | collective-permute-done | bytes 65568 | tf_op jit(solution)/shard_map/ppermute | solution.py:52
  12.9 1.2 %collective-permute-done.2 = bf16[8,4096]{1,0:T(8,128)(2,1)S(1)} collective-permute-done((bf16[8,4096]{1,0:T(8,128)(2,1)S(1)}, bf16[8,4096]{1,0:T(8,128)(2,1)S(1)}, u32[]{:S(2)}, u32[]{:S(2)}) %collective-permute-start.2) | collective-permute-done | bytes 65568 | tf_op jit(solution)/shard_map/ppermute | solution.py:52
  14.1 0.5 %collective-permute-done.1 = bf16[8,4096]{1,0:T(8,128)(2,1)S(1)} collective-permute-done((bf16[8,4096]{1,0:T(8,128)(2,1)S(1)}, bf16[8,4096]{1,0:T(8,128)(2,1)S(1)}, u32[]{:S(2)}, u32[]{:S(2)}) %collective-permute-start.1) | collective-permute-done | bytes 65568 | tf_op jit(solution)/shard_map/ppermute | solution.py:52
  14.7 1.0 %shard_map.222 = (f32[8,4096]{1,0:T(8,128)S(1)}, bf16[8,4096]{1,0:T(8,128)(2,1)S(1)}, bf16[8,4096]{1,0:T(8,128)(2,1)S(1)}, bf16[8,4096]{1,0:T(8,128)(2,1)S(1)}) custom-call(bf16[32,4096]{1,0:T(8,128)(2,1)S(1)} %get-tuple-element.87.tokens_ref, bf16[82,4096]{1,0:T(8,128)(2,1)S(1)} %get-tuple-element.49.encoder_ref, ...), custom_call_target="tpu_custom_call" | custom-call | flops 85983232 | bytes 2686976 | tf_op jit(solution)/shard_map/pallas_call | solution.py:124
  15.7 1.6 %collective-permute-start.7 = (bf16[8,4096]{1,0:T(8,128)(2,1)S(1)}, bf16[8,4096]{1,0:T(8,128)(2,1)S(1)}, u32[]{:S(2)}, u32[]{:S(2)}) collective-permute-start(bf16[8,4096]{1,0:T(8,128)(2,1)S(1)} %get-tuple-element.53), channel_id=1, source_target_pairs={{0,2},{1,3},{2,0},{3,1},{4,6},{5,7},{6,4},{7,5},{8,10},{9,11},{10,... | collective-permute-start | bytes 196616 | tf_op jit(solution)/shard_map/ppermute | solution.py:52
  17.3 0.7 %collective-permute-start.8 = (bf16[8,4096]{1,0:T(8,128)(2,1)S(1)}, bf16[8,4096]{1,0:T(8,128)(2,1)S(1)}, u32[]{:S(2)}, u32[]{:S(2)}) collective-permute-start(bf16[8,4096]{1,0:T(8,128)(2,1)S(1)} %get-tuple-element.54), channel_id=1, source_target_pairs={{0,4},{1,5},{2,6},{3,7},{4,0},{5,1},{6,2},{7,3},{8,12},{9,13},{10,... | collective-permute-start | bytes 196616 | tf_op jit(solution)/shard_map/ppermute | solution.py:52
  17.9 1.3 %collective-permute-start.9 = (bf16[8,4096]{1,0:T(8,128)(2,1)S(1)}, bf16[8,4096]{1,0:T(8,128)(2,1)S(1)}, u32[]{:S(2)}, u32[]{:S(2)}) collective-permute-start(bf16[8,4096]{1,0:T(8,128)(2,1)S(1)} %get-tuple-element.55), channel_id=1, source_target_pairs={{0,6},{1,7},{2,4},{3,5},{4,2},{5,3},{6,0},{7,1},{8,14},{9,15},{10,... | collective-permute-start | bytes 196616 | tf_op jit(solution)/shard_map/ppermute | solution.py:52
  19.2 2.7 %shard_map.223 = (f32[82,4096]{1,0:T(8,128)S(1)}, f32[82,4096]{1,0:T(8,128)S(1)}, f32[82,4096]{1,0:T(8,128)S(1)}, f32[82,4096]{1,0:T(8,128)S(1)}) custom-call(f32[82,4096]{1,0:T(8,128)} %refs_0_.5, f32[82,4096]{1,0:T(8,128)} %refs_1_.3, f32[82,4096]{1,0:T(8,128)} %refs_2_.1, f32[82,4096]{1,0:T(8,128)} %refs_3_.1), custom_call_target="tpu_custom_call" | custom-call | bytes 10747904 | tf_op jit(solution)/shard_map/pallas_call | solution.py:77
  22.0 1.1 %collective-permute-done.9 = bf16[8,4096]{1,0:T(8,128)(2,1)S(1)} collective-permute-done((bf16[8,4096]{1,0:T(8,128)(2,1)S(1)}, bf16[8,4096]{1,0:T(8,128)(2,1)S(1)}, u32[]{:S(2)}, u32[]{:S(2)}) %collective-permute-start.9) | collective-permute-done | bytes 65568 | tf_op jit(solution)/shard_map/ppermute | solution.py:52
  23.1 2.7 %collective-permute-start.10 = (bf16[8,4096]{1,0:T(8,128)(2,1)S(1)}, bf16[8,4096]{1,0:T(8,128)(2,1)S(1)}, u32[]{:S(2)}, u32[]{:S(2)}) collective-permute-start(bf16[8,4096]{1,0:T(8,128)(2,1)S(1)} %fusion.2), channel_id=1, source_target_pairs={{0,8},{1,9},{2,10},{3,11},{4,12},{5,13},{6,14},{7,15},{8,0},{9,1},... | collective-permute-start | bytes 196616 | tf_op jit(solution)/shard_map/ppermute | solution.py:52
  25.9 2.5 %collective-permute-done.10 = bf16[8,4096]{1,0:T(8,128)(2,1)S(1)} collective-permute-done((bf16[8,4096]{1,0:T(8,128)(2,1)S(1)}, bf16[8,4096]{1,0:T(8,128)(2,1)S(1)}, u32[]{:S(2)}, u32[]{:S(2)}) %collective-permute-start.10) | collective-permute-done | bytes 65568 | tf_op jit(solution)/shard_map/ppermute | solution.py:52
  28.4 0.1 subtract_convert_fusion
  28.5 1.5 %collective-permute-start.13 = (bf16[8,4096]{1,0:T(8,128)(2,1)S(1)}, bf16[8,4096]{1,0:T(8,128)(2,1)S(1)}, u32[]{:S(2)}, u32[]{:S(2)}) collective-permute-start(bf16[8,4096]{1,0:T(8,128)(2,1)S(1)} %subtract_convert_fusion), channel_id=1, source_target_pairs={{0,6},{1,7},{2,4},{3,5},{4,2},{5,3},{6,0},{7,1},{8,14},{9,15},{10,... | collective-permute-start | bytes 196616 | tf_op jit(solution)/shard_map/ppermute | solution.py:52
  30.0 0.6 %collective-permute-start.12 = (bf16[8,4096]{1,0:T(8,128)(2,1)S(1)}, bf16[8,4096]{1,0:T(8,128)(2,1)S(1)}, u32[]{:S(2)}, u32[]{:S(2)}) collective-permute-start(bf16[8,4096]{1,0:T(8,128)(2,1)S(1)} %subtract_convert_fusion), channel_id=1, source_target_pairs={{0,4},{1,5},{2,6},{3,7},{4,0},{5,1},{6,2},{7,3},{8,12},{9,13},{10,... | collective-permute-start | bytes 196616 | tf_op jit(solution)/shard_map/ppermute | solution.py:52
  30.6 1.4 %collective-permute-start.11 = (bf16[8,4096]{1,0:T(8,128)(2,1)S(1)}, bf16[8,4096]{1,0:T(8,128)(2,1)S(1)}, u32[]{:S(2)}, u32[]{:S(2)}) collective-permute-start(bf16[8,4096]{1,0:T(8,128)(2,1)S(1)} %subtract_convert_fusion), channel_id=1, source_target_pairs={{0,2},{1,3},{2,0},{3,1},{4,6},{5,7},{6,4},{7,5},{8,10},{9,11},{10,... | collective-permute-start | bytes 196616 | tf_op jit(solution)/shard_map/ppermute | solution.py:52
  32.1 1.7 %collective-permute-done.13 = bf16[8,4096]{1,0:T(8,128)(2,1)S(1)} collective-permute-done((bf16[8,4096]{1,0:T(8,128)(2,1)S(1)}, bf16[8,4096]{1,0:T(8,128)(2,1)S(1)}, u32[]{:S(2)}, u32[]{:S(2)}) %collective-permute-start.13) | collective-permute-done | bytes 65568 | tf_op jit(solution)/shard_map/ppermute | solution.py:52
  33.7 0.6 %collective-permute-done.12 = bf16[8,4096]{1,0:T(8,128)(2,1)S(1)} collective-permute-done((bf16[8,4096]{1,0:T(8,128)(2,1)S(1)}, bf16[8,4096]{1,0:T(8,128)(2,1)S(1)}, u32[]{:S(2)}, u32[]{:S(2)}) %collective-permute-start.12) | collective-permute-done | bytes 65568 | tf_op jit(solution)/shard_map/ppermute | solution.py:52
  34.3 0.6 %collective-permute-done.11 = bf16[8,4096]{1,0:T(8,128)(2,1)S(1)} collective-permute-done((bf16[8,4096]{1,0:T(8,128)(2,1)S(1)}, bf16[8,4096]{1,0:T(8,128)(2,1)S(1)}, u32[]{:S(2)}, u32[]{:S(2)}) %collective-permute-start.11) | collective-permute-done | bytes 65568 | tf_op jit(solution)/shard_map/ppermute | solution.py:52
  34.9 0.0 copy-start.2
  34.9 0.0 copy-start.3
  35.0 0.1 collective-permute-start.14
  35.1 0.5 %shard_map.224 = (bf16[64,4096]{1,0:T(8,128)(2,1)S(1)}, f32[82,64]{1,0:T(8,128)S(1)}, bf16[82,64]{1,0:T(8,128)(2,1)S(1)}, f32[82,1]{1,0:T(8,128)S(1)}, f32[82,1]{1,0:T(8,128)S(1)}) custom-call(bf16[32,4096]{1,0:T(8,128)(2,1)S(1)} %get-tuple-element.64.tokens_ref, bf16[32,4096]{1,0:T(8,128)(2,1)S(1)} %collective-permute-done.15.mate_tokens_ref, ...), custom_call_target="tpu_custom_call" | custom-call | flops 42991616 | bytes 3358720 | tf_op jit(solution)/shard_map/pallas_call | solution.py:154
  35.6 1.0 %collective-permute-done.14 = bf16[32,4096]{1,0:T(8,128)(2,1)S(1)} collective-permute-done((bf16[32,4096]{1,0:T(8,128)(2,1)S(1)}, bf16[32,4096]{1,0:T(8,128)(2,1)S(1)}, u32[]{:S(2)}, u32[]{:S(2)}) %collective-permute-start.14) | collective-permute-done | bytes 262176 | tf_op jit(solution)/shard_map/ppermute | solution.py:52
  36.6 3.6 %shard_map.225 = (bf16[82,4096]{1,0:T(8,128)(2,1)}, bf16[82,4096]{1,0:T(8,128)(2,1)}, f32[82,4096]{1,0:T(8,128)}, f32[82,4096]{1,0:T(8,128)}, f32[82,4096]{1,0:T...) custom-call(bf16[64,4096]{1,0:T(8,128)(2,1)S(1)} %pad_maximum_fusion, ...), custom_call_target="tpu_custom_call" | custom-call | flops 128974848 | bytes 13434880 | tf_op jit(solution)/shard_map/pallas_call | solution.py:259
  (25 shorter events, 0.2 us)
Async XLA Ops:
  0.6 12.2 %copy-start.5 = (f32[82]{0:T(128)S(1)}, f32[82]{0:T(128)}, u32[]{:S(2)}) copy-start(f32[82]{0:T(128)} %param.15) | copy-start | bytes 988
  0.7 6.6 %collective-permute-start = (bf16[4,4096]{1,0:T(4,128)(2,1)}, bf16[4,4096]{1,0:T(4,128)(2,1)S(1)}, u32[]{:S(2)}, u32[]{:S(2)}) collective-permute-start(bf16[4,4096]{1,0:T(4,128)(2,1)} %refs_0_.3), channel_id=1, source_target_pairs={{0,8},{1,9},{2,10},{3,11},{4,12},{5,13},{6,14},{7,15},{8,0},{9,1},... | collective-permute-start | bytes 98312 | tf_op jit(solution)/shard_map/ppermute | solution.py:52
  4.8 9.9 %collective-permute-start.4 = (bf16[82,4096]{1,0:T(8,128)(2,1)}, bf16[82,4096]{1,0:T(8,128)(2,1)S(1)}, u32[]{:S(2)}, u32[]{:S(2)}) collective-permute-start(bf16[82,4096]{1,0:T(8,128)(2,1)} %refs_0_.4), channel_id=1, source_target_pairs={{0,1},{1,0},{2,3},{3,2},{4,5},{5,4},{6,7},{7,6},{8,9},{9,8},{10,11... | collective-permute-start | bytes 2015240 | tf_op jit(solution)/shard_map/ppermute | solution.py:52
  4.8 9.9 %collective-permute-start.6 = (bf16[82,4096]{1,0:T(8,128)(2,1)}, bf16[82,4096]{1,0:T(8,128)(2,1)S(1)}, u32[]{:S(2)}, u32[]{:S(2)}) collective-permute-start(bf16[82,4096]{1,0:T(8,128)(2,1)} %refs_1_.2), channel_id=1, source_target_pairs={{0,1},{1,0},{2,3},{3,2},{4,5},{5,4},{6,7},{7,6},{8,9},{9,8},{10,11... | collective-permute-start | bytes 2015240 | tf_op jit(solution)/shard_map/ppermute | solution.py:52
  7.3 5.6 %collective-permute-start.3 = (bf16[8,4096]{1,0:T(8,128)(2,1)S(1)}, bf16[8,4096]{1,0:T(8,128)(2,1)S(1)}, u32[]{:S(2)}, u32[]{:S(2)}) collective-permute-start(bf16[8,4096]{1,0:T(8,128)(2,1)S(1)} %pad_maximum_fusion.6), channel_id=1, source_target_pairs={{0,6},{1,7},{2,4},{3,5},{4,2},{5,3},{6,0},{7,1},{8,14},{9,15},{10,... | collective-permute-start | bytes 196616 | tf_op jit(solution)/shard_map/ppermute | solution.py:52
  9.8 4.3 %collective-permute-start.2 = (bf16[8,4096]{1,0:T(8,128)(2,1)S(1)}, bf16[8,4096]{1,0:T(8,128)(2,1)S(1)}, u32[]{:S(2)}, u32[]{:S(2)}) collective-permute-start(bf16[8,4096]{1,0:T(8,128)(2,1)S(1)} %pad_maximum_fusion.6), channel_id=1, source_target_pairs={{0,2},{1,3},{2,0},{3,1},{4,6},{5,7},{6,4},{7,5},{8,10},{9,11},{10,... | collective-permute-start | bytes 196616 | tf_op jit(solution)/shard_map/ppermute | solution.py:52
  10.3 4.3 %collective-permute-start.1 = (bf16[8,4096]{1,0:T(8,128)(2,1)S(1)}, bf16[8,4096]{1,0:T(8,128)(2,1)S(1)}, u32[]{:S(2)}, u32[]{:S(2)}) collective-permute-start(bf16[8,4096]{1,0:T(8,128)(2,1)S(1)} %pad_maximum_fusion.6), channel_id=1, source_target_pairs={{0,4},{1,5},{2,6},{3,7},{4,0},{5,1},{6,2},{7,3},{8,12},{9,13},{10,... | collective-permute-start | bytes 196616 | tf_op jit(solution)/shard_map/ppermute | solution.py:52
  12.9 1.8 %collective-permute-start.5 = (f32[1,82]{1,0:T(1,128)S(1)}, f32[1,82]{1,0:T(1,128)S(1)}, u32[]{:S(2)}, u32[]{:S(2)}) collective-permute-start(f32[1,82]{1,0:T(1,128)S(1)} %bitcast.18), channel_id=1, source_target_pairs={{0,1},{1,0},{2,3},{3,2},{4,5},{5,4},{6,7},{7,6},{8,9},{9,8},{10,11... | collective-permute-start | bytes 992 | tf_op jit(solution)/shard_map/ppermute | solution.py:52
  15.7 6.3 %collective-permute-start.7 = (bf16[8,4096]{1,0:T(8,128)(2,1)S(1)}, bf16[8,4096]{1,0:T(8,128)(2,1)S(1)}, u32[]{:S(2)}, u32[]{:S(2)}) collective-permute-start(bf16[8,4096]{1,0:T(8,128)(2,1)S(1)} %get-tuple-element.53), channel_id=1, source_target_pairs={{0,2},{1,3},{2,0},{3,1},{4,6},{5,7},{6,4},{7,5},{8,10},{9,11},{10,... | collective-permute-start | bytes 196616 | tf_op jit(solution)/shard_map/ppermute | solution.py:52
  17.3 4.7 %collective-permute-start.8 = (bf16[8,4096]{1,0:T(8,128)(2,1)S(1)}, bf16[8,4096]{1,0:T(8,128)(2,1)S(1)}, u32[]{:S(2)}, u32[]{:S(2)}) collective-permute-start(bf16[8,4096]{1,0:T(8,128)(2,1)S(1)} %get-tuple-element.54), channel_id=1, source_target_pairs={{0,4},{1,5},{2,6},{3,7},{4,0},{5,1},{6,2},{7,3},{8,12},{9,13},{10,... | collective-permute-start | bytes 196616 | tf_op jit(solution)/shard_map/ppermute | solution.py:52
  17.9 10.5 %copy-start = (f32[4096]{0:T(1024)S(1)}, f32[4096]{0:T(1024)}, u32[]{:S(2)}) copy-start(f32[4096]{0:T(1024)} %param.17) | copy-start | bytes 49156
  17.9 5.2 %collective-permute-start.9 = (bf16[8,4096]{1,0:T(8,128)(2,1)S(1)}, bf16[8,4096]{1,0:T(8,128)(2,1)S(1)}, u32[]{:S(2)}, u32[]{:S(2)}) collective-permute-start(bf16[8,4096]{1,0:T(8,128)(2,1)S(1)} %get-tuple-element.55), channel_id=1, source_target_pairs={{0,6},{1,7},{2,4},{3,5},{4,2},{5,3},{6,0},{7,1},{8,14},{9,15},{10,... | collective-permute-start | bytes 196616 | tf_op jit(solution)/shard_map/ppermute | solution.py:52
  23.1 5.2 %collective-permute-start.10 = (bf16[8,4096]{1,0:T(8,128)(2,1)S(1)}, bf16[8,4096]{1,0:T(8,128)(2,1)S(1)}, u32[]{:S(2)}, u32[]{:S(2)}) collective-permute-start(bf16[8,4096]{1,0:T(8,128)(2,1)S(1)} %fusion.2), channel_id=1, source_target_pairs={{0,8},{1,9},{2,10},{3,11},{4,12},{5,13},{6,14},{7,15},{8,0},{9,1},... | collective-permute-start | bytes 196616 | tf_op jit(solution)/shard_map/ppermute | solution.py:52
  28.5 5.2 %collective-permute-start.13 = (bf16[8,4096]{1,0:T(8,128)(2,1)S(1)}, bf16[8,4096]{1,0:T(8,128)(2,1)S(1)}, u32[]{:S(2)}, u32[]{:S(2)}) collective-permute-start(bf16[8,4096]{1,0:T(8,128)(2,1)S(1)} %subtract_convert_fusion), channel_id=1, source_target_pairs={{0,6},{1,7},{2,4},{3,5},{4,2},{5,3},{6,0},{7,1},{8,14},{9,15},{10,... | collective-permute-start | bytes 196616 | tf_op jit(solution)/shard_map/ppermute | solution.py:52
  30.0 4.3 %collective-permute-start.12 = (bf16[8,4096]{1,0:T(8,128)(2,1)S(1)}, bf16[8,4096]{1,0:T(8,128)(2,1)S(1)}, u32[]{:S(2)}, u32[]{:S(2)}) collective-permute-start(bf16[8,4096]{1,0:T(8,128)(2,1)S(1)} %subtract_convert_fusion), channel_id=1, source_target_pairs={{0,4},{1,5},{2,6},{3,7},{4,0},{5,1},{6,2},{7,3},{8,12},{9,13},{10,... | collective-permute-start | bytes 196616 | tf_op jit(solution)/shard_map/ppermute | solution.py:52
  30.6 4.3 %collective-permute-start.11 = (bf16[8,4096]{1,0:T(8,128)(2,1)S(1)}, bf16[8,4096]{1,0:T(8,128)(2,1)S(1)}, u32[]{:S(2)}, u32[]{:S(2)}) collective-permute-start(bf16[8,4096]{1,0:T(8,128)(2,1)S(1)} %subtract_convert_fusion), channel_id=1, source_target_pairs={{0,2},{1,3},{2,0},{3,1},{4,6},{5,7},{6,4},{7,5},{8,10},{9,11},{10,... | collective-permute-start | bytes 196616 | tf_op jit(solution)/shard_map/ppermute | solution.py:52
  32.1 3.0 %collective-permute-start.15 = (bf16[32,4096]{1,0:T(8,128)(2,1)S(1)}, bf16[32,4096]{1,0:T(8,128)(2,1)S(1)}, u32[]{:S(2)}, u32[]{:S(2)}) collective-permute-start(bf16[32,4096]{1,0:T(8,128)(2,1)S(1)} %get-tuple-element.64.tokens_ref), channel_id=1, source_target_pairs={{0,1},{1,0},{2,3},{3,2},{4,5},{5,4},{6,7},{7,6},{8,9},{9,8},{10,11... | collective-permute-start | bytes 786440 | tf_op jit(solution)/shard_map/ppermute | solution.py:52
  34.9 1.7 %copy-start.1 = (f32[4096]{0:T(1024)S(1)}, f32[4096]{0:T(1024)}, u32[]{:S(2)}) copy-start(f32[4096]{0:T(1024)} %param.24) | copy-start | bytes 49156
  34.9 1.7 %copy-start.2 = (f32[4096]{0:T(1024)S(1)}, f32[4096]{0:T(1024)}, u32[]{:S(2)}) copy-start(f32[4096]{0:T(1024)} %param.25) | copy-start | bytes 49156
  34.9 1.7 %copy-start.3 = (f32[82]{0:T(128)S(1)}, f32[82]{0:T(128)}, u32[]{:S(2)}) copy-start(f32[82]{0:T(128)} %param.22) | copy-start | bytes 988
  34.9 1.7 %copy-start.4 = (f32[82]{0:T(128)S(1)}, f32[82]{0:T(128)}, u32[]{:S(2)}) copy-start(f32[82]{0:T(128)} %param.23) | copy-start | bytes 988
  35.0 1.6 %collective-permute-start.14 = (bf16[32,4096]{1,0:T(8,128)(2,1)S(1)}, bf16[32,4096]{1,0:T(8,128)(2,1)S(1)}, u32[]{:S(2)}, u32[]{:S(2)}) collective-permute-start(bf16[32,4096]{1,0:T(8,128)(2,1)S(1)} %pad_maximum_fusion.5), channel_id=1, source_target_pairs={{0,1},{1,0},{2,3},{3,2},{4,5},{5,4},{6,7},{7,6},{8,9},{9,8},{10,11... | collective-permute-start | bytes 786440 | tf_op jit(solution)/shard_map/ppermute | solution.py:52

commit v7 on v6

--- a/solution.py
+++ b/solution.py
@@ -208,7 +208,9 @@
             yield pl.ds(start, width)
             start += width
 
+    act_grad = floor_ref[...]
     for columns in blocks(DECODER_BLOCKS):
+        act_grad = act_grad + nt_dot(decoder_ref[:, columns], errors_ref[:, columns])
         weight = decoder_ref[:, columns].astype(f32)
         grad = jnp.dot(act_ref[...], errors_ref[:, columns], preferred_element_type=f32) + pull_ref[...] * weight
         new, slots[4][:, columns], slots[5][:, columns] = adam_update(
@@ -218,14 +220,9 @@
         for which in (1, 4, 5):
             send(which, columns)
 
-    grad = (nt_dot(decoder_ref[...], errors_ref[...]) + floor_ref[...]) * slope_ref[...]
+    grad = act_grad * slope_ref[...]
     pre_ref[...] = grad.astype(bf16)
-    total = turn(jnp.sum(grad, axis=1, keepdims=True))
-    slots[6][...], slots[7][...], slots[8][...] = adam_update(
-        encoder_bias_ref[...], total, latent_first_ref[...], latent_second_ref[...]
-    )
-    for which in range(6, 9):
-        send(which)
+    latent_grad = jnp.sum(grad, axis=1, keepdims=True)
 
     for columns in blocks(ENCODER_BLOCKS):
         grad = jnp.dot(pre_ref[...], tokens_ref[:, columns], preferred_element_type=f32)
@@ -235,6 +232,12 @@
         slots[0][:, columns] = new.astype(bf16)
         for which in (0, 2, 3):
             send(which, columns)
+    total = turn(latent_grad)
+    slots[6][...], slots[7][...], slots[8][...] = adam_update(
+        encoder_bias_ref[...], total, latent_first_ref[...], latent_second_ref[...]
+    )
+    for which in range(6, 9):
+        send(which)
     rows = errors_ref[...].astype(f32)
     while rows.shape[0] > own:
         half = rows.shape[0] // 2

time: 40.4 us -> 40.2 us (level)
  no operation moved by 1% of the time
where the time goes in v7:
time: 40.2 us; the launch traced here: 40 us
  starting transfers between devices  18.1 us (45%)
  waiting for transfers between devices  11.1 us (28%)
  Pallas kernels  9.69 us (24%)
  between operations  0.85 us (2%)
    ppermute x16, starting transfers between devices, swap(): return lax.ppermute(x, 'dict', [(i, i ^ bit) for i in range(devices)])  18.1 us
    ppermute x16, waiting for transfers between devices, swap(): return lax.ppermute(x, 'dict', [(i, i ^ bit) for i in range(devices)])  11.1 us
    pallas_call x3, Pallas kernels, load(): pl.pallas_call(load_kernel, in_specs=[ANY_SPEC] * len(arrays), out_specs=...  4.82 us
    pallas_call x1, Pallas kernels, update(): pl.pallas_call(functools.partial(update_kernel, own), in_specs=[VMEM_SPEC...  3.35 us
    pallas_call x1, Pallas kernels, forward(): pl.pallas_call(forward_kernel, in_specs=[VMEM_SPEC] * 7, out_specs=[VMEM_...  1 us
  transfers between devices with their start and end apart: 16, of which 10 were waited for; matrix products, arithmetic and copies ran while one was open for 0% of the time, Pallas kernels for 13%

profile of v7, /device:TPU:0, one launch (start us, length us, event | category | flops | bytes accessed | tf_op | source)
XLA Modules:
  0.0 40.0 jit_solution(15209719756325489997)
XLA Ops:
  0.6 0.0 copy-start.5
  0.7 4.1 %collective-permute-start = (bf16[4,4096]{1,0:T(4,128)(2,1)}, bf16[4,4096]{1,0:T(4,128)(2,1)S(1)}, u32[]{:S(2)}, u32[]{:S(2)}) collective-permute-start(bf16[4,4096]{1,0:T(4,128)(2,1)} %refs_0_.3), channel_id=1, source_target_pairs={{0,8},{1,9},{2,10},{3,11},{4,12},{5,13},{6,14},{7,15},{8,0},{9,1},... | collective-permute-start | bytes 98312 | tf_op jit(solution)/shard_map/ppermute | solution.py:52
  4.8 0.5 %collective-permute-start.6 = (bf16[82,4096]{1,0:T(8,128)(2,1)}, bf16[82,4096]{1,0:T(8,128)(2,1)S(1)}, u32[]{:S(2)}, u32[]{:S(2)}) collective-permute-start(bf16[82,4096]{1,0:T(8,128)(2,1)} %refs_1_.2), channel_id=1, source_target_pairs={{0,1},{1,0},{2,3},{3,2},{4,5},{5,4},{6,7},{7,6},{8,9},{9,8},{10,11... | collective-permute-start | bytes 2015240 | tf_op jit(solution)/shard_map/ppermute | solution.py:52
  5.3 0.8 %shard_map.220 = bf16[4,4096]{1,0:T(4,128)(2,1)S(1)} custom-call(bf16[4,4096]{1,0:T(4,128)(2,1)} %refs_0_.3), custom_call_target="tpu_custom_call" | custom-call | bytes 65536 | tf_op jit(solution)/shard_map/pallas_call | solution.py:77
  6.0 1.2 %collective-permute-done = bf16[4,4096]{1,0:T(4,128)(2,1)S(1)} collective-permute-done((bf16[4,4096]{1,0:T(4,128)(2,1)}, bf16[4,4096]{1,0:T(4,128)(2,1)S(1)}, u32[]{:S(2)}, u32[]{:S(2)}) %collective-permute-start) | collective-permute-done | bytes 32800 | tf_op jit(solution)/shard_map/ppermute | solution.py:52
  7.3 2.6 %collective-permute-start.3 = (bf16[8,4096]{1,0:T(8,128)(2,1)S(1)}, bf16[8,4096]{1,0:T(8,128)(2,1)S(1)}, u32[]{:S(2)}, u32[]{:S(2)}) collective-permute-start(bf16[8,4096]{1,0:T(8,128)(2,1)S(1)} %pad_maximum_fusion.6), channel_id=1, source_target_pairs={{0,6},{1,7},{2,4},{3,5},{4,2},{5,3},{6,0},{7,1},{8,14},{9,15},{10,... | collective-permute-start | bytes 196616 | tf_op jit(solution)/shard_map/ppermute | solution.py:52
  9.8 0.5 %collective-permute-start.2 = (bf16[8,4096]{1,0:T(8,128)(2,1)S(1)}, bf16[8,4096]{1,0:T(8,128)(2,1)S(1)}, u32[]{:S(2)}, u32[]{:S(2)}) collective-permute-start(bf16[8,4096]{1,0:T(8,128)(2,1)S(1)} %pad_maximum_fusion.6), channel_id=1, source_target_pairs={{0,2},{1,3},{2,0},{3,1},{4,6},{5,7},{6,4},{7,5},{8,10},{9,11},{10,... | collective-permute-start | bytes 196616 | tf_op jit(solution)/shard_map/ppermute | solution.py:52
  10.3 0.5 %collective-permute-start.1 = (bf16[8,4096]{1,0:T(8,128)(2,1)S(1)}, bf16[8,4096]{1,0:T(8,128)(2,1)S(1)}, u32[]{:S(2)}, u32[]{:S(2)}) collective-permute-start(bf16[8,4096]{1,0:T(8,128)(2,1)S(1)} %pad_maximum_fusion.6), channel_id=1, source_target_pairs={{0,4},{1,5},{2,6},{3,7},{4,0},{5,1},{6,2},{7,3},{8,12},{9,13},{10,... | collective-permute-start | bytes 196616 | tf_op jit(solution)/shard_map/ppermute | solution.py:52
  10.8 1.4 %shard_map.221 = (bf16[82,4096]{1,0:T(8,128)(2,1)S(1)}, bf16[82,4096]{1,0:T(8,128)(2,1)S(1)}, f32[1,82]{1,0:T(1,128)S(1)}) custom-call(bf16[82,4096]{1,0:T(8,128)(2,1)} %refs_0_.4, bf16[82,4096]{1,0:T(8,128)(2,1)} %refs_1_.2, f32[1,82]{1,0:T(1,128)} %bitcast.17), custom_call_target="tpu_custom_call" | custom-call | bytes 2687632 | tf_op jit(solution)/shard_map/pallas_call | solution.py:77
  12.2 0.7 %collective-permute-done.3 = bf16[8,4096]{1,0:T(8,128)(2,1)S(1)} collective-permute-done((bf16[8,4096]{1,0:T(8,128)(2,1)S(1)}, bf16[8,4096]{1,0:T(8,128)(2,1)S(1)}, u32[]{:S(2)}, u32[]{:S(2)}) %collective-permute-start.3) | collective-permute-done | bytes 65568 | tf_op jit(solution)/shard_map/ppermute | solution.py:52
  12.9 1.2 %collective-permute-done.2 = bf16[8,4096]{1,0:T(8,128)(2,1)S(1)} collective-permute-done((bf16[8,4096]{1,0:T(8,128)(2,1)S(1)}, bf16[8,4096]{1,0:T(8,128)(2,1)S(1)}, u32[]{:S(2)}, u32[]{:S(2)}) %collective-permute-start.2) | collective-permute-done | bytes 65568 | tf_op jit(solution)/shard_map/ppermute | solution.py:52
  14.1 0.5 %collective-permute-done.1 = bf16[8,4096]{1,0:T(8,128)(2,1)S(1)} collective-permute-done((bf16[8,4096]{1,0:T(8,128)(2,1)S(1)}, bf16[8,4096]{1,0:T(8,128)(2,1)S(1)}, u32[]{:S(2)}, u32[]{:S(2)}) %collective-permute-start.1) | collective-permute-done | bytes 65568 | tf_op jit(solution)/shard_map/ppermute | solution.py:52
  14.7 1.0 %shard_map.222 = (f32[8,4096]{1,0:T(8,128)S(1)}, bf16[8,4096]{1,0:T(8,128)(2,1)S(1)}, bf16[8,4096]{1,0:T(8,128)(2,1)S(1)}, bf16[8,4096]{1,0:T(8,128)(2,1)S(1)}) custom-call(bf16[32,4096]{1,0:T(8,128)(2,1)S(1)} %get-tuple-element.87.tokens_ref, bf16[82,4096]{1,0:T(8,128)(2,1)S(1)} %get-tuple-element.49.encoder_ref, ...), custom_call_target="tpu_custom_call" | custom-call | flops 85983232 | bytes 2686976 | tf_op jit(solution)/shard_map/pallas_call | solution.py:124
  15.7 1.6 %collective-permute-start.7 = (bf16[8,4096]{1,0:T(8,128)(2,1)S(1)}, bf16[8,4096]{1,0:T(8,128)(2,1)S(1)}, u32[]{:S(2)}, u32[]{:S(2)}) collective-permute-start(bf16[8,4096]{1,0:T(8,128)(2,1)S(1)} %get-tuple-element.53), channel_id=1, source_target_pairs={{0,2},{1,3},{2,0},{3,1},{4,6},{5,7},{6,4},{7,5},{8,10},{9,11},{10,... | collective-permute-start | bytes 196616 | tf_op jit(solution)/shard_map/ppermute | solution.py:52
  17.3 0.7 %collective-permute-start.8 = (bf16[8,4096]{1,0:T(8,128)(2,1)S(1)}, bf16[8,4096]{1,0:T(8,128)(2,1)S(1)}, u32[]{:S(2)}, u32[]{:S(2)}) collective-permute-start(bf16[8,4096]{1,0:T(8,128)(2,1)S(1)} %get-tuple-element.54), channel_id=1, source_target_pairs={{0,4},{1,5},{2,6},{3,7},{4,0},{5,1},{6,2},{7,3},{8,12},{9,13},{10,... | collective-permute-start | bytes 196616 | tf_op jit(solution)/shard_map/ppermute | solution.py:52
  17.9 1.3 %collective-permute-start.9 = (bf16[8,4096]{1,0:T(8,128)(2,1)S(1)}, bf16[8,4096]{1,0:T(8,128)(2,1)S(1)}, u32[]{:S(2)}, u32[]{:S(2)}) collective-permute-start(bf16[8,4096]{1,0:T(8,128)(2,1)S(1)} %get-tuple-element.55), channel_id=1, source_target_pairs={{0,6},{1,7},{2,4},{3,5},{4,2},{5,3},{6,0},{7,1},{8,14},{9,15},{10,... | collective-permute-start | bytes 196616 | tf_op jit(solution)/shard_map/ppermute | solution.py:52
  19.2 2.7 %shard_map.223 = (f32[82,4096]{1,0:T(8,128)S(1)}, f32[82,4096]{1,0:T(8,128)S(1)}, f32[82,4096]{1,0:T(8,128)S(1)}, f32[82,4096]{1,0:T(8,128)S(1)}) custom-call(f32[82,4096]{1,0:T(8,128)} %refs_0_.5, f32[82,4096]{1,0:T(8,128)} %refs_1_.3, f32[82,4096]{1,0:T(8,128)} %refs_2_.1, f32[82,4096]{1,0:T(8,128)} %refs_3_.1), custom_call_target="tpu_custom_call" | custom-call | bytes 10747904 | tf_op jit(solution)/shard_map/pallas_call | solution.py:77
  22.0 1.1 %collective-permute-done.9 = bf16[8,4096]{1,0:T(8,128)(2,1)S(1)} collective-permute-done((bf16[8,4096]{1,0:T(8,128)(2,1)S(1)}, bf16[8,4096]{1,0:T(8,128)(2,1)S(1)}, u32[]{:S(2)}, u32[]{:S(2)}) %collective-permute-start.9) | collective-permute-done | bytes 65568 | tf_op jit(solution)/shard_map/ppermute | solution.py:52
  23.1 2.7 %collective-permute-start.10 = (bf16[8,4096]{1,0:T(8,128)(2,1)S(1)}, bf16[8,4096]{1,0:T(8,128)(2,1)S(1)}, u32[]{:S(2)}, u32[]{:S(2)}) collective-permute-start(bf16[8,4096]{1,0:T(8,128)(2,1)S(1)} %fusion.2), channel_id=1, source_target_pairs={{0,8},{1,9},{2,10},{3,11},{4,12},{5,13},{6,14},{7,15},{8,0},{9,1},... | collective-permute-start | bytes 196616 | tf_op jit(solution)/shard_map/ppermute | solution.py:52
  25.9 2.5 %collective-permute-done.10 = bf16[8,4096]{1,0:T(8,128)(2,1)S(1)} collective-permute-done((bf16[8,4096]{1,0:T(8,128)(2,1)S(1)}, bf16[8,4096]{1,0:T(8,128)(2,1)S(1)}, u32[]{:S(2)}, u32[]{:S(2)}) %collective-permute-start.10) | collective-permute-done | bytes 65568 | tf_op jit(solution)/shard_map/ppermute | solution.py:52
  28.4 0.1 subtract_convert_fusion
  28.5 1.5 %collective-permute-start.13 = (bf16[8,4096]{1,0:T(8,128)(2,1)S(1)}, bf16[8,4096]{1,0:T(8,128)(2,1)S(1)}, u32[]{:S(2)}, u32[]{:S(2)}) collective-permute-start(bf16[8,4096]{1,0:T(8,128)(2,1)S(1)} %subtract_convert_fusion), channel_id=1, source_target_pairs={{0,6},{1,7},{2,4},{3,5},{4,2},{5,3},{6,0},{7,1},{8,14},{9,15},{10,... | collective-permute-start | bytes 196616 | tf_op jit(solution)/shard_map/ppermute | solution.py:52
  30.0 0.6 %collective-permute-start.12 = (bf16[8,4096]{1,0:T(8,128)(2,1)S(1)}, bf16[8,4096]{1,0:T(8,128)(2,1)S(1)}, u32[]{:S(2)}, u32[]{:S(2)}) collective-permute-start(bf16[8,4096]{1,0:T(8,128)(2,1)S(1)} %subtract_convert_fusion), channel_id=1, source_target_pairs={{0,4},{1,5},{2,6},{3,7},{4,0},{5,1},{6,2},{7,3},{8,12},{9,13},{10,... | collective-permute-start | bytes 196616 | tf_op jit(solution)/shard_map/ppermute | solution.py:52
  30.6 1.4 %collective-permute-start.11 = (bf16[8,4096]{1,0:T(8,128)(2,1)S(1)}, bf16[8,4096]{1,0:T(8,128)(2,1)S(1)}, u32[]{:S(2)}, u32[]{:S(2)}) collective-permute-start(bf16[8,4096]{1,0:T(8,128)(2,1)S(1)} %subtract_convert_fusion), channel_id=1, source_target_pairs={{0,2},{1,3},{2,0},{3,1},{4,6},{5,7},{6,4},{7,5},{8,10},{9,11},{10,... | collective-permute-start | bytes 196616 | tf_op jit(solution)/shard_map/ppermute | solution.py:52
  32.1 1.7 %collective-permute-done.13 = bf16[8,4096]{1,0:T(8,128)(2,1)S(1)} collective-permute-done((bf16[8,4096]{1,0:T(8,128)(2,1)S(1)}, bf16[8,4096]{1,0:T(8,128)(2,1)S(1)}, u32[]{:S(2)}, u32[]{:S(2)}) %collective-permute-start.13) | collective-permute-done | bytes 65568 | tf_op jit(solution)/shard_map/ppermute | solution.py:52
  33.7 0.6 %collective-permute-done.12 = bf16[8,4096]{1,0:T(8,128)(2,1)S(1)} collective-permute-done((bf16[8,4096]{1,0:T(8,128)(2,1)S(1)}, bf16[8,4096]{1,0:T(8,128)(2,1)S(1)}, u32[]{:S(2)}, u32[]{:S(2)}) %collective-permute-start.12) | collective-permute-done | bytes 65568 | tf_op jit(solution)/shard_map/ppermute | solution.py:52
  34.3 0.6 %collective-permute-done.11 = bf16[8,4096]{1,0:T(8,128)(2,1)S(1)} collective-permute-done((bf16[8,4096]{1,0:T(8,128)(2,1)S(1)}, bf16[8,4096]{1,0:T(8,128)(2,1)S(1)}, u32[]{:S(2)}, u32[]{:S(2)}) %collective-permute-start.11) | collective-permute-done | bytes 65568 | tf_op jit(solution)/shard_map/ppermute | solution.py:52
  34.9 0.0 copy-start.1
  35.0 0.1 collective-permute-start.14
  35.1 0.5 %shard_map.224 = (bf16[64,4096]{1,0:T(8,128)(2,1)S(1)}, f32[82,64]{1,0:T(8,128)S(1)}, bf16[82,64]{1,0:T(8,128)(2,1)S(1)}, f32[82,1]{1,0:T(8,128)S(1)}, f32[82,1]{1,0:T(8,128)S(1)}) custom-call(bf16[32,4096]{1,0:T(8,128)(2,1)S(1)} %get-tuple-element.64.tokens_ref, bf16[32,4096]{1,0:T(8,128)(2,1)S(1)} %collective-permute-done.15.mate_tokens_ref, ...), custom_call_target="tpu_custom_call" | custom-call | flops 42991616 | bytes 3358720 | tf_op jit(solution)/shard_map/pallas_call | solution.py:154
  35.6 1.0 %collective-permute-done.14 = bf16[32,4096]{1,0:T(8,128)(2,1)S(1)} collective-permute-done((bf16[32,4096]{1,0:T(8,128)(2,1)S(1)}, bf16[32,4096]{1,0:T(8,128)(2,1)S(1)}, u32[]{:S(2)}, u32[]{:S(2)}) %collective-permute-start.14) | collective-permute-done | bytes 262176 | tf_op jit(solution)/shard_map/ppermute | solution.py:52
  36.6 3.3 %shard_map.225 = (bf16[82,4096]{1,0:T(8,128)(2,1)}, bf16[82,4096]{1,0:T(8,128)(2,1)}, f32[82,4096]{1,0:T(8,128)}, f32[82,4096]{1,0:T(8,128)}, f32[82,4096]{1,0:T...) custom-call(bf16[64,4096]{1,0:T(8,128)(2,1)S(1)} %pad_maximum_fusion, ...), custom_call_target="tpu_custom_call" | custom-call | flops 128974848 | bytes 13434880 | tf_op jit(solution)/shard_map/pallas_call | solution.py:262
  (25 shorter events, 0.2 us)
Async XLA Ops:
  0.6 12.2 %copy-start.5 = (f32[82]{0:T(128)S(1)}, f32[82]{0:T(128)}, u32[]{:S(2)}) copy-start(f32[82]{0:T(128)} %param.15) | copy-start | bytes 988
  0.7 6.6 %collective-permute-start = (bf16[4,4096]{1,0:T(4,128)(2,1)}, bf16[4,4096]{1,0:T(4,128)(2,1)S(1)}, u32[]{:S(2)}, u32[]{:S(2)}) collective-permute-start(bf16[4,4096]{1,0:T(4,128)(2,1)} %refs_0_.3), channel_id=1, source_target_pairs={{0,8},{1,9},{2,10},{3,11},{4,12},{5,13},{6,14},{7,15},{8,0},{9,1},... | collective-permute-start | bytes 98312 | tf_op jit(solution)/shard_map/ppermute | solution.py:52
  4.8 9.9 %collective-permute-start.4 = (bf16[82,4096]{1,0:T(8,128)(2,1)}, bf16[82,4096]{1,0:T(8,128)(2,1)S(1)}, u32[]{:S(2)}, u32[]{:S(2)}) collective-permute-start(bf16[82,4096]{1,0:T(8,128)(2,1)} %refs_0_.4), channel_id=1, source_target_pairs={{0,1},{1,0},{2,3},{3,2},{4,5},{5,4},{6,7},{7,6},{8,9},{9,8},{10,11... | collective-permute-start | bytes 2015240 | tf_op jit(solution)/shard_map/ppermute | solution.py:52
  4.8 9.9 %collective-permute-start.6 = (bf16[82,4096]{1,0:T(8,128)(2,1)}, bf16[82,4096]{1,0:T(8,128)(2,1)S(1)}, u32[]{:S(2)}, u32[]{:S(2)}) collective-permute-start(bf16[82,4096]{1,0:T(8,128)(2,1)} %refs_1_.2), channel_id=1, source_target_pairs={{0,1},{1,0},{2,3},{3,2},{4,5},{5,4},{6,7},{7,6},{8,9},{9,8},{10,11... | collective-permute-start | bytes 2015240 | tf_op jit(solution)/shard_map/ppermute | solution.py:52
  7.3 5.6 %collective-permute-start.3 = (bf16[8,4096]{1,0:T(8,128)(2,1)S(1)}, bf16[8,4096]{1,0:T(8,128)(2,1)S(1)}, u32[]{:S(2)}, u32[]{:S(2)}) collective-permute-start(bf16[8,4096]{1,0:T(8,128)(2,1)S(1)} %pad_maximum_fusion.6), channel_id=1, source_target_pairs={{0,6},{1,7},{2,4},{3,5},{4,2},{5,3},{6,0},{7,1},{8,14},{9,15},{10,... | collective-permute-start | bytes 196616 | tf_op jit(solution)/shard_map/ppermute | solution.py:52
  9.8 4.3 %collective-permute-start.2 = (bf16[8,4096]{1,0:T(8,128)(2,1)S(1)}, bf16[8,4096]{1,0:T(8,128)(2,1)S(1)}, u32[]{:S(2)}, u32[]{:S(2)}) collective-permute-start(bf16[8,4096]{1,0:T(8,128)(2,1)S(1)} %pad_maximum_fusion.6), channel_id=1, source_target_pairs={{0,2},{1,3},{2,0},{3,1},{4,6},{5,7},{6,4},{7,5},{8,10},{9,11},{10,... | collective-permute-start | bytes 196616 | tf_op jit(solution)/shard_map/ppermute | solution.py:52
  10.3 4.3 %collective-permute-start.1 = (bf16[8,4096]{1,0:T(8,128)(2,1)S(1)}, bf16[8,4096]{1,0:T(8,128)(2,1)S(1)}, u32[]{:S(2)}, u32[]{:S(2)}) collective-permute-start(bf16[8,4096]{1,0:T(8,128)(2,1)S(1)} %pad_maximum_fusion.6), channel_id=1, source_target_pairs={{0,4},{1,5},{2,6},{3,7},{4,0},{5,1},{6,2},{7,3},{8,12},{9,13},{10,... | collective-permute-start | bytes 196616 | tf_op jit(solution)/shard_map/ppermute | solution.py:52
  12.9 1.8 %collective-permute-start.5 = (f32[1,82]{1,0:T(1,128)S(1)}, f32[1,82]{1,0:T(1,128)S(1)}, u32[]{:S(2)}, u32[]{:S(2)}) collective-permute-start(f32[1,82]{1,0:T(1,128)S(1)} %bitcast.18), channel_id=1, source_target_pairs={{0,1},{1,0},{2,3},{3,2},{4,5},{5,4},{6,7},{7,6},{8,9},{9,8},{10,11... | collective-permute-start | bytes 992 | tf_op jit(solution)/shard_map/ppermute | solution.py:52
  15.7 6.3 %collective-permute-start.7 = (bf16[8,4096]{1,0:T(8,128)(2,1)S(1)}, bf16[8,4096]{1,0:T(8,128)(2,1)S(1)}, u32[]{:S(2)}, u32[]{:S(2)}) collective-permute-start(bf16[8,4096]{1,0:T(8,128)(2,1)S(1)} %get-tuple-element.53), channel_id=1, source_target_pairs={{0,2},{1,3},{2,0},{3,1},{4,6},{5,7},{6,4},{7,5},{8,10},{9,11},{10,... | collective-permute-start | bytes 196616 | tf_op jit(solution)/shard_map/ppermute | solution.py:52
  17.3 4.7 %collective-permute-start.8 = (bf16[8,4096]{1,0:T(8,128)(2,1)S(1)}, bf16[8,4096]{1,0:T(8,128)(2,1)S(1)}, u32[]{:S(2)}, u32[]{:S(2)}) collective-permute-start(bf16[8,4096]{1,0:T(8,128)(2,1)S(1)} %get-tuple-element.54), channel_id=1, source_target_pairs={{0,4},{1,5},{2,6},{3,7},{4,0},{5,1},{6,2},{7,3},{8,12},{9,13},{10,... | collective-permute-start | bytes 196616 | tf_op jit(solution)/shard_map/ppermute | solution.py:52
  17.9 10.5 %copy-start = (f32[4096]{0:T(1024)S(1)}, f32[4096]{0:T(1024)}, u32[]{:S(2)}) copy-start(f32[4096]{0:T(1024)} %param.17) | copy-start | bytes 49156
  17.9 5.2 %collective-permute-start.9 = (bf16[8,4096]{1,0:T(8,128)(2,1)S(1)}, bf16[8,4096]{1,0:T(8,128)(2,1)S(1)}, u32[]{:S(2)}, u32[]{:S(2)}) collective-permute-start(bf16[8,4096]{1,0:T(8,128)(2,1)S(1)} %get-tuple-element.55), channel_id=1, source_target_pairs={{0,6},{1,7},{2,4},{3,5},{4,2},{5,3},{6,0},{7,1},{8,14},{9,15},{10,... | collective-permute-start | bytes 196616 | tf_op jit(solution)/shard_map/ppermute | solution.py:52
  23.1 5.2 %collective-permute-start.10 = (bf16[8,4096]{1,0:T(8,128)(2,1)S(1)}, bf16[8,4096]{1,0:T(8,128)(2,1)S(1)}, u32[]{:S(2)}, u32[]{:S(2)}) collective-permute-start(bf16[8,4096]{1,0:T(8,128)(2,1)S(1)} %fusion.2), channel_id=1, source_target_pairs={{0,8},{1,9},{2,10},{3,11},{4,12},{5,13},{6,14},{7,15},{8,0},{9,1},... | collective-permute-start | bytes 196616 | tf_op jit(solution)/shard_map/ppermute | solution.py:52
  28.5 5.2 %collective-permute-start.13 = (bf16[8,4096]{1,0:T(8,128)(2,1)S(1)}, bf16[8,4096]{1,0:T(8,128)(2,1)S(1)}, u32[]{:S(2)}, u32[]{:S(2)}) collective-permute-start(bf16[8,4096]{1,0:T(8,128)(2,1)S(1)} %subtract_convert_fusion), channel_id=1, source_target_pairs={{0,6},{1,7},{2,4},{3,5},{4,2},{5,3},{6,0},{7,1},{8,14},{9,15},{10,... | collective-permute-start | bytes 196616 | tf_op jit(solution)/shard_map/ppermute | solution.py:52
  30.0 4.3 %collective-permute-start.12 = (bf16[8,4096]{1,0:T(8,128)(2,1)S(1)}, bf16[8,4096]{1,0:T(8,128)(2,1)S(1)}, u32[]{:S(2)}, u32[]{:S(2)}) collective-permute-start(bf16[8,4096]{1,0:T(8,128)(2,1)S(1)} %subtract_convert_fusion), channel_id=1, source_target_pairs={{0,4},{1,5},{2,6},{3,7},{4,0},{5,1},{6,2},{7,3},{8,12},{9,13},{10,... | collective-permute-start | bytes 196616 | tf_op jit(solution)/shard_map/ppermute | solution.py:52
  30.6 4.3 %collective-permute-start.11 = (bf16[8,4096]{1,0:T(8,128)(2,1)S(1)}, bf16[8,4096]{1,0:T(8,128)(2,1)S(1)}, u32[]{:S(2)}, u32[]{:S(2)}) collective-permute-start(bf16[8,4096]{1,0:T(8,128)(2,1)S(1)} %subtract_convert_fusion), channel_id=1, source_target_pairs={{0,2},{1,3},{2,0},{3,1},{4,6},{5,7},{6,4},{7,5},{8,10},{9,11},{10,... | collective-permute-start | bytes 196616 | tf_op jit(solution)/shard_map/ppermute | solution.py:52
  32.1 3.0 %collective-permute-start.15 = (bf16[32,4096]{1,0:T(8,128)(2,1)S(1)}, bf16[32,4096]{1,0:T(8,128)(2,1)S(1)}, u32[]{:S(2)}, u32[]{:S(2)}) collective-permute-start(bf16[32,4096]{1,0:T(8,128)(2,1)S(1)} %get-tuple-element.64.tokens_ref), channel_id=1, source_target_pairs={{0,1},{1,0},{2,3},{3,2},{4,5},{5,4},{6,7},{7,6},{8,9},{9,8},{10,11... | collective-permute-start | bytes 786440 | tf_op jit(solution)/shard_map/ppermute | solution.py:52
  34.9 1.7 %copy-start.1 = (f32[4096]{0:T(1024)S(1)}, f32[4096]{0:T(1024)}, u32[]{:S(2)}) copy-start(f32[4096]{0:T(1024)} %param.24) | copy-start | bytes 49156
  34.9 1.7 %copy-start.2 = (f32[4096]{0:T(1024)S(1)}, f32[4096]{0:T(1024)}, u32[]{:S(2)}) copy-start(f32[4096]{0:T(1024)} %param.25) | copy-start | bytes 49156
  34.9 1.7 %copy-start.3 = (f32[82]{0:T(128)S(1)}, f32[82]{0:T(128)}, u32[]{:S(2)}) copy-start(f32[82]{0:T(128)} %param.22) | copy-start | bytes 988
  34.9 1.7 %copy-start.4 = (f32[82]{0:T(128)S(1)}, f32[82]{0:T(128)}, u32[]{:S(2)}) copy-start(f32[82]{0:T(128)} %param.23) | copy-start | bytes 988
  35.0 1.6 %collective-permute-start.14 = (bf16[32,4096]{1,0:T(8,128)(2,1)S(1)}, bf16[32,4096]{1,0:T(8,128)(2,1)S(1)}, u32[]{:S(2)}, u32[]{:S(2)}) collective-permute-start(bf16[32,4096]{1,0:T(8,128)(2,1)S(1)} %pad_maximum_fusion.5), channel_id=1, source_target_pairs={{0,1},{1,0},{2,3},{3,2},{4,5},{5,4},{6,7},{7,6},{8,9},{9,8},{10,11... | collective-permute-start | bytes 786440 | tf_op jit(solution)/shard_map/ppermute | solution.py:52

commit v8 on v7

--- a/solution.py
+++ b/solution.py
@@ -322,11 +322,10 @@
         part = part + piece.astype(f32)
     for level in reversed(range(len(far))):
         part = lax.reduce_precision(part, 8, 7)
-        piece = part.astype(bf16)
-        other = swap(piece, far[level], devices)
         size = own << level
-        pieces = [other[start ^ size : (start ^ size) + size] for start in range(0, rows, size)]
-        part = part + jnp.concatenate(pieces, axis=0).astype(f32)
+        low = part.astype(bf16)
+        pieces = [low[start ^ size : (start ^ size) + size] for start in range(0, rows, size)]
+        part = part + swap(jnp.concatenate(pieces, axis=0), far[level], devices).astype(f32)
     errors = (part + decoder_bias - column[:rows].astype(f32)).astype(bf16)
     column = last_column
     errors, column = lax.optimization_barrier((errors, column))

time: 40.2 us -> 40.2 us (level)
  no operation moved by 1% of the time
where the time goes in v8:
time: 40.2 us; the launch traced here: 40 us
  starting transfers between devices  18.1 us (45%)
  waiting for transfers between devices  11.1 us (28%)
  Pallas kernels  9.69 us (24%)
  between operations  0.85 us (2%)
    ppermute x16, starting transfers between devices, swap(): return lax.ppermute(x, 'dict', [(i, i ^ bit) for i in range(devices)])  18.1 us
    ppermute x16, waiting for transfers between devices, swap(): return lax.ppermute(x, 'dict', [(i, i ^ bit) for i in range(devices)])  11.1 us
    pallas_call x3, Pallas kernels, load(): pl.pallas_call(load_kernel, in_specs=[ANY_SPEC] * len(arrays), out_specs=...  4.82 us
    pallas_call x1, Pallas kernels, update(): pl.pallas_call(functools.partial(update_kernel, own), in_specs=[VMEM_SPEC...  3.35 us
    pallas_call x1, Pallas kernels, forward(): pl.pallas_call(forward_kernel, in_specs=[VMEM_SPEC] * 7, out_specs=[VMEM_...  1 us
  transfers between devices with their start and end apart: 16, of which 10 were waited for; matrix products, arithmetic and copies ran while one was open for 0% of the time, Pallas kernels for 13%

profile of v8, /device:TPU:0, one launch (start us, length us, event | category | flops | bytes accessed | tf_op | source)
XLA Modules:
  0.0 40.0 jit_solution(12176967630084501495)
XLA Ops:
  0.7 4.1 %collective-permute-start = (bf16[4,4096]{1,0:T(4,128)(2,1)}, bf16[4,4096]{1,0:T(4,128)(2,1)S(1)}, u32[]{:S(2)}, u32[]{:S(2)}) collective-permute-start(bf16[4,4096]{1,0:T(4,128)(2,1)} %refs_0_.3), channel_id=1, source_target_pairs={{0,8},{1,9},{2,10},{3,11},{4,12},{5,13},{6,14},{7,15},{8,0},{9,1},... | collective-permute-start | bytes 98312 | tf_op jit(solution)/shard_map/ppermute | solution.py:52
  4.8 0.5 %collective-permute-start.6 = (bf16[82,4096]{1,0:T(8,128)(2,1)}, bf16[82,4096]{1,0:T(8,128)(2,1)S(1)}, u32[]{:S(2)}, u32[]{:S(2)}) collective-permute-start(bf16[82,4096]{1,0:T(8,128)(2,1)} %refs_1_.2), channel_id=1, source_target_pairs={{0,1},{1,0},{2,3},{3,2},{4,5},{5,4},{6,7},{7,6},{8,9},{9,8},{10,11... | collective-permute-start | bytes 2015240 | tf_op jit(solution)/shard_map/ppermute | solution.py:52
  5.3 0.8 %shard_map.220 = bf16[4,4096]{1,0:T(4,128)(2,1)S(1)} custom-call(bf16[4,4096]{1,0:T(4,128)(2,1)} %refs_0_.3), custom_call_target="tpu_custom_call" | custom-call | bytes 65536 | tf_op jit(solution)/shard_map/pallas_call | solution.py:77
  6.0 1.2 %collective-permute-done = bf16[4,4096]{1,0:T(4,128)(2,1)S(1)} collective-permute-done((bf16[4,4096]{1,0:T(4,128)(2,1)}, bf16[4,4096]{1,0:T(4,128)(2,1)S(1)}, u32[]{:S(2)}, u32[]{:S(2)}) %collective-permute-start) | collective-permute-done | bytes 32800 | tf_op jit(solution)/shard_map/ppermute | solution.py:52
  7.3 2.6 %collective-permute-start.3 = (bf16[8,4096]{1,0:T(8,128)(2,1)S(1)}, bf16[8,4096]{1,0:T(8,128)(2,1)S(1)}, u32[]{:S(2)}, u32[]{:S(2)}) collective-permute-start(bf16[8,4096]{1,0:T(8,128)(2,1)S(1)} %pad_maximum_fusion.6), channel_id=1, source_target_pairs={{0,6},{1,7},{2,4},{3,5},{4,2},{5,3},{6,0},{7,1},{8,14},{9,15},{10,... | collective-permute-start | bytes 196616 | tf_op jit(solution)/shard_map/ppermute | solution.py:52
  9.8 0.5 %collective-permute-start.2 = (bf16[8,4096]{1,0:T(8,128)(2,1)S(1)}, bf16[8,4096]{1,0:T(8,128)(2,1)S(1)}, u32[]{:S(2)}, u32[]{:S(2)}) collective-permute-start(bf16[8,4096]{1,0:T(8,128)(2,1)S(1)} %pad_maximum_fusion.6), channel_id=1, source_target_pairs={{0,2},{1,3},{2,0},{3,1},{4,6},{5,7},{6,4},{7,5},{8,10},{9,11},{10,... | collective-permute-start | bytes 196616 | tf_op jit(solution)/shard_map/ppermute | solution.py:52
  10.3 0.5 %collective-permute-start.1 = (bf16[8,4096]{1,0:T(8,128)(2,1)S(1)}, bf16[8,4096]{1,0:T(8,128)(2,1)S(1)}, u32[]{:S(2)}, u32[]{:S(2)}) collective-permute-start(bf16[8,4096]{1,0:T(8,128)(2,1)S(1)} %pad_maximum_fusion.6), channel_id=1, source_target_pairs={{0,4},{1,5},{2,6},{3,7},{4,0},{5,1},{6,2},{7,3},{8,12},{9,13},{10,... | collective-permute-start | bytes 196616 | tf_op jit(solution)/shard_map/ppermute | solution.py:52
  10.8 1.4 %shard_map.221 = (bf16[82,4096]{1,0:T(8,128)(2,1)S(1)}, bf16[82,4096]{1,0:T(8,128)(2,1)S(1)}, f32[1,82]{1,0:T(1,128)S(1)}) custom-call(bf16[82,4096]{1,0:T(8,128)(2,1)} %refs_0_.4, bf16[82,4096]{1,0:T(8,128)(2,1)} %refs_1_.2, f32[1,82]{1,0:T(1,128)} %bitcast.17), custom_call_target="tpu_custom_call" | custom-call | bytes 2687632 | tf_op jit(solution)/shard_map/pallas_call | solution.py:77
  12.2 0.7 %collective-permute-done.3 = bf16[8,4096]{1,0:T(8,128)(2,1)S(1)} collective-permute-done((bf16[8,4096]{1,0:T(8,128)(2,1)S(1)}, bf16[8,4096]{1,0:T(8,128)(2,1)S(1)}, u32[]{:S(2)}, u32[]{:S(2)}) %collective-permute-start.3) | collective-permute-done | bytes 65568 | tf_op jit(solution)/shard_map/ppermute | solution.py:52
  12.9 1.2 %collective-permute-done.2 = bf16[8,4096]{1,0:T(8,128)(2,1)S(1)} collective-permute-done((bf16[8,4096]{1,0:T(8,128)(2,1)S(1)}, bf16[8,4096]{1,0:T(8,128)(2,1)S(1)}, u32[]{:S(2)}, u32[]{:S(2)}) %collective-permute-start.2) | collective-permute-done | bytes 65568 | tf_op jit(solution)/shard_map/ppermute | solution.py:52
  14.1 0.5 %collective-permute-done.1 = bf16[8,4096]{1,0:T(8,128)(2,1)S(1)} collective-permute-done((bf16[8,4096]{1,0:T(8,128)(2,1)S(1)}, bf16[8,4096]{1,0:T(8,128)(2,1)S(1)}, u32[]{:S(2)}, u32[]{:S(2)}) %collective-permute-start.1) | collective-permute-done | bytes 65568 | tf_op jit(solution)/shard_map/ppermute | solution.py:52
  14.7 1.0 %shard_map.222 = (f32[8,4096]{1,0:T(8,128)S(1)}, bf16[8,4096]{1,0:T(8,128)(2,1)S(1)}, bf16[8,4096]{1,0:T(8,128)(2,1)S(1)}, bf16[8,4096]{1,0:T(8,128)(2,1)S(1)}) custom-call(bf16[32,4096]{1,0:T(8,128)(2,1)S(1)} %get-tuple-element.87.tokens_ref, bf16[82,4096]{1,0:T(8,128)(2,1)S(1)} %get-tuple-element.49.encoder_ref, ...), custom_call_target="tpu_custom_call" | custom-call | flops 85983232 | bytes 2686976 | tf_op jit(solution)/shard_map/pallas_call | solution.py:124
  15.7 1.6 %collective-permute-start.7 = (bf16[8,4096]{1,0:T(8,128)(2,1)S(1)}, bf16[8,4096]{1,0:T(8,128)(2,1)S(1)}, u32[]{:S(2)}, u32[]{:S(2)}) collective-permute-start(bf16[8,4096]{1,0:T(8,128)(2,1)S(1)} %get-tuple-element.53), channel_id=1, source_target_pairs={{0,2},{1,3},{2,0},{3,1},{4,6},{5,7},{6,4},{7,5},{8,10},{9,11},{10,... | collective-permute-start | bytes 196616 | tf_op jit(solution)/shard_map/ppermute | solution.py:52
  17.3 0.7 %collective-permute-start.8 = (bf16[8,4096]{1,0:T(8,128)(2,1)S(1)}, bf16[8,4096]{1,0:T(8,128)(2,1)S(1)}, u32[]{:S(2)}, u32[]{:S(2)}) collective-permute-start(bf16[8,4096]{1,0:T(8,128)(2,1)S(1)} %get-tuple-element.54), channel_id=1, source_target_pairs={{0,4},{1,5},{2,6},{3,7},{4,0},{5,1},{6,2},{7,3},{8,12},{9,13},{10,... | collective-permute-start | bytes 196616 | tf_op jit(solution)/shard_map/ppermute | solution.py:52
  17.9 1.3 %collective-permute-start.9 = (bf16[8,4096]{1,0:T(8,128)(2,1)S(1)}, bf16[8,4096]{1,0:T(8,128)(2,1)S(1)}, u32[]{:S(2)}, u32[]{:S(2)}) collective-permute-start(bf16[8,4096]{1,0:T(8,128)(2,1)S(1)} %get-tuple-element.55), channel_id=1, source_target_pairs={{0,6},{1,7},{2,4},{3,5},{4,2},{5,3},{6,0},{7,1},{8,14},{9,15},{10,... | collective-permute-start | bytes 196616 | tf_op jit(solution)/shard_map/ppermute | solution.py:52
  19.2 2.7 %shard_map.223 = (f32[82,4096]{1,0:T(8,128)S(1)}, f32[82,4096]{1,0:T(8,128)S(1)}, f32[82,4096]{1,0:T(8,128)S(1)}, f32[82,4096]{1,0:T(8,128)S(1)}) custom-call(f32[82,4096]{1,0:T(8,128)} %refs_0_.5, f32[82,4096]{1,0:T(8,128)} %refs_1_.3, f32[82,4096]{1,0:T(8,128)} %refs_2_.1, f32[82,4096]{1,0:T(8,128)} %refs_3_.1), custom_call_target="tpu_custom_call" | custom-call | bytes 10747904 | tf_op jit(solution)/shard_map/pallas_call | solution.py:77
  22.0 1.1 %collective-permute-done.9 = bf16[8,4096]{1,0:T(8,128)(2,1)S(1)} collective-permute-done((bf16[8,4096]{1,0:T(8,128)(2,1)S(1)}, bf16[8,4096]{1,0:T(8,128)(2,1)S(1)}, u32[]{:S(2)}, u32[]{:S(2)}) %collective-permute-start.9) | collective-permute-done | bytes 65568 | tf_op jit(solution)/shard_map/ppermute | solution.py:52
  23.2 2.7 %collective-permute-start.10 = (bf16[8,4096]{1,0:T(8,128)(2,1)S(1)}, bf16[8,4096]{1,0:T(8,128)(2,1)S(1)}, u32[]{:S(2)}, u32[]{:S(2)}) collective-permute-start(bf16[8,4096]{1,0:T(8,128)(2,1)S(1)} %pad_maximum_fusion.7), channel_id=1, source_target_pairs={{0,8},{1,9},{2,10},{3,11},{4,12},{5,13},{6,14},{7,15},{8,0},{9,1},... | collective-permute-start | bytes 196616 | tf_op jit(solution)/shard_map/ppermute | solution.py:52
  25.9 2.5 %collective-permute-done.10 = bf16[8,4096]{1,0:T(8,128)(2,1)S(1)} collective-permute-done((bf16[8,4096]{1,0:T(8,128)(2,1)S(1)}, bf16[8,4096]{1,0:T(8,128)(2,1)S(1)}, u32[]{:S(2)}, u32[]{:S(2)}) %collective-permute-start.10) | collective-permute-done | bytes 65568 | tf_op jit(solution)/shard_map/ppermute | solution.py:52
  28.5 0.1 subtract_convert_fusion
  28.5 1.5 %collective-permute-start.13 = (bf16[8,4096]{1,0:T(8,128)(2,1)S(1)}, bf16[8,4096]{1,0:T(8,128)(2,1)S(1)}, u32[]{:S(2)}, u32[]{:S(2)}) collective-permute-start(bf16[8,4096]{1,0:T(8,128)(2,1)S(1)} %subtract_convert_fusion), channel_id=1, source_target_pairs={{0,6},{1,7},{2,4},{3,5},{4,2},{5,3},{6,0},{7,1},{8,14},{9,15},{10,... | collective-permute-start | bytes 196616 | tf_op jit(solution)/shard_map/ppermute | solution.py:52
  30.1 0.6 %collective-permute-start.12 = (bf16[8,4096]{1,0:T(8,128)(2,1)S(1)}, bf16[8,4096]{1,0:T(8,128)(2,1)S(1)}, u32[]{:S(2)}, u32[]{:S(2)}) collective-permute-start(bf16[8,4096]{1,0:T(8,128)(2,1)S(1)} %subtract_convert_fusion), channel_id=1, source_target_pairs={{0,4},{1,5},{2,6},{3,7},{4,0},{5,1},{6,2},{7,3},{8,12},{9,13},{10,... | collective-permute-start | bytes 196616 | tf_op jit(solution)/shard_map/ppermute | solution.py:52
  30.6 1.4 %collective-permute-start.11 = (bf16[8,4096]{1,0:T(8,128)(2,1)S(1)}, bf16[8,4096]{1,0:T(8,128)(2,1)S(1)}, u32[]{:S(2)}, u32[]{:S(2)}) collective-permute-start(bf16[8,4096]{1,0:T(8,128)(2,1)S(1)} %subtract_convert_fusion), channel_id=1, source_target_pairs={{0,2},{1,3},{2,0},{3,1},{4,6},{5,7},{6,4},{7,5},{8,10},{9,11},{10,... | collective-permute-start | bytes 196616 | tf_op jit(solution)/shard_map/ppermute | solution.py:52
  32.1 1.7 %collective-permute-done.13 = bf16[8,4096]{1,0:T(8,128)(2,1)S(1)} collective-permute-done((bf16[8,4096]{1,0:T(8,128)(2,1)S(1)}, bf16[8,4096]{1,0:T(8,128)(2,1)S(1)}, u32[]{:S(2)}, u32[]{:S(2)}) %collective-permute-start.13) | collective-permute-done | bytes 65568 | tf_op jit(solution)/shard_map/ppermute | solution.py:52
  33.8 0.6 %collective-permute-done.12 = bf16[8,4096]{1,0:T(8,128)(2,1)S(1)} collective-permute-done((bf16[8,4096]{1,0:T(8,128)(2,1)S(1)}, bf16[8,4096]{1,0:T(8,128)(2,1)S(1)}, u32[]{:S(2)}, u32[]{:S(2)}) %collective-permute-start.12) | collective-permute-done | bytes 65568 | tf_op jit(solution)/shard_map/ppermute | solution.py:52
  34.3 0.6 %collective-permute-done.11 = bf16[8,4096]{1,0:T(8,128)(2,1)S(1)} collective-permute-done((bf16[8,4096]{1,0:T(8,128)(2,1)S(1)}, bf16[8,4096]{1,0:T(8,128)(2,1)S(1)}, u32[]{:S(2)}, u32[]{:S(2)}) %collective-permute-start.11) | collective-permute-done | bytes 65568 | tf_op jit(solution)/shard_map/ppermute | solution.py:52
  34.9 0.0 copy-start.1
  35.0 0.0 copy-start.4
  35.0 0.1 collective-permute-start.14
  35.1 0.5 %shard_map.224 = (bf16[64,4096]{1,0:T(8,128)(2,1)S(1)}, f32[82,64]{1,0:T(8,128)S(1)}, bf16[82,64]{1,0:T(8,128)(2,1)S(1)}, f32[82,1]{1,0:T(8,128)S(1)}, f32[82,1]{1,0:T(8,128)S(1)}) custom-call(bf16[32,4096]{1,0:T(8,128)(2,1)S(1)} %get-tuple-element.64.tokens_ref, bf16[32,4096]{1,0:T(8,128)(2,1)S(1)} %collective-permute-done.15.mate_tokens_ref, ...), custom_call_target="tpu_custom_call" | custom-call | flops 42991616 | bytes 3358720 | tf_op jit(solution)/shard_map/pallas_call | solution.py:154
  35.6 1.0 %collective-permute-done.14 = bf16[32,4096]{1,0:T(8,128)(2,1)S(1)} collective-permute-done((bf16[32,4096]{1,0:T(8,128)(2,1)S(1)}, bf16[32,4096]{1,0:T(8,128)(2,1)S(1)}, u32[]{:S(2)}, u32[]{:S(2)}) %collective-permute-start.14) | collective-permute-done | bytes 262176 | tf_op jit(solution)/shard_map/ppermute | solution.py:52
  36.7 3.3 %shard_map.225 = (bf16[82,4096]{1,0:T(8,128)(2,1)}, bf16[82,4096]{1,0:T(8,128)(2,1)}, f32[82,4096]{1,0:T(8,128)}, f32[82,4096]{1,0:T(8,128)}, f32[82,4096]{1,0:T...) custom-call(bf16[64,4096]{1,0:T(8,128)(2,1)S(1)} %pad_maximum_fusion, ...), custom_call_target="tpu_custom_call" | custom-call | flops 128974848 | bytes 13434880 | tf_op jit(solution)/shard_map/pallas_call | solution.py:262
  (26 shorter events, 0.3 us)
Async XLA Ops:
  0.6 12.2 %copy-start.5 = (f32[82]{0:T(128)S(1)}, f32[82]{0:T(128)}, u32[]{:S(2)}) copy-start(f32[82]{0:T(128)} %param.15) | copy-start | bytes 988
  0.7 6.6 %collective-permute-start = (bf16[4,4096]{1,0:T(4,128)(2,1)}, bf16[4,4096]{1,0:T(4,128)(2,1)S(1)}, u32[]{:S(2)}, u32[]{:S(2)}) collective-permute-start(bf16[4,4096]{1,0:T(4,128)(2,1)} %refs_0_.3), channel_id=1, source_target_pairs={{0,8},{1,9},{2,10},{3,11},{4,12},{5,13},{6,14},{7,15},{8,0},{9,1},... | collective-permute-start | bytes 98312 | tf_op jit(solution)/shard_map/ppermute | solution.py:52
  4.8 9.9 %collective-permute-start.4 = (bf16[82,4096]{1,0:T(8,128)(2,1)}, bf16[82,4096]{1,0:T(8,128)(2,1)S(1)}, u32[]{:S(2)}, u32[]{:S(2)}) collective-permute-start(bf16[82,4096]{1,0:T(8,128)(2,1)} %refs_0_.4), channel_id=1, source_target_pairs={{0,1},{1,0},{2,3},{3,2},{4,5},{5,4},{6,7},{7,6},{8,9},{9,8},{10,11... | collective-permute-start | bytes 2015240 | tf_op jit(solution)/shard_map/ppermute | solution.py:52
  4.8 9.9 %collective-permute-start.6 = (bf16[82,4096]{1,0:T(8,128)(2,1)}, bf16[82,4096]{1,0:T(8,128)(2,1)S(1)}, u32[]{:S(2)}, u32[]{:S(2)}) collective-permute-start(bf16[82,4096]{1,0:T(8,128)(2,1)} %refs_1_.2), channel_id=1, source_target_pairs={{0,1},{1,0},{2,3},{3,2},{4,5},{5,4},{6,7},{7,6},{8,9},{9,8},{10,11... | collective-permute-start | bytes 2015240 | tf_op jit(solution)/shard_map/ppermute | solution.py:52
  7.3 5.6 %collective-permute-start.3 = (bf16[8,4096]{1,0:T(8,128)(2,1)S(1)}, bf16[8,4096]{1,0:T(8,128)(2,1)S(1)}, u32[]{:S(2)}, u32[]{:S(2)}) collective-permute-start(bf16[8,4096]{1,0:T(8,128)(2,1)S(1)} %pad_maximum_fusion.6), channel_id=1, source_target_pairs={{0,6},{1,7},{2,4},{3,5},{4,2},{5,3},{6,0},{7,1},{8,14},{9,15},{10,... | collective-permute-start | bytes 196616 | tf_op jit(solution)/shard_map/ppermute | solution.py:52
  9.8 4.3 %collective-permute-start.2 = (bf16[8,4096]{1,0:T(8,128)(2,1)S(1)}, bf16[8,4096]{1,0:T(8,128)(2,1)S(1)}, u32[]{:S(2)}, u32[]{:S(2)}) collective-permute-start(bf16[8,4096]{1,0:T(8,128)(2,1)S(1)} %pad_maximum_fusion.6), channel_id=1, source_target_pairs={{0,2},{1,3},{2,0},{3,1},{4,6},{5,7},{6,4},{7,5},{8,10},{9,11},{10,... | collective-permute-start | bytes 196616 | tf_op jit(solution)/shard_map/ppermute | solution.py:52
  10.3 4.3 %collective-permute-start.1 = (bf16[8,4096]{1,0:T(8,128)(2,1)S(1)}, bf16[8,4096]{1,0:T(8,128)(2,1)S(1)}, u32[]{:S(2)}, u32[]{:S(2)}) collective-permute-start(bf16[8,4096]{1,0:T(8,128)(2,1)S(1)} %pad_maximum_fusion.6), channel_id=1, source_target_pairs={{0,4},{1,5},{2,6},{3,7},{4,0},{5,1},{6,2},{7,3},{8,12},{9,13},{10,... | collective-permute-start | bytes 196616 | tf_op jit(solution)/shard_map/ppermute | solution.py:52
  12.9 1.8 %collective-permute-start.5 = (f32[1,82]{1,0:T(1,128)S(1)}, f32[1,82]{1,0:T(1,128)S(1)}, u32[]{:S(2)}, u32[]{:S(2)}) collective-permute-start(f32[1,82]{1,0:T(1,128)S(1)} %bitcast.18), channel_id=1, source_target_pairs={{0,1},{1,0},{2,3},{3,2},{4,5},{5,4},{6,7},{7,6},{8,9},{9,8},{10,11... | collective-permute-start | bytes 992 | tf_op jit(solution)/shard_map/ppermute | solution.py:52
  15.7 6.3 %collective-permute-start.7 = (bf16[8,4096]{1,0:T(8,128)(2,1)S(1)}, bf16[8,4096]{1,0:T(8,128)(2,1)S(1)}, u32[]{:S(2)}, u32[]{:S(2)}) collective-permute-start(bf16[8,4096]{1,0:T(8,128)(2,1)S(1)} %get-tuple-element.53), channel_id=1, source_target_pairs={{0,2},{1,3},{2,0},{3,1},{4,6},{5,7},{6,4},{7,5},{8,10},{9,11},{10,... | collective-permute-start | bytes 196616 | tf_op jit(solution)/shard_map/ppermute | solution.py:52
  17.3 4.7 %collective-permute-start.8 = (bf16[8,4096]{1,0:T(8,128)(2,1)S(1)}, bf16[8,4096]{1,0:T(8,128)(2,1)S(1)}, u32[]{:S(2)}, u32[]{:S(2)}) collective-permute-start(bf16[8,4096]{1,0:T(8,128)(2,1)S(1)} %get-tuple-element.54), channel_id=1, source_target_pairs={{0,4},{1,5},{2,6},{3,7},{4,0},{5,1},{6,2},{7,3},{8,12},{9,13},{10,... | collective-permute-start | bytes 196616 | tf_op jit(solution)/shard_map/ppermute | solution.py:52
  17.9 10.5 %copy-start = (f32[4096]{0:T(1024)S(1)}, f32[4096]{0:T(1024)}, u32[]{:S(2)}) copy-start(f32[4096]{0:T(1024)} %param.17) | copy-start | bytes 49156
  17.9 5.2 %collective-permute-start.9 = (bf16[8,4096]{1,0:T(8,128)(2,1)S(1)}, bf16[8,4096]{1,0:T(8,128)(2,1)S(1)}, u32[]{:S(2)}, u32[]{:S(2)}) collective-permute-start(bf16[8,4096]{1,0:T(8,128)(2,1)S(1)} %get-tuple-element.55), channel_id=1, source_target_pairs={{0,6},{1,7},{2,4},{3,5},{4,2},{5,3},{6,0},{7,1},{8,14},{9,15},{10,... | collective-permute-start | bytes 196616 | tf_op jit(solution)/shard_map/ppermute | solution.py:52
  23.2 5.2 %collective-permute-start.10 = (bf16[8,4096]{1,0:T(8,128)(2,1)S(1)}, bf16[8,4096]{1,0:T(8,128)(2,1)S(1)}, u32[]{:S(2)}, u32[]{:S(2)}) collective-permute-start(bf16[8,4096]{1,0:T(8,128)(2,1)S(1)} %pad_maximum_fusion.7), channel_id=1, source_target_pairs={{0,8},{1,9},{2,10},{3,11},{4,12},{5,13},{6,14},{7,15},{8,0},{9,1},... | collective-permute-start | bytes 196616 | tf_op jit(solution)/shard_map/ppermute | solution.py:52
  28.5 5.2 %collective-permute-start.13 = (bf16[8,4096]{1,0:T(8,128)(2,1)S(1)}, bf16[8,4096]{1,0:T(8,128)(2,1)S(1)}, u32[]{:S(2)}, u32[]{:S(2)}) collective-permute-start(bf16[8,4096]{1,0:T(8,128)(2,1)S(1)} %subtract_convert_fusion), channel_id=1, source_target_pairs={{0,6},{1,7},{2,4},{3,5},{4,2},{5,3},{6,0},{7,1},{8,14},{9,15},{10,... | collective-permute-start | bytes 196616 | tf_op jit(solution)/shard_map/ppermute | solution.py:52
  30.1 4.3 %collective-permute-start.12 = (bf16[8,4096]{1,0:T(8,128)(2,1)S(1)}, bf16[8,4096]{1,0:T(8,128)(2,1)S(1)}, u32[]{:S(2)}, u32[]{:S(2)}) collective-permute-start(bf16[8,4096]{1,0:T(8,128)(2,1)S(1)} %subtract_convert_fusion), channel_id=1, source_target_pairs={{0,4},{1,5},{2,6},{3,7},{4,0},{5,1},{6,2},{7,3},{8,12},{9,13},{10,... | collective-permute-start | bytes 196616 | tf_op jit(solution)/shard_map/ppermute | solution.py:52
  30.6 4.3 %collective-permute-start.11 = (bf16[8,4096]{1,0:T(8,128)(2,1)S(1)}, bf16[8,4096]{1,0:T(8,128)(2,1)S(1)}, u32[]{:S(2)}, u32[]{:S(2)}) collective-permute-start(bf16[8,4096]{1,0:T(8,128)(2,1)S(1)} %subtract_convert_fusion), channel_id=1, source_target_pairs={{0,2},{1,3},{2,0},{3,1},{4,6},{5,7},{6,4},{7,5},{8,10},{9,11},{10,... | collective-permute-start | bytes 196616 | tf_op jit(solution)/shard_map/ppermute | solution.py:52
  32.1 3.0 %collective-permute-start.15 = (bf16[32,4096]{1,0:T(8,128)(2,1)S(1)}, bf16[32,4096]{1,0:T(8,128)(2,1)S(1)}, u32[]{:S(2)}, u32[]{:S(2)}) collective-permute-start(bf16[32,4096]{1,0:T(8,128)(2,1)S(1)} %get-tuple-element.64.tokens_ref), channel_id=1, source_target_pairs={{0,1},{1,0},{2,3},{3,2},{4,5},{5,4},{6,7},{7,6},{8,9},{9,8},{10,11... | collective-permute-start | bytes 786440 | tf_op jit(solution)/shard_map/ppermute | solution.py:52
  34.9 1.7 %copy-start.1 = (f32[4096]{0:T(1024)S(1)}, f32[4096]{0:T(1024)}, u32[]{:S(2)}) copy-start(f32[4096]{0:T(1024)} %param.24) | copy-start | bytes 49156
  34.9 1.7 %copy-start.2 = (f32[4096]{0:T(1024)S(1)}, f32[4096]{0:T(1024)}, u32[]{:S(2)}) copy-start(f32[4096]{0:T(1024)} %param.25) | copy-start | bytes 49156
  35.0 1.7 %copy-start.3 = (f32[82]{0:T(128)S(1)}, f32[82]{0:T(128)}, u32[]{:S(2)}) copy-start(f32[82]{0:T(128)} %param.22) | copy-start | bytes 988
  35.0 1.7 %copy-start.4 = (f32[82]{0:T(128)S(1)}, f32[82]{0:T(128)}, u32[]{:S(2)}) copy-start(f32[82]{0:T(128)} %param.23) | copy-start | bytes 988
  35.0 1.6 %collective-permute-start.14 = (bf16[32,4096]{1,0:T(8,128)(2,1)S(1)}, bf16[32,4096]{1,0:T(8,128)(2,1)S(1)}, u32[]{:S(2)}, u32[]{:S(2)}) collective-permute-start(bf16[32,4096]{1,0:T(8,128)(2,1)S(1)} %pad_maximum_fusion.5), channel_id=1, source_target_pairs={{0,1},{1,0},{2,3},{3,2},{4,5},{5,4},{6,7},{7,6},{8,9},{9,8},{10,11... | collective-permute-start | bytes 786440 | tf_op jit(solution)/shard_map/ppermute | solution.py:52
